TPU v7x, 32 devices: a whole 2x2x4 slice. The times are simulated.
32 devices in a mesh: row: 8 (over z, y), col: 4 (over x, core).
Axes of the slice: x: 2, y: 2, z: 4, core: 2. Of those that a mesh axis runs over, the one named last changes fastest.
Arguments:
- anc_inverse: bfloat16 [1, 8, 256, 2, 4, 256], P(None, 'row', None, None, 'col'), may hold values from -6 to 6
- factor_one: bfloat16 [1, 8, 256, 2, 4, 256], P(None, 'row', None, None, 'col'), may hold values from -0.125 to 0.125
- factor_two: bfloat16 [1, 8, 256, 1, 4, 256], P(None, 'row', None, None, 'col'), may hold values from -0.125 to 0.125
- parent_block: bfloat16 [1, 4, 256, 256], P(None, 'col'), may hold values from -0.375 to 0.375
- diag_one: float32 [2, 4, 256, 256], P(None, 'col'), may hold values from -6 to 6
- diag_two: float32 [1, 4, 256, 256], P(None, 'col'), may hold values from -6 to 6
- pattern_one: int32 [1, 8, 2, 4], P(None, 'row', None, 'col'), may hold values from 0 to 1
- pattern_two: int32 [1, 8, 1, 4], P(None, 'row', None, 'col'), may hold values from 0 to 1, as said below
- parent: int32 [1, 4], P(None, 'col'), may hold values from 0 to 7, as said below
Outputs:
- inv_one: bfloat16 [1, 8, 256, 2, 4, 256], P(None, 'row', None, None, 'col')
- diag_inv_one: float32 [2, 4, 256, 256], P(None, 'col')
- inv_two: bfloat16 [1, 8, 256, 1, 4, 256], P(None, 'row', None, None, 'col')
- parent_inv: bfloat16 [1, 4, 256, 256], P(None, 'col')
- diag_inv_two: float32 [1, 4, 256, 256], P(None, 'col')
Inputs may be any that keep to these rules, and one draw needn't show every extreme that they name: pattern_two[J, K] is zero wherever pattern_one[J, P(K)] is zero. parent[k, c] is a level-one supernode whose index leaves remainder c when divided by 4.
All inputs are finite; a program needn't handle non-finite values.
Results may differ from a plain program's by a relative error of at most 0.007.
Values may be sent and summed in bfloat16 or wider, within the bound.
No kernel may reach another device: no remote copies, remote signals or barrier semaphores. Data moves between devices by JAX's collectives and lax.ppermute only.
A program may use at most 64 MiB of HBM per device.

v0:
```python
import jax
import jax.numpy as jnp
from jax import lax
from jax.sharding import PartitionSpec as P


def rows_step(whole_anc, anc_rows, block):

    def add_rows(total, piece, start):
        count = piece.shape[1]
        left = whole_anc.reshape(anc_rows * block, anc_rows * count * block)
        right = piece.reshape(anc_rows * count * block, piece.shape[3] * block)
        return jnp.dot(left, right, preferred_element_type=jnp.float32)

    return add_rows


def body(
    anc_inverse,
    factor_one,
    factor_two,
    parent_block,
    diag_one,
    diag_two,
    pattern_one,
    pattern_two,
    parent,
):
    anc_rows = anc_inverse.shape[0]
    block = anc_inverse.shape[2]
    first_count = factor_one.shape[3]
    second_count = factor_two.shape[3]
    grid_rows = lax.axis_size("row")
    grid_cols = lax.axis_size("col")
    first_factor = factor_one * pattern_one.astype(jnp.bfloat16)[:, :, None, :, :, None]
    second_factor = factor_two * pattern_two.astype(jnp.bfloat16)[:, :, None, :, :, None]
    first_empty = jnp.zeros((anc_rows * block, first_count * block), jnp.float32)
    second_empty = jnp.zeros((anc_rows * block, second_count * block), jnp.float32)
    whole_anc = lax.all_gather(anc_inverse, "col", axis=4, tiled=True).reshape(
        anc_rows * block, anc_rows, grid_rows, block
    )
    add_rows = rows_step(whole_anc, anc_rows, block)
    first_total = add_rows(
        first_empty, lax.all_gather(first_factor, "row", axis=1, tiled=True), jnp.int32(0)
    )
    first_shape = (anc_rows, block, first_count, block)
    second_shape = (anc_rows, block, second_count, block)
    first_keep = pattern_one.astype(jnp.float32)
    second_keep = pattern_two.astype(jnp.float32)
    first_inv = (-first_total.reshape(first_shape) * first_keep).astype(jnp.bfloat16)
    first_cols = first_factor.reshape(first_shape)
    second_cols = second_factor.reshape(second_shape)
    diag_part = jnp.einsum(
        "ixky,ixkz->kyz", first_cols, first_inv, preferred_element_type=jnp.float32
    )
    local_parent = parent.reshape(second_count) // grid_cols
    parent_cols = jnp.take(first_inv, local_parent, axis=2)
    cross_part = jnp.einsum(
        "ixky,ixkz->kyz", parent_cols, second_cols, preferred_element_type=jnp.float32
    )
    diag_sum, cross_sum = lax.psum((diag_part, cross_part), "row")
    first_diag = diag_one.reshape(first_count, block, block) - diag_sum
    parent_diag = jnp.take(first_diag.astype(jnp.bfloat16), local_parent, axis=0)
    coupling = parent_block.reshape(second_count, block, block)
    parent_inv = (
        -(
            jnp.einsum("kyx,kxz->kyz", parent_diag, coupling, preferred_element_type=jnp.float32)
            + cross_sum
        )
    ).astype(jnp.bfloat16)
    second_total = add_rows(
        second_empty, lax.all_gather(second_factor, "row", axis=1, tiled=True), jnp.int32(0)
    )
    side = jnp.einsum("ixky,kyz->ixkz", parent_cols, coupling, preferred_element_type=jnp.float32)
    second_inv = (-(second_total.reshape(second_shape) + side) * second_keep).astype(jnp.bfloat16)
    child_part = jnp.einsum(
        "ixky,ixkz->kyz", second_cols, second_inv, preferred_element_type=jnp.float32
    )
    child_sum = lax.psum(child_part.astype(jnp.bfloat16), "row").astype(jnp.float32)
    parent_terms = jnp.einsum(
        "kxy,kxz->kyz", coupling, parent_inv, preferred_element_type=jnp.float32
    )
    second_diag = diag_two.reshape(second_count, block, block) - (child_sum + parent_terms)
    return (
        first_inv.reshape(factor_one.shape),
        first_diag.reshape(diag_one.shape),
        second_inv.reshape(factor_two.shape),
        parent_inv.reshape(parent_block.shape),
        second_diag.reshape(diag_two.shape),
    )


def solution(mesh):
    placed = (
        P(None, "row", None, None, "col", None),
        P(None, "row", None, None, "col", None),
        P(None, "row", None, None, "col", None),
        P(None, "col", None, None),
        P(None, "col", None, None),
        P(None, "col", None, None),
        P(None, "row", None, "col"),
        P(None, "row", None, "col"),
        P(None, "col"),
    )
    return jax.shard_map(
        body,
        mesh=mesh,
        in_specs=placed,
        out_specs=(
            P(None, "row", None, None, "col", None),
            P(None, "col", None, None),
            P(None, "row", None, None, "col", None),
            P(None, "col", None, None),
            P(None, "col", None, None),
        ),
        check_vma=False,
    )
```

profile of v0, /device:TPU:1, one launch (start us, length us, event | category | flops | bytes accessed | tf_op | source)
XLA Modules:
  0.0 279.3 jit_solution(9864667952453709372)
XLA Ops:
  7.2 0.0 all-gather.4.cloned.1.call-start
  7.2 0.7 convert_bitcast_fusion
  8.0 1.7 copy_multiply_fusion
  9.7 0.0 all-gather.4.cloned.1.call-update
  9.7 0.0 all-gather.6.cloned.1.call-start
  9.8 1.8 copy.41
  11.6 0.0 all-gather.6.cloned.1.call-update
  11.6 0.0 all-gather.8.cloned.1.call-start
  12.3 1.6 bitcast_multiply_fusion
  13.9 0.0 all-reduce.6.cloned.1.call-start
  14.6 0.6 dynamic-slice.9
  15.2 45.8 %all-gather.4.cloned.1.call-done = bf16[1,8,256,2,1,256]{5,2,4,3,0,1:T(8,128)(2,1)} async-done(((bf16[1,1,256,2,1,256]{5,2,4,3,0,1:T(8,128)(2,1)}), bf16[1,8,256,2,1,256]{5,2,4,3,0,1:T(8,128)(2,1)}) %all-gather.4.cloned.1.call-update) | async-done | bytes 2097168 | tf_op jit(solution)/shard_map/all_gather | solution.py:44
  61.0 3.4 %copy.40 = bf16[1,8,256,2,1,256]{2,1,5,3,4,0:T(8,128)(2,1)S(1)} copy(bf16[1,8,256,2,1,256]{5,2,4,3,0,1:T(8,128)(2,1)} %all-gather.4.cloned.1.call-done) | data formatting | bytes 4194304 | tf_op jit(solution)/shard_map/all_gather | solution.py:44
  64.4 2.0 copy.53
  66.4 13.5 %all-gather.6.cloned.1.call-done = bf16[1,1,256,2,4,256]{2,5,4,3,1,0:T(8,128)(2,1)} async-done(((bf16[1,1,256,2,1,256]{2,5,4,3,1,0:T(8,128)(2,1)}), bf16[1,1,256,2,4,256]{2,5,4,3,1,0:T(8,128)(2,1)}) %all-gather.6.cloned.1.call-update) | async-done | bytes 1048592 | tf_op jit(solution)/shard_map/all_gather | solution.py:39
  79.9 2.6 convolution_negate_fusion
  82.5 0.2 copy.43
  82.7 1.6 convolution_bitcast_fusion.1
  84.4 1.1 fusion.11
  85.5 0.0 all-reduce.4.cloned.1.call-start
  85.5 0.2 copy.42
  85.8 0.9 convolution_bitcast_fusion.3
  86.7 34.7 %all-gather.8.cloned.1.call-done = bf16[1,8,256,1,1,256]{5,2,4,3,0,1:T(8,128)(2,1)} async-done(((bf16[1,1,256,1,1,256]{5,2,4,3,0,1:T(8,128)(2,1)}), bf16[1,8,256,1,1,256]{5,2,4,3,0,1:T(8,128)(2,1)}) %all-gather.8.cloned.1.call-update) | async-done | bytes 1048592 | tf_op jit(solution)/shard_map/all_gather | solution.py:72
  121.4 1.7 fusion.9
  123.1 0.8 copy.49
  123.9 0.9 fusion.10
  124.8 0.9 multiply_convert_fusion.1
  125.7 73.2 %all-reduce.6.cloned.1.call-done = (f32[2,256,256]{2,1,0:T(8,128)}, f32[1,256,256]{2,1,0:T(8,128)}) async-done(((f32[2,256,256]{2,1,0:T(8,128)}, f32[1,256,256]{2,1,0:T(8,128)}), (f32[2,256,256]{2,1,0:T(8,128)}, f32[1,256,256]{2,1,0:T(8,128)})) %all-reduce.6.cloned.1.call-update) | async-done | bytes 786448 | tf_op jit(solution)/shard_map/psum | solution.py:61
  199.0 1.1 bitcast_subtract_fusion
  200.1 1.3 fusion.8
  201.4 69.5 %all-reduce.4.cloned.1.call-done = bf16[1,256,256]{2,1,0:T(8,128)(2,1)} async-done(((bf16[1,256,256]{2,1,0:T(8,128)(2,1)}), bf16[1,256,256]{2,1,0:T(8,128)(2,1)}) %all-reduce.4.cloned.1.call-update) | async-done | bytes 131088 | tf_op jit(solution)/shard_map/psum | solution.py:79
  270.9 1.8 fusion.7
  (19 shorter events, 0.1 us)
Async XLA Ops:
  7.2 78.6 %copy-start = (bf16[1,1,256,256]{3,2,1,0:T(8,128)(2,1)S(1)}, bf16[1,1,256,256]{3,2,1,0:T(8,128)(2,1)}, u32[]{:S(2)}) copy-start(bf16[1,1,256,256]{3,2,1,0:T(8,128)(2,1)} %param.12) | copy-start | bytes 393220
  7.2 53.8 %all-gather.4.cloned.1.call-start = ((), (), s32[]{:S(2)}) async-start(), calls=%async_computation | async-start | bytes 2359296 | tf_op jit(solution)/shard_map/all_gather | solution.py:44
  9.7 70.2 %all-gather.6.cloned.1.call-start = ((), (), s32[]{:S(2)}) async-start(), calls=%async_computation.1 | async-start | bytes 1310720 | tf_op jit(solution)/shard_map/all_gather | solution.py:39
  11.6 109.8 %all-gather.8.cloned.1.call-start = ((), (), s32[]{:S(2)}) async-start(), calls=%async_computation.2 | async-start | bytes 1179648 | tf_op jit(solution)/shard_map/all_gather | solution.py:72
  13.9 185.1 %all-reduce.6.cloned.1.call-start = ((), (), s32[]{:S(2)}) async-start(), calls=%async_computation.4 | async-start | bytes 1572864 | tf_op jit(solution)/shard_map/psum | solution.py:61
  79.9 2.8 %copy-start.2 = (bf16[1,1,256,1,1,256]{5,2,4,3,0,1:T(8,128)(2,1)S(1)}, bf16[1,1,256,1,1,256]{5,2,4,3,0,1:T(8,128)(2,1)}, u32[]{:S(2)}) copy-start(bf16[1,1,256,1,1,256]{5,2,4,3,0,1:T(8,128)(2,1)} %bitcast_multiply_fusion) | copy-start | bytes 393220
  79.9 4.5 %copy-start.1 = (bf16[1,1,256,2,1,256]{5,2,4,3,0,1:T(8,128)(2,1)S(1)}, bf16[1,1,256,2,1,256]{5,2,4,3,0,1:T(8,128)(2,1)}, u32[]{:S(2)}) copy-start(bf16[1,1,256,2,1,256]{5,2,4,3,0,1:T(8,128)(2,1)} %copy_multiply_fusion) | copy-start | bytes 786436
  82.7 38.7 %copy-start.3 = (bf16[1,1,256,2,4,256]{2,5,4,3,1,0:T(8,128)(2,1)S(1)}, bf16[1,1,256,2,4,256]{2,5,4,3,1,0:T(8,128)(2,1)}, u32[]{:S(2)}) copy-start(bf16[1,1,256,2,4,256]{2,5,4,3,1,0:T(8,128)(2,1)} %all-gather.6.cloned.1.call-done) | copy-start | bytes 3145732
  85.5 185.4 %all-reduce.4.cloned.1.call-start = ((), (), s32[]{:S(2)}) async-start(), calls=%async_computation.3 | async-start | bytes 262144 | tf_op jit(solution)/shard_map/psum | solution.py:79
  86.7 112.3 %copy-start.5 = (f32[2,1,256,256]{3,2,1,0:T(8,128)S(1)}, f32[2,1,256,256]{3,2,1,0:T(8,128)}, u32[]{:S(2)}) copy-start(f32[2,1,256,256]{3,2,1,0:T(8,128)} %param.13) | copy-start | bytes 1572868
  123.1 147.8 %copy-start.7 = (f32[1,1,256,256]{3,2,1,0:T(8,128)S(1)}, f32[1,1,256,256]{3,2,1,0:T(8,128)}, u32[]{:S(2)}) copy-start(f32[1,1,256,256]{3,2,1,0:T(8,128)} %param.14) | copy-start | bytes 786436
  200.1 72.7 %copy-start.4 = (f32[2,256,256]{2,1,0:T(8,128)}, f32[2,256,256]{2,1,0:T(8,128)S(1)}, u32[]{:S(2)}) copy-start(f32[2,256,256]{2,1,0:T(8,128)S(1)} %bitcast_subtract_fusion) | copy-start | bytes 1572868
  201.4 71.4 %copy-start.6 = (bf16[1,256,256]{2,1,0:T(8,128)(2,1)}, bf16[1,256,256]{2,1,0:T(8,128)(2,1)S(1)}, u32[]{:S(2)}) copy-start(bf16[1,256,256]{2,1,0:T(8,128)(2,1)S(1)} %fusion.8) | copy-start | bytes 393220
Sparse Core Ops, SparseCore 0:
  10.7 50.2 all-gather.3
  63.1 16.7 all-gather.5
  82.6 38.7 all-gather.7
  125.3 73.5 all-reduce.5
  203.1 67.7 all-reduce.3
where the time goes:
time: 282 us; the launch traced here: 279 us
  waiting for transfers between devices  237 us (84%)
  between operations  15.2 us (5%)
  matrix products  12 us (4%)
  local copies, waits for them, and re-layouts  9.01 us (3%)
  other arithmetic  6.1 us (2%)
    psum x1, waiting for transfers between devices, body(): diag_sum, cross_sum = lax.psum((diag_part, cross_part), 'row')  73.2 us
    psum x1, waiting for transfers between devices, body(): lax.psum(child_part.astype(jnp.bfloat16), 'row').astype(jnp.float32)  69.5 us
    all_gather x1, waiting for transfers between devices, body(): lax.all_gather(first_factor, 'row', axis=1, tiled=True)  45.8 us
    all_gather x1, waiting for transfers between devices, body(): lax.all_gather(second_factor, 'row', axis=1, tiled=True)  34.7 us
    all_gather x1, waiting for transfers between devices, body(): lax.all_gather(anc_inverse, 'col', axis=4, tiled=True)  13.5 us
  transfers between devices with their start and end apart: 5, of which 5 were waited for; matrix products, arithmetic and copies ran while one was open for 8% of the time, Pallas kernels for 0%

commit v1 on v0

v1 whole, which is shorter than its diff:
```python
import functools

import jax
import jax.numpy as jnp
from jax import lax
from jax.experimental import pallas as pl
from jax.experimental.pallas import tpu as pltpu
from jax.sharding import PartitionSpec as P

AXES = ("row", "col")


def send(value, sizes, source):
    high, wide = sizes
    pairs = []
    for z in range(high):
        for y in range(2):
            for x in range(wide):
                for k in range(2):
                    sz, sy, sx, sk = source(z, y, x, k)
                    pairs.append(
                        ((2 * sz + sy) * 2 * wide + 2 * sx + sk, (2 * z + y) * 2 * wide + 2 * x + k)
                    )
    return lax.ppermute(value, AXES, pairs)


def place():
    row, col = lax.axis_index("row"), lax.axis_index("col")
    return row // 2, row % 2, col // 2, col % 2


def tdot(left, right):
    return lax.dot_general(
        left, right, (((0,), (0,)), ((), ())), preferred_element_type=jnp.float32
    )


def product_kernel(high, wide, *refs):
    a_refs = refs[: 2 * wide]
    x_refs = refs[2 * wide : 2 * wide + high]
    other_ref, couple_ref = refs[2 * wide + high : 2 * wide + high + 2]
    keep_y, send_y, keep_g, send_g, a_all, x_all, x_row, y_all, g_all = refs[2 * wide + high + 2 :]
    block = other_ref.shape[0]
    z, y, x, k = place()
    turn = z ^ x
    swap = y ^ k
    for step in range(high):
        x_all[pl.ds(pl.multiple_of((turn ^ step) * block, block), block), :] = x_refs[step][...]
    for dy in range(2):
        for dx in range(wide):
            for kk in range(2):
                t = kk * wide + dx
                a_all[dy * block : (dy + 1) * block, t * block : (t + 1) * block] = a_refs[
                    dy * wide + dx
                ][kk]
    x_row[pl.ds(pl.multiple_of(swap * block, block), block), :] = x_refs[0][...]
    x_row[pl.ds(pl.multiple_of((1 - swap) * block, block), block), :] = other_ref[...]
    total = jnp.dot(a_all[...], x_all[...], preferred_element_type=jnp.float32)
    near = total[:, :block].astype(jnp.bfloat16)
    far = total[:, block : 2 * block]
    last = total[:, 2 * block :] - jnp.dot(
        near, couple_ref[...], preferred_element_type=jnp.float32
    )
    y_all[:, : 2 * block] = total[:, : 2 * block]
    y_all[:, 2 * block :] = last
    g_all[:block] = tdot(x_row[:, :block], near)
    g_all[block : 2 * block] = tdot(x_row[:, block : 2 * block], far.astype(jnp.bfloat16))
    g_all[2 * block : 3 * block] = tdot(near, x_row[:, 2 * block :])
    g_all[3 * block :] = tdot(x_row[:, 2 * block :], last.astype(jnp.bfloat16))
    keep_y[...] = y_all[pl.ds(pl.multiple_of(swap * block, block), block), :]
    send_y[...] = y_all[pl.ds(pl.multiple_of((1 - swap) * block, block), block), :]
    keep_g[...] = g_all[pl.ds(pl.multiple_of(k * 2 * block, block), 2 * block), :]
    send_g[...] = g_all[pl.ds(pl.multiple_of((1 - k) * 2 * block, block), 2 * block), :].astype(
        jnp.bfloat16
    )


def finish_kernel(first_ref, second_ref, one_ref, two_ref, couple_ref, which_ref, out_one, out_parent, out_two, terms):
    block = couple_ref.shape[0]
    z, y, x, k = place()
    terms[y] = first_ref[...].astype(jnp.float32)
    terms[1 - y] = second_ref[...].astype(jnp.float32)
    near = which_ref[0]
    out_one[near] = one_ref[near] + terms[0, :block]
    out_one[1 - near] = one_ref[1 - near] + terms[0, block:]
    couple = couple_ref[...]
    diag = out_one[near].astype(jnp.bfloat16)
    parent = -(jnp.dot(diag, couple, preferred_element_type=jnp.float32) - terms[1, :block])
    parent = parent.astype(jnp.bfloat16)
    out_parent[...] = parent
    out_two[...] = two_ref[...] + terms[1, block:] - tdot(couple, parent)


def body(
    anc_inverse,
    factor_one,
    factor_two,
    parent_block,
    diag_one,
    diag_two,
    pattern_one,
    pattern_two,
    parent,
):
    block = anc_inverse.shape[2]
    high = lax.axis_size("row") // 2
    wide = lax.axis_size("col") // 2
    sizes = (high, wide)
    z, y, x, k = place()
    near = parent.reshape(1) // lax.axis_size("col")
    keep_one = pattern_one.reshape(2)
    keep_two = pattern_two.reshape(1)
    flip = near[0] == 1
    one = factor_one.reshape(block, 2, block)
    two = factor_two.reshape(block, block)
    masked = one * keep_one.astype(jnp.bfloat16)[None, :, None]
    zero, unit = masked[:, 0], masked[:, 1]
    cols = jnp.concatenate(
        [
            jnp.where(flip, unit, zero),
            jnp.where(flip, zero, unit),
            two * keep_two.astype(jnp.bfloat16)[0],
        ],
        axis=1,
    )
    coupling = parent_block.reshape(block, block)
    anc = anc_inverse.reshape(block, 2, block).transpose(1, 0, 2)

    pieces = [
        send(cols, sizes, lambda z, y, x, k, d=d: (z ^ d, k, x, y)) for d in range(high)
    ]
    couple = send(coupling, sizes, lambda z, y, x, k: (z, k, x, y))
    other = send(pieces[0], sizes, lambda z, y, x, k: (z, y, x, 1 - k))
    ancs = [
        anc
        if dy == 0 and dx == 0
        else send(anc, sizes, lambda z, y, x, k, dy=dy, dx=dx: (z, y ^ dy, x ^ dx, k))
        for dy in range(2)
        for dx in range(wide)
    ]
    width = 3 * block
    keep_y, send_y, keep_g, send_g = pl.pallas_call(
        functools.partial(product_kernel, high, wide),
        out_shape=(
            jax.ShapeDtypeStruct((block, width), jnp.float32),
            jax.ShapeDtypeStruct((block, width), jnp.float32),
            jax.ShapeDtypeStruct((2 * block, block), jnp.float32),
            jax.ShapeDtypeStruct((2 * block, block), jnp.bfloat16),
        ),
        scratch_shapes=[
            pltpu.VMEM((2 * block, high * block), jnp.bfloat16),
            pltpu.VMEM((high * block, width), jnp.bfloat16),
            pltpu.VMEM((2 * block, width), jnp.bfloat16),
            pltpu.VMEM((2 * block, width), jnp.float32),
            pltpu.VMEM((4 * block, block), jnp.float32),
        ],
        compiler_params=pltpu.CompilerParams(vmem_limit_bytes=48 * 1024 * 1024),
        name="products",
    )(*ancs, *pieces, other, couple)

    def core_swap(value):
        return send(value, sizes, lambda z, y, x, k: (z, y, x, 1 - k))

    mine = keep_g + core_swap(send_g).astype(jnp.float32)
    rows = 2 * block // high

    def part(value, at):
        return lax.dynamic_slice_in_dim(value, at * rows, rows, axis=0)

    coarse = mine.astype(jnp.bfloat16)
    share = part(mine, z)
    for d in range(1, high):
        got = send(part(coarse, z ^ d), sizes, lambda z, y, x, k, d=d: (z ^ d, y, x, k))
        share = share + got.astype(jnp.float32)
    share = share.astype(jnp.bfloat16)
    half = jnp.zeros((2 * block, block), jnp.bfloat16)
    half = lax.dynamic_update_slice_in_dim(half, share, z * rows, axis=0)
    for d in range(1, high):
        got = send(share, sizes, lambda z, y, x, k, d=d: (z ^ d, y, x, k))
        half = lax.dynamic_update_slice_in_dim(half, got, (z ^ d) * rows, axis=0)
    first = send(half, sizes, lambda z, y, x, k: (z, k, x, y))
    second = send(half, sizes, lambda z, y, x, k: (z, k, x, 1 - y))

    row_y = (keep_y + core_swap(send_y)).astype(jnp.bfloat16)
    row_y = send(row_y, sizes, lambda z, y, x, k: (z, k, x, y))
    near_y, far_y, last_y = row_y[:, :block], row_y[:, block : 2 * block], row_y[:, 2 * block :]
    inv_zero = jnp.where(flip, far_y, near_y)
    inv_unit = jnp.where(flip, near_y, far_y)
    inv_one = jnp.stack([inv_zero, inv_unit], axis=1) * -keep_one.astype(jnp.bfloat16)[None, :, None]
    inv_two = last_y * -keep_two.astype(jnp.bfloat16)[0]

    out_one, out_parent, out_two = pl.pallas_call(
        finish_kernel,
        out_shape=(
            jax.ShapeDtypeStruct((2, block, block), jnp.float32),
            jax.ShapeDtypeStruct((block, block), jnp.bfloat16),
            jax.ShapeDtypeStruct((block, block), jnp.float32),
        ),
        in_specs=[pl.BlockSpec(memory_space=pltpu.VMEM)] * 5
        + [pl.BlockSpec(memory_space=pltpu.SMEM)],
        scratch_shapes=[pltpu.VMEM((2, 2 * block, block), jnp.float32)],
        name="finish",
    )(
        first,
        second,
        diag_one.reshape(2, block, block),
        diag_two.reshape(block, block),
        coupling,
        near.astype(jnp.int32),
    )
    return (
        inv_one.reshape(factor_one.shape),
        out_one.reshape(diag_one.shape),
        inv_two.reshape(factor_two.shape),
        out_parent.reshape(parent_block.shape),
        out_two.reshape(diag_two.shape),
    )


def solution(mesh):
    placed = (
        P(None, "row", None, None, "col", None),
        P(None, "row", None, None, "col", None),
        P(None, "row", None, None, "col", None),
        P(None, "col", None, None),
        P(None, "col", None, None),
        P(None, "col", None, None),
        P(None, "row", None, "col"),
        P(None, "row", None, "col"),
        P(None, "col"),
    )
    return jax.shard_map(
        body,
        mesh=mesh,
        in_specs=placed,
        out_specs=(
            P(None, "row", None, None, "col", None),
            P(None, "col", None, None),
            P(None, "row", None, None, "col", None),
            P(None, "col", None, None),
            P(None, "col", None, None),
        ),
        check_vma=False,
    )
```

time: 282 us -> 95.1 us (0.34)
  waiting for transfers between devices: 237 us -> 38.5 us
  starting transfers between devices: 0.21 us -> 40.4 us
  between operations: 15.2 us -> 2.19 us
  matrix products: 12 us -> 0 us
  Pallas kernels: 0 us -> 4.19 us
  local copies, waits for them, and re-layouts: 9.01 us -> 5.88 us
    psum x2 -> x0, waiting for transfers between devices: 143 us -> none  [the longest x1 73.2 us: body(): diag_sum, cross_sum = lax.psum((diag_part, cross_part), 'row')]
    all_gather x3 -> x0, waiting for transfers between devices: 94 us -> none  [the longest x1 45.8 us: body(): lax.all_gather(first_factor, 'row', axis=1, tiled=True)]
    ppermute x0 -> x20, starting transfers between devices: none -> 40.4 us  [send(): return lax.ppermute(value, AXES, pairs)]
    ppermute x0 -> x20, waiting for transfers between devices: none -> 38.5 us  [send(): return lax.ppermute(value, AXES, pairs)]
    dot_general x8 -> x0, matrix products: 12 us -> none  [the longest x2 4.32 us: add_rows(): return jnp.dot(left, right, preferred_element_type=jnp.float32)]
    pallas_call x0 -> x2, Pallas kernels: none -> 4.19 us  [the longest x1 2.5 us: body(): pl.pallas_call(finish_kernel, out_shape=(jax.ShapeDtypeStruct((2, block,...]
    all_gather x1 -> x0, local copies, waits for them, and re-layouts: 3.36 us -> none  [body(): lax.all_gather(first_factor, 'row', axis=1, tiled=True)]
    mul x3, other arithmetic: 4.05 us -> 1.14 us  [the longest x1 1.04 us: body(): masked = one * keep_one.astype(jnp.bfloat16)[None, :, None]]
  transfers between devices with their start and end apart: 5 -> 20, of which waited for: 5 -> 8; matrix products, arithmetic and copies ran while one was open for 8% -> 5% of each run, Pallas kernels for 0% -> 3%
where the time goes in v1:
time: 95.1 us; the launch traced here: 94.8 us
  starting transfers between devices  40.4 us (42%)
  waiting for transfers between devices  38.5 us (40%)
  local copies, waits for them, and re-layouts  5.88 us (6%)
  Pallas kernels  4.19 us (4%)
  other arithmetic  3.65 us (4%)
  between operations  2.19 us (2%)
    ppermute x20, starting transfers between devices, send(): return lax.ppermute(value, AXES, pairs)  40.4 us
    ppermute x20, waiting for transfers between devices, send(): return lax.ppermute(value, AXES, pairs)  38.5 us
    unnamed x14, local copies, waits for them, and re-layouts  3.22 us
    pallas_call x1, Pallas kernels, body(): pl.pallas_call(finish_kernel, out_shape=(jax.ShapeDtypeStruct((2, block,...  2.5 us
    dynamic_update_slice x3, local copies, waits for them, and re-layouts, body(): half = lax.dynamic_update_slice_in_dim(half, got, (z ^ d) * rows, axis=0)  1.91 us
  transfers between devices with their start and end apart: 20, of which 8 were waited for; matrix products, arithmetic and copies ran while one was open for 5% of the time, Pallas kernels for 3%

profile of v1, /device:TPU:1, one launch (start us, length us, event | category | flops | bytes accessed | tf_op | source)
XLA Modules:
  0.0 94.8 jit_solution(15504805306655231900)
XLA Ops:
  1.3 0.6 copy-done.5
  2.6 1.0 %bitcast_multiply_fusion = bf16[256,2,256]{2,0,1:T(8,128)(2,1)S(1)} fusion(bf16[1,1,256,2,1,256]{5,3,4,2,1,0:T(2,128)(2,1)} %param.10, bf16[2]{0:T(256)(128)(2,1)S(1)} %convert_bitcast_fusion), kind=kLoop, calls=%fused_computation.4 | loop fusion | flops 131072 | bytes 524292 | tf_op jit(solution)/shard_map/mul | solution.py:116
  3.7 0.9 copy-done.3
  4.6 4.7 %collective-permute-start.3 = (bf16[256,768]{1,0:T(8,128)(2,1)S(1)}, bf16[256,768]{1,0:T(8,128)(2,1)S(1)}, u32[]{:S(2)}, u32[]{:S(2)}) collective-permute-start(bf16[256,768]{1,0:T(8,128)(2,1)S(1)} %pad_maximum_fusion), channel_id=1, source_target_pairs={{0,0},{4,1},{2,2},{6,3},{1,4},{5,5},{3,6},{7,7},{8,8},{12,9},{10,1... | collective-permute-start | bytes 1179656 | tf_op jit(solution)/shard_map/ppermute | solution.py:24
  9.4 1.3 %collective-permute-start = (bf16[2,256,256]{2,1,0:T(8,128)(2,1)S(1)}, bf16[2,256,256]{2,1,0:T(8,128)(2,1)S(1)}, u32[]{:S(2)}, u32[]{:S(2)}) collective-permute-start(bf16[2,256,256]{2,1,0:T(8,128)(2,1)S(1)} %bitcast.38), channel_id=1, source_target_pairs={{2,0},{3,1},{0,2},{1,3},{6,4},{7,5},{4,6},{5,7},{10,8},{11,9},{8,1... | collective-permute-start | bytes 786440 | tf_op jit(solution)/shard_map/ppermute | solution.py:24
  10.6 2.2 %collective-permute-start.8 = (bf16[256,256]{1,0:T(8,128)(2,1)S(1)}, bf16[256,256]{1,0:T(8,128)(2,1)S(1)}, u32[]{:S(2)}, u32[]{:S(2)}) collective-permute-start(bf16[256,256]{1,0:T(8,128)(2,1)S(1)} %bitcast.45), channel_id=1, source_target_pairs={{0,0},{4,1},{2,2},{6,3},{1,4},{5,5},{3,6},{7,7},{8,8},{12,9},{10,1... | collective-permute-start | bytes 393224 | tf_op jit(solution)/shard_map/ppermute | solution.py:24
  12.9 2.5 %collective-permute-start.4 = (bf16[256,768]{1,0:T(8,128)(2,1)S(1)}, bf16[256,768]{1,0:T(8,128)(2,1)S(1)}, u32[]{:S(2)}, u32[]{:S(2)}) collective-permute-start(bf16[256,768]{1,0:T(8,128)(2,1)S(1)} %pad_maximum_fusion), channel_id=1, source_target_pairs={{8,0},{12,1},{10,2},{14,3},{9,4},{13,5},{11,6},{15,7},{0,8},{4,9},... | collective-permute-start | bytes 1179656 | tf_op jit(solution)/shard_map/ppermute | solution.py:24
  15.5 4.2 %collective-permute-done.8.refs_9_ = bf16[256,256]{1,0:T(8,128)(2,1)S(1)} collective-permute-done((bf16[256,256]{1,0:T(8,128)(2,1)S(1)}, bf16[256,256]{1,0:T(8,128)(2,1)S(1)}, u32[]{:S(2)}, u32[]{:S(2)}) %collective-permute-start.8) | collective-permute-done | bytes 131104 | tf_op jit(solution)/shard_map/ppermute | solution.py:24
  19.6 1.6 %collective-permute-start.5 = (bf16[256,768]{1,0:T(8,128)(2,1)S(1)}, bf16[256,768]{1,0:T(8,128)(2,1)S(1)}, u32[]{:S(2)}, u32[]{:S(2)}) collective-permute-start(bf16[256,768]{1,0:T(8,128)(2,1)S(1)} %pad_maximum_fusion), channel_id=1, source_target_pairs={{16,0},{20,1},{18,2},{22,3},{17,4},{21,5},{19,6},{23,7},{24,8},{28... | collective-permute-start | bytes 1179656 | tf_op jit(solution)/shard_map/ppermute | solution.py:24
  21.2 3.5 %collective-permute-start.6 = (bf16[256,768]{1,0:T(8,128)(2,1)S(1)}, bf16[256,768]{1,0:T(8,128)(2,1)S(1)}, u32[]{:S(2)}, u32[]{:S(2)}) collective-permute-start(bf16[256,768]{1,0:T(8,128)(2,1)S(1)} %pad_maximum_fusion), channel_id=1, source_target_pairs={{24,0},{28,1},{26,2},{30,3},{25,4},{29,5},{27,6},{31,7},{16,8},{20... | collective-permute-start | bytes 1179656 | tf_op jit(solution)/shard_map/ppermute | solution.py:24
  24.7 2.8 %collective-permute-start.2 = (bf16[2,256,256]{2,1,0:T(8,128)(2,1)S(1)}, bf16[2,256,256]{2,1,0:T(8,128)(2,1)S(1)}, u32[]{:S(2)}, u32[]{:S(2)}) collective-permute-start(bf16[2,256,256]{2,1,0:T(8,128)(2,1)S(1)} %bitcast.40), channel_id=1, source_target_pairs={{6,0},{7,1},{4,2},{5,3},{2,4},{3,5},{0,6},{1,7},{14,8},{15,9},{12,... | collective-permute-start | bytes 786440 | tf_op jit(solution)/shard_map/ppermute | solution.py:24
  27.6 7.5 %collective-permute-done.2.refs_3_ = bf16[2,256,256]{2,1,0:T(8,128)(2,1)S(1)} collective-permute-done((bf16[2,256,256]{2,1,0:T(8,128)(2,1)S(1)}, bf16[2,256,256]{2,1,0:T(8,128)(2,1)S(1)}, u32[]{:S(2)}, u32[]{:S(2)}) %collective-permute-start.2) | collective-permute-done | bytes 262176 | tf_op jit(solution)/shard_map/ppermute | solution.py:24
  35.1 13.2 %collective-permute-done.5.refs_6_ = bf16[256,768]{1,0:T(8,128)(2,1)S(1)} collective-permute-done((bf16[256,768]{1,0:T(8,128)(2,1)S(1)}, bf16[256,768]{1,0:T(8,128)(2,1)S(1)}, u32[]{:S(2)}, u32[]{:S(2)}) %collective-permute-start.5) | collective-permute-done | bytes 393248 | tf_op jit(solution)/shard_map/ppermute | solution.py:24
  48.3 1.7 %products.1 = (f32[256,768]{1,0:T(8,128)S(1)}, f32[256,768]{1,0:T(8,128)S(1)}, f32[512,256]{1,0:T(8,128)S(1)}, bf16[512,256]{1,0:T(8,128)(2,1)S(1)}) custom-call(bf16[2,256,256]{2,1,0:T(8,128)(2,1)S(1)} %bitcast.41, bf16[2,256,256]{2,1,0:T(8,128)(2,1)S(1)} %collective-permute-done.refs_1_, bf16[2,256,256]{2,1,0:T(8,128)(2,1)S(1)} %collective-permute-done.1.refs_2_, ...), custom_call_target="tpu_custom_call" | custom-call | tf_op jit(solution)/shard_map/products/pallas_call | solution.py:142
  50.5 1.2 %collective-permute-done.11 = bf16[512,256]{1,0:T(8,128)(2,1)} collective-permute-done((bf16[512,256]{1,0:T(8,128)(2,1)S(1)}, bf16[512,256]{1,0:T(8,128)(2,1)}, u32[]{:S(2)}, u32[]{:S(2)}) %collective-permute-start.11) | collective-permute-done | bytes 262176 | tf_op jit(solution)/shard_map/ppermute | solution.py:24
  51.7 1.0 %fusion.2 = (bf16[512,256]{1,0:T(8,128)(2,1)S(1)}, f32[512,256]{1,0:T(8,128)S(1)}) fusion(f32[512,256]{1,0:T(8,128)S(1)} %get-tuple-element.14, bf16[512,256]{1,0:T(8,128)(2,1)} %collective-permute-done.11), kind=kLoop, calls=%fused_computation.23 | loop fusion | flops 393216 | bytes 1572864 | tf_op jit(solution)/shard_map/convert_element_type | solution.py:170
  52.7 5.4 %collective-permute-start.12 = (bf16[128,256]{1,0:T(8,128)(2,1)S(1)}, bf16[128,256]{1,0:T(8,128)(2,1)S(1)}, u32[]{:S(2)}, u32[]{:S(2)}) collective-permute-start(bf16[128,256]{1,0:T(8,128)(2,1)S(1)} %get-tuple-element.31), channel_id=1, source_target_pairs={{8,0},{9,1},{10,2},{11,3},{12,4},{13,5},{14,6},{15,7},{0,8},{1,9},... | collective-permute-start | bytes 196616 | tf_op jit(solution)/shard_map/ppermute | solution.py:24
  58.4 1.9 %collective-permute-start.14 = (bf16[128,256]{1,0:T(8,128)(2,1)S(1)}, bf16[128,256]{1,0:T(8,128)(2,1)S(1)}, u32[]{:S(2)}, u32[]{:S(2)}) collective-permute-start(bf16[128,256]{1,0:T(8,128)(2,1)S(1)} %get-tuple-element.32), channel_id=1, source_target_pairs={{24,0},{25,1},{26,2},{27,3},{28,4},{29,5},{30,6},{31,7},{16,8},{17... | collective-permute-start | bytes 196616 | tf_op jit(solution)/shard_map/ppermute | solution.py:24
  60.4 5.0 %collective-permute-done.13 = bf16[128,256]{1,0:T(8,128)(2,1)S(1)} collective-permute-done((bf16[128,256]{1,0:T(8,128)(2,1)S(1)}, bf16[128,256]{1,0:T(8,128)(2,1)S(1)}, u32[]{:S(2)}, u32[]{:S(2)}) %collective-permute-start.13) | collective-permute-done | bytes 65568 | tf_op jit(solution)/shard_map/ppermute | solution.py:24
  65.4 0.7 broadcast_in_dim.2
  66.1 0.7 constant_dynamic-update-slice_fusion.3
  66.8 1.7 %collective-permute-start.15 = (bf16[128,256]{1,0:T(8,128)(2,1)S(1)}, bf16[128,256]{1,0:T(8,128)(2,1)S(1)}, u32[]{:S(2)}, u32[]{:S(2)}) collective-permute-start(bf16[128,256]{1,0:T(8,128)(2,1)S(1)} %get-tuple-element.25), channel_id=1, source_target_pairs={{8,0},{9,1},{10,2},{11,3},{12,4},{13,5},{14,6},{15,7},{0,8},{1,9},... | collective-permute-start | bytes 196616 | tf_op jit(solution)/shard_map/ppermute | solution.py:24
  68.6 2.0 %collective-permute-start.17 = (bf16[128,256]{1,0:T(8,128)(2,1)S(1)}, bf16[128,256]{1,0:T(8,128)(2,1)S(1)}, u32[]{:S(2)}, u32[]{:S(2)}) collective-permute-start(bf16[128,256]{1,0:T(8,128)(2,1)S(1)} %get-tuple-element.25), channel_id=1, source_target_pairs={{24,0},{25,1},{26,2},{27,3},{28,4},{29,5},{30,6},{31,7},{16,8},{17... | collective-permute-start | bytes 196616 | tf_op jit(solution)/shard_map/ppermute | solution.py:24
  71.3 6.6 %collective-permute-start.10 = (bf16[256,768]{1,0:T(8,128)(2,1)S(1)}, bf16[256,768]{1,0:T(8,128)(2,1)S(1)}, u32[]{:S(2)}, u32[]{:S(2)}) collective-permute-start(bf16[256,768]{1,0:T(8,128)(2,1)S(1)} %add_convert_fusion), channel_id=1, source_target_pairs={{0,0},{4,1},{2,2},{6,3},{1,4},{5,5},{3,6},{7,7},{8,8},{12,9},{10,1... | collective-permute-start | bytes 1179656 | tf_op jit(solution)/shard_map/ppermute | solution.py:24
  77.9 0.6 constant_dynamic-update-slice_fusion.1
  79.2 3.3 %collective-permute-start.18 = (bf16[512,256]{1,0:T(8,128)(2,1)}, bf16[512,256]{1,0:T(8,128)(2,1)S(1)}, u32[]{:S(2)}, u32[]{:S(2)}) collective-permute-start(bf16[512,256]{1,0:T(8,128)(2,1)} %constant_dynamic-update-slice_fusion), channel_id=1, source_target_pairs={{0,0},{4,1},{2,2},{6,3},{1,4},{5,5},{3,6},{7,7},{8,8},{12,9},{10,1... | collective-permute-start | bytes 786440 | tf_op jit(solution)/shard_map/ppermute | solution.py:24
  82.6 6.4 %collective-permute-done.18.first_ref = bf16[512,256]{1,0:T(8,128)(2,1)S(1)} collective-permute-done((bf16[512,256]{1,0:T(8,128)(2,1)}, bf16[512,256]{1,0:T(8,128)(2,1)S(1)}, u32[]{:S(2)}, u32[]{:S(2)}) %collective-permute-start.18) | collective-permute-done | bytes 262176 | tf_op jit(solution)/shard_map/ppermute | solution.py:24
  89.0 0.9 collective-permute-done.19.second_ref
  89.9 0.7 copy-done.2
  90.6 2.5 %finish.1 = (f32[2,256,256]{2,1,0:T(8,128)}, bf16[256,256]{1,0:T(8,128)(2,1)}, f32[256,256]{1,0:T(8,128)}) custom-call(bf16[512,256]{1,0:T(8,128)(2,1)} %copy-done.1, bf16[512,256]{1,0:T(8,128)(2,1)} %copy-done.2, f32[2,256,256]{2,1,0:T(8,128)} %bitcast.42, f32[256,256]{1,0:T(8,128)} %bitcast.43, bf16[256,256]{1,0:T(8,128)(2,1)} %bitcast.44, ...), custom_call_target="tpu_custom_call" | custom-call | tf_op jit(solution)/shard_map/finish/pallas_call | solution.py:192
  93.1 0.7 fusion
  93.8 1.0 %copy.16 = bf16[1,1,256,2,1,256]{5,3,4,2,1,0:T(2,128)(2,1)} copy(bf16[1,1,256,2,1,256]{5,2,4,3,1,0:T(8,128)(2,1)S(1)} %maximum_multiply_fusion) | data formatting | bytes 524288
  (40 shorter events, 2.8 us)
Async XLA Ops:
  1.3 0.7 copy-start.5
  3.7 0.9 copy-start.3
  4.6 4.7 %copy-start = (bf16[1,1,256,2,1,256]{5,3,4,2,1,0:T(2,128)(2,1)S(1)}, bf16[1,1,256,2,1,256]{5,3,4,2,1,0:T(2,128)(2,1)}, u32[]{:S(2)}) copy-start(bf16[1,1,256,2,1,256]{5,3,4,2,1,0:T(2,128)(2,1)} %param.9) | copy-start | bytes 786436
  4.6 6.0 %copy-start.4 = (bf16[1,1,256,256]{3,2,1,0:T(8,128)(2,1)S(1)}, bf16[1,1,256,256]{3,2,1,0:T(8,128)(2,1)}, u32[]{:S(2)}) copy-start(bf16[1,1,256,256]{3,2,1,0:T(8,128)(2,1)} %param.12) | copy-start | bytes 393220
  4.6 20.1 %collective-permute-start.3 = (bf16[256,768]{1,0:T(8,128)(2,1)S(1)}, bf16[256,768]{1,0:T(8,128)(2,1)S(1)}, u32[]{:S(2)}, u32[]{:S(2)}) collective-permute-start(bf16[256,768]{1,0:T(8,128)(2,1)S(1)} %pad_maximum_fusion), channel_id=1, source_target_pairs={{0,0},{4,1},{2,2},{6,3},{1,4},{5,5},{3,6},{7,7},{8,8},{12,9},{10,1... | collective-permute-start | bytes 1179656 | tf_op jit(solution)/shard_map/ppermute | solution.py:24
  9.4 11.9 %collective-permute-start = (bf16[2,256,256]{2,1,0:T(8,128)(2,1)S(1)}, bf16[2,256,256]{2,1,0:T(8,128)(2,1)S(1)}, u32[]{:S(2)}, u32[]{:S(2)}) collective-permute-start(bf16[2,256,256]{2,1,0:T(8,128)(2,1)S(1)} %bitcast.38), channel_id=1, source_target_pairs={{2,0},{3,1},{0,2},{1,3},{6,4},{7,5},{4,6},{5,7},{10,8},{11,9},{8,1... | collective-permute-start | bytes 786440 | tf_op jit(solution)/shard_map/ppermute | solution.py:24
  10.6 9.0 %collective-permute-start.8 = (bf16[256,256]{1,0:T(8,128)(2,1)S(1)}, bf16[256,256]{1,0:T(8,128)(2,1)S(1)}, u32[]{:S(2)}, u32[]{:S(2)}) collective-permute-start(bf16[256,256]{1,0:T(8,128)(2,1)S(1)} %bitcast.45), channel_id=1, source_target_pairs={{0,0},{4,1},{2,2},{6,3},{1,4},{5,5},{3,6},{7,7},{8,8},{12,9},{10,1... | collective-permute-start | bytes 393224 | tf_op jit(solution)/shard_map/ppermute | solution.py:24
  12.8 11.9 %collective-permute-start.1 = (bf16[2,256,256]{2,1,0:T(8,128)(2,1)S(1)}, bf16[2,256,256]{2,1,0:T(8,128)(2,1)S(1)}, u32[]{:S(2)}, u32[]{:S(2)}) collective-permute-start(bf16[2,256,256]{2,1,0:T(8,128)(2,1)S(1)} %bitcast.39), channel_id=1, source_target_pairs={{4,0},{5,1},{6,2},{7,3},{0,4},{1,5},{2,6},{3,7},{12,8},{13,9},{14,... | collective-permute-start | bytes 786440 | tf_op jit(solution)/shard_map/ppermute | solution.py:24
  12.9 22.1 %collective-permute-start.4 = (bf16[256,768]{1,0:T(8,128)(2,1)S(1)}, bf16[256,768]{1,0:T(8,128)(2,1)S(1)}, u32[]{:S(2)}, u32[]{:S(2)}) collective-permute-start(bf16[256,768]{1,0:T(8,128)(2,1)S(1)} %pad_maximum_fusion), channel_id=1, source_target_pairs={{8,0},{12,1},{10,2},{14,3},{9,4},{13,5},{11,6},{15,7},{0,8},{4,9},... | collective-permute-start | bytes 1179656 | tf_op jit(solution)/shard_map/ppermute | solution.py:24
  19.6 28.6 %collective-permute-start.5 = (bf16[256,768]{1,0:T(8,128)(2,1)S(1)}, bf16[256,768]{1,0:T(8,128)(2,1)S(1)}, u32[]{:S(2)}, u32[]{:S(2)}) collective-permute-start(bf16[256,768]{1,0:T(8,128)(2,1)S(1)} %pad_maximum_fusion), channel_id=1, source_target_pairs={{16,0},{20,1},{18,2},{22,3},{17,4},{21,5},{19,6},{23,7},{24,8},{28... | collective-permute-start | bytes 1179656 | tf_op jit(solution)/shard_map/ppermute | solution.py:24
  21.2 27.0 %collective-permute-start.6 = (bf16[256,768]{1,0:T(8,128)(2,1)S(1)}, bf16[256,768]{1,0:T(8,128)(2,1)S(1)}, u32[]{:S(2)}, u32[]{:S(2)}) collective-permute-start(bf16[256,768]{1,0:T(8,128)(2,1)S(1)} %pad_maximum_fusion), channel_id=1, source_target_pairs={{24,0},{28,1},{26,2},{30,3},{25,4},{29,5},{27,6},{31,7},{16,8},{20... | collective-permute-start | bytes 1179656 | tf_op jit(solution)/shard_map/ppermute | solution.py:24
  24.7 23.5 %collective-permute-start.7 = (bf16[256,768]{1,0:T(8,128)(2,1)S(1)}, bf16[256,768]{1,0:T(8,128)(2,1)S(1)}, u32[]{:S(2)}, u32[]{:S(2)}) collective-permute-start(bf16[256,768]{1,0:T(8,128)(2,1)S(1)} %collective-permute-done.3.refs_4_), channel_id=1, source_target_pairs={{1,0},{0,1},{3,2},{2,3},{5,4},{4,5},{7,6},{6,7},{9,8},{8,9},{11,10... | collective-permute-start | bytes 1179656 | tf_op jit(solution)/shard_map/ppermute | solution.py:24
  24.7 10.3 %collective-permute-start.2 = (bf16[2,256,256]{2,1,0:T(8,128)(2,1)S(1)}, bf16[2,256,256]{2,1,0:T(8,128)(2,1)S(1)}, u32[]{:S(2)}, u32[]{:S(2)}) collective-permute-start(bf16[2,256,256]{2,1,0:T(8,128)(2,1)S(1)} %bitcast.40), channel_id=1, source_target_pairs={{6,0},{7,1},{4,2},{5,3},{2,4},{3,5},{0,6},{1,7},{14,8},{15,9},{12,... | collective-permute-start | bytes 786440 | tf_op jit(solution)/shard_map/ppermute | solution.py:24
  49.9 1.7 %collective-permute-start.11 = (bf16[512,256]{1,0:T(8,128)(2,1)S(1)}, bf16[512,256]{1,0:T(8,128)(2,1)}, u32[]{:S(2)}, u32[]{:S(2)}) collective-permute-start(bf16[512,256]{1,0:T(8,128)(2,1)S(1)} %get-tuple-element.15), channel_id=1, source_target_pairs={{1,0},{0,1},{3,2},{2,3},{5,4},{4,5},{7,6},{6,7},{9,8},{8,9},{11,10... | collective-permute-start | bytes 786440 | tf_op jit(solution)/shard_map/ppermute | solution.py:24
  50.1 21.2 %collective-permute-start.9 = (f32[256,768]{1,0:T(8,128)S(1)}, f32[256,768]{1,0:T(8,128)S(1)}, u32[]{:S(2)}, u32[]{:S(2)}) collective-permute-start(f32[256,768]{1,0:T(8,128)S(1)} %get-tuple-element.13), channel_id=1, source_target_pairs={{1,0},{0,1},{3,2},{2,3},{5,4},{4,5},{7,6},{6,7},{9,8},{8,9},{11,10... | collective-permute-start | bytes 2359304 | tf_op jit(solution)/shard_map/ppermute | solution.py:24
  52.7 7.7 %collective-permute-start.12 = (bf16[128,256]{1,0:T(8,128)(2,1)S(1)}, bf16[128,256]{1,0:T(8,128)(2,1)S(1)}, u32[]{:S(2)}, u32[]{:S(2)}) collective-permute-start(bf16[128,256]{1,0:T(8,128)(2,1)S(1)} %get-tuple-element.31), channel_id=1, source_target_pairs={{8,0},{9,1},{10,2},{11,3},{12,4},{13,5},{14,6},{15,7},{0,8},{1,9},... | collective-permute-start | bytes 196616 | tf_op jit(solution)/shard_map/ppermute | solution.py:24
  58.1 7.3 %collective-permute-start.13 = (bf16[128,256]{1,0:T(8,128)(2,1)S(1)}, bf16[128,256]{1,0:T(8,128)(2,1)S(1)}, u32[]{:S(2)}, u32[]{:S(2)}) collective-permute-start(bf16[128,256]{1,0:T(8,128)(2,1)S(1)} %get-tuple-element.33), channel_id=1, source_target_pairs={{16,0},{17,1},{18,2},{19,3},{20,4},{21,5},{22,6},{23,7},{24,8},{25... | collective-permute-start | bytes 196616 | tf_op jit(solution)/shard_map/ppermute | solution.py:24
  58.4 7.0 %collective-permute-start.14 = (bf16[128,256]{1,0:T(8,128)(2,1)S(1)}, bf16[128,256]{1,0:T(8,128)(2,1)S(1)}, u32[]{:S(2)}, u32[]{:S(2)}) collective-permute-start(bf16[128,256]{1,0:T(8,128)(2,1)S(1)} %get-tuple-element.32), channel_id=1, source_target_pairs={{24,0},{25,1},{26,2},{27,3},{28,4},{29,5},{30,6},{31,7},{16,8},{17... | collective-permute-start | bytes 196616 | tf_op jit(solution)/shard_map/ppermute | solution.py:24
  66.8 3.8 %collective-permute-start.15 = (bf16[128,256]{1,0:T(8,128)(2,1)S(1)}, bf16[128,256]{1,0:T(8,128)(2,1)S(1)}, u32[]{:S(2)}, u32[]{:S(2)}) collective-permute-start(bf16[128,256]{1,0:T(8,128)(2,1)S(1)} %get-tuple-element.25), channel_id=1, source_target_pairs={{8,0},{9,1},{10,2},{11,3},{12,4},{13,5},{14,6},{15,7},{0,8},{1,9},... | collective-permute-start | bytes 196616 | tf_op jit(solution)/shard_map/ppermute | solution.py:24
  68.5 9.4 %collective-permute-start.16 = (bf16[128,256]{1,0:T(8,128)(2,1)S(1)}, bf16[128,256]{1,0:T(8,128)(2,1)S(1)}, u32[]{:S(2)}, u32[]{:S(2)}) collective-permute-start(bf16[128,256]{1,0:T(8,128)(2,1)S(1)} %get-tuple-element.25), channel_id=1, source_target_pairs={{16,0},{17,1},{18,2},{19,3},{20,4},{21,5},{22,6},{23,7},{24,8},{25... | collective-permute-start | bytes 196616 | tf_op jit(solution)/shard_map/ppermute | solution.py:24
  68.6 10.0 %collective-permute-start.17 = (bf16[128,256]{1,0:T(8,128)(2,1)S(1)}, bf16[128,256]{1,0:T(8,128)(2,1)S(1)}, u32[]{:S(2)}, u32[]{:S(2)}) collective-permute-start(bf16[128,256]{1,0:T(8,128)(2,1)S(1)} %get-tuple-element.25), channel_id=1, source_target_pairs={{24,0},{25,1},{26,2},{27,3},{28,4},{29,5},{30,6},{31,7},{16,8},{17... | collective-permute-start | bytes 196616 | tf_op jit(solution)/shard_map/ppermute | solution.py:24
  71.3 21.8 %collective-permute-start.10 = (bf16[256,768]{1,0:T(8,128)(2,1)S(1)}, bf16[256,768]{1,0:T(8,128)(2,1)S(1)}, u32[]{:S(2)}, u32[]{:S(2)}) collective-permute-start(bf16[256,768]{1,0:T(8,128)(2,1)S(1)} %add_convert_fusion), channel_id=1, source_target_pairs={{0,0},{4,1},{2,2},{6,3},{1,4},{5,5},{3,6},{7,7},{8,8},{12,9},{10,1... | collective-permute-start | bytes 1179656 | tf_op jit(solution)/shard_map/ppermute | solution.py:24
  79.2 9.8 %collective-permute-start.18 = (bf16[512,256]{1,0:T(8,128)(2,1)}, bf16[512,256]{1,0:T(8,128)(2,1)S(1)}, u32[]{:S(2)}, u32[]{:S(2)}) collective-permute-start(bf16[512,256]{1,0:T(8,128)(2,1)} %constant_dynamic-update-slice_fusion), channel_id=1, source_target_pairs={{0,0},{4,1},{2,2},{6,3},{1,4},{5,5},{3,6},{7,7},{8,8},{12,9},{10,1... | collective-permute-start | bytes 786440 | tf_op jit(solution)/shard_map/ppermute | solution.py:24
  82.5 7.4 %collective-permute-start.19 = (bf16[512,256]{1,0:T(8,128)(2,1)}, bf16[512,256]{1,0:T(8,128)(2,1)S(1)}, u32[]{:S(2)}, u32[]{:S(2)}) collective-permute-start(bf16[512,256]{1,0:T(8,128)(2,1)} %constant_dynamic-update-slice_fusion), channel_id=1, source_target_pairs={{1,0},{5,1},{3,2},{7,3},{0,4},{4,5},{2,6},{6,7},{9,8},{13,9},{11,1... | collective-permute-start | bytes 786440 | tf_op jit(solution)/shard_map/ppermute | solution.py:24
  89.0 0.9 copy-start.1
  89.9 0.7 copy-start.2

commit v2 on v1

--- a/solution.py
+++ b/solution.py
@@ -42,6 +42,7 @@
     keep_y, send_y, keep_g, send_g, a_all, x_all, x_row, y_all, g_all = refs[2 * wide + high + 2 :]
     block = other_ref.shape[0]
     z, y, x, k = place()
+    low = z % 2
     turn = z ^ x
     swap = y ^ k
     for step in range(high):
@@ -63,32 +64,36 @@
     )
     y_all[:, : 2 * block] = total[:, : 2 * block]
     y_all[:, 2 * block :] = last
-    g_all[:block] = tdot(x_row[:, :block], near)
-    g_all[block : 2 * block] = tdot(x_row[:, block : 2 * block], far.astype(jnp.bfloat16))
-    g_all[2 * block : 3 * block] = tdot(near, x_row[:, 2 * block :])
-    g_all[3 * block :] = tdot(x_row[:, 2 * block :], last.astype(jnp.bfloat16))
+    g_all[0] = tdot(x_row[:, :block], near)
+    g_all[1] = tdot(x_row[:, block : 2 * block], far.astype(jnp.bfloat16))
+    g_all[2] = tdot(near, x_row[:, 2 * block :])
+    g_all[3] = tdot(x_row[:, 2 * block :], last.astype(jnp.bfloat16))
     keep_y[...] = y_all[pl.ds(pl.multiple_of(swap * block, block), block), :]
     send_y[...] = y_all[pl.ds(pl.multiple_of((1 - swap) * block, block), block), :]
-    keep_g[...] = g_all[pl.ds(pl.multiple_of(k * 2 * block, block), 2 * block), :]
-    send_g[...] = g_all[pl.ds(pl.multiple_of((1 - k) * 2 * block, block), 2 * block), :].astype(
-        jnp.bfloat16
-    )
-
-
-def finish_kernel(first_ref, second_ref, one_ref, two_ref, couple_ref, which_ref, out_one, out_parent, out_two, terms):
-    block = couple_ref.shape[0]
+    keep_g[:block] = g_all[2 * k + low]
+    keep_g[block:] = g_all[2 * k + 1 - low]
+    send_g[:block] = g_all[2 * (1 - k) + low].astype(jnp.bfloat16)
+    send_g[block:] = g_all[2 * (1 - k) + 1 - low].astype(jnp.bfloat16)
+
+
+def finish_kernel(*refs):
+    got_refs = refs[:4]
+    one_ref, two_ref, couple_ref, which_ref, out_one, out_parent, out_two, terms = refs[4:]
     z, y, x, k = place()
-    terms[y] = first_ref[...].astype(jnp.float32)
-    terms[1 - y] = second_ref[...].astype(jnp.float32)
+    low = z % 2
+    for i, ref in enumerate(got_refs):
+        terms[2 * (y ^ (i % 2)) + (low ^ (i // 2))] = ref[...].astype(jnp.float32)
     near = which_ref[0]
-    out_one[near] = one_ref[near] + terms[0, :block]
-    out_one[1 - near] = one_ref[1 - near] + terms[0, block:]
+    one = one_ref[near] + terms[0]
+    out_one[near] = one
+    out_one[1 - near] = one_ref[1 - near] + terms[1]
     couple = couple_ref[...]
-    diag = out_one[near].astype(jnp.bfloat16)
-    parent = -(jnp.dot(diag, couple, preferred_element_type=jnp.float32) - terms[1, :block])
+    parent = -(
+        jnp.dot(one.astype(jnp.bfloat16), couple, preferred_element_type=jnp.float32) - terms[2]
+    )
     parent = parent.astype(jnp.bfloat16)
     out_parent[...] = parent
-    out_two[...] = two_ref[...] + terms[1, block:] - tdot(couple, parent)
+    out_two[...] = two_ref[...] + terms[3] - tdot(couple, parent)
 
 
 def body(
@@ -152,7 +157,7 @@
             pltpu.VMEM((high * block, width), jnp.bfloat16),
             pltpu.VMEM((2 * block, width), jnp.bfloat16),
             pltpu.VMEM((2 * block, width), jnp.float32),
-            pltpu.VMEM((4 * block, block), jnp.float32),
+            pltpu.VMEM((4, block, block), jnp.float32),
         ],
         compiler_params=pltpu.CompilerParams(vmem_limit_bytes=48 * 1024 * 1024),
         name="products",
@@ -161,25 +166,21 @@
     def core_swap(value):
         return send(value, sizes, lambda z, y, x, k: (z, y, x, 1 - k))
 
-    mine = keep_g + core_swap(send_g).astype(jnp.float32)
-    rows = 2 * block // high
-
-    def part(value, at):
-        return lax.dynamic_slice_in_dim(value, at * rows, rows, axis=0)
-
-    coarse = mine.astype(jnp.bfloat16)
-    share = part(mine, z)
-    for d in range(1, high):
-        got = send(part(coarse, z ^ d), sizes, lambda z, y, x, k, d=d: (z ^ d, y, x, k))
-        share = share + got.astype(jnp.float32)
-    share = share.astype(jnp.bfloat16)
-    half = jnp.zeros((2 * block, block), jnp.bfloat16)
-    half = lax.dynamic_update_slice_in_dim(half, share, z * rows, axis=0)
-    for d in range(1, high):
-        got = send(share, sizes, lambda z, y, x, k, d=d: (z ^ d, y, x, k))
-        half = lax.dynamic_update_slice_in_dim(half, got, (z ^ d) * rows, axis=0)
-    first = send(half, sizes, lambda z, y, x, k: (z, k, x, y))
-    second = send(half, sizes, lambda z, y, x, k: (z, k, x, 1 - y))
+    def along(value, d):
+        return send(value, sizes, lambda z, y, x, k: (z ^ d, y, x, k))
+
+    chip = keep_g + core_swap(send_g).astype(jnp.float32)
+    total = chip[:block] + along(chip[block:].astype(jnp.bfloat16), 1).astype(jnp.float32)
+    total = total.astype(jnp.bfloat16)
+    d = 2
+    while d < high:
+        total = (total.astype(jnp.float32) + along(total, d).astype(jnp.float32)).astype(jnp.bfloat16)
+        d *= 2
+    terms = [
+        send(total, sizes, lambda z, y, x, k, d=d, e=e: (z ^ d, k, x, y ^ e))
+        for d in range(2)
+        for e in range(2)
+    ]
 
     row_y = (keep_y + core_swap(send_y)).astype(jnp.bfloat16)
     row_y = send(row_y, sizes, lambda z, y, x, k: (z, k, x, y))
@@ -196,13 +197,12 @@
             jax.ShapeDtypeStruct((block, block), jnp.bfloat16),
             jax.ShapeDtypeStruct((block, block), jnp.float32),
         ),
-        in_specs=[pl.BlockSpec(memory_space=pltpu.VMEM)] * 5
+        in_specs=[pl.BlockSpec(memory_space=pltpu.VMEM)] * 7
         + [pl.BlockSpec(memory_space=pltpu.SMEM)],
-        scratch_shapes=[pltpu.VMEM((2, 2 * block, block), jnp.float32)],
+        scratch_shapes=[pltpu.VMEM((4, block, block), jnp.float32)],
         name="finish",
     )(
-        first,
-        second,
+        *terms,
         diag_one.reshape(2, block, block),
         diag_two.reshape(block, block),
         coupling,

time: 95.1 us -> 88.4 us (0.930)
  local copies, waits for them, and re-layouts: 5.88 us -> 3.19 us
  other arithmetic: 3.65 us -> 2.09 us
  waiting for transfers between devices: 38.5 us -> 37.2 us
  starting transfers between devices: 40.4 us -> 39.2 us
    dynamic_update_slice x3 -> x0, local copies, waits for them, and re-layouts: 1.91 us -> none  [body(): half = lax.dynamic_update_slice_in_dim(half, got, (z ^ d) * rows, axis=0)]
    ppermute x20 -> x18, waiting for transfers between devices: 38.5 us -> 37.2 us  [send(): return lax.ppermute(value, AXES, pairs)]
    ppermute x20 -> x18, starting transfers between devices: 40.4 us -> 39.2 us  [send(): return lax.ppermute(value, AXES, pairs)]
    convert_element_type x1 -> x2, other arithmetic: 1.01 us -> 0.06 us  [the longest x1 0.03 us: body(): (total.astype(jnp.float32) + along(total, d).astype(jnp.float32)).astype(...]
    unnamed x14 -> x18, local copies, waits for them, and re-layouts: 3.22 us -> 3.17 us
  transfers between devices with their start and end apart: 20 -> 18, of which waited for: 8 -> 10; matrix products, arithmetic and copies ran while one was open for 5% -> 0% of each run, Pallas kernels for 3% -> 3%
where the time goes in v2:
time: 88.4 us; the launch traced here: 88.1 us
  starting transfers between devices  39.2 us (44%)
  waiting for transfers between devices  37.2 us (42%)
  Pallas kernels  4.23 us (5%)
  local copies, waits for them, and re-layouts  3.19 us (4%)
  between operations  2.15 us (2%)
  other arithmetic  2.09 us (2%)
    ppermute x18, starting transfers between devices, send(): return lax.ppermute(value, AXES, pairs)  39.2 us
    ppermute x18, waiting for transfers between devices, send(): return lax.ppermute(value, AXES, pairs)  37.2 us
    unnamed x18, local copies, waits for them, and re-layouts  3.17 us
    pallas_call x1, Pallas kernels, body(): pl.pallas_call(finish_kernel, out_shape=(jax.ShapeDtypeStruct((2, block,...  2.65 us
  transfers between devices with their start and end apart: 18, of which 10 were waited for; matrix products, arithmetic and copies ran while one was open for 0% of the time, Pallas kernels for 3%

profile of v2, /device:TPU:1, one launch (start us, length us, event | category | flops | bytes accessed | tf_op | source)
XLA Modules:
  0.0 88.1 jit_solution(12895101042869914198)
XLA Ops:
  1.3 0.6 copy-done.7
  2.6 1.0 %bitcast_multiply_fusion = bf16[256,2,256]{2,0,1:T(8,128)(2,1)S(1)} fusion(bf16[1,1,256,2,1,256]{5,3,4,2,1,0:T(2,128)(2,1)} %param.10, bf16[2]{0:T(256)(128)(2,1)S(1)} %convert_bitcast_fusion), kind=kLoop, calls=%fused_computation.7 | loop fusion | flops 131072 | bytes 524292 | tf_op jit(solution)/shard_map/mul | solution.py:121
  3.7 0.9 copy-done.1
  4.6 4.7 %collective-permute-start.3 = (bf16[256,768]{1,0:T(8,128)(2,1)S(1)}, bf16[256,768]{1,0:T(8,128)(2,1)S(1)}, u32[]{:S(2)}, u32[]{:S(2)}) collective-permute-start(bf16[256,768]{1,0:T(8,128)(2,1)S(1)} %pad_maximum_fusion), channel_id=1, source_target_pairs={{0,0},{4,1},{2,2},{6,3},{1,4},{5,5},{3,6},{7,7},{8,8},{12,9},{10,1... | collective-permute-start | bytes 1179656 | tf_op jit(solution)/shard_map/ppermute | solution.py:24
  9.4 1.3 %collective-permute-start = (bf16[2,256,256]{2,1,0:T(8,128)(2,1)S(1)}, bf16[2,256,256]{2,1,0:T(8,128)(2,1)S(1)}, u32[]{:S(2)}, u32[]{:S(2)}) collective-permute-start(bf16[2,256,256]{2,1,0:T(8,128)(2,1)S(1)} %bitcast.38), channel_id=1, source_target_pairs={{2,0},{3,1},{0,2},{1,3},{6,4},{7,5},{4,6},{5,7},{10,8},{11,9},{8,1... | collective-permute-start | bytes 786440 | tf_op jit(solution)/shard_map/ppermute | solution.py:24
  10.6 2.2 %collective-permute-start.8 = (bf16[256,256]{1,0:T(8,128)(2,1)S(1)}, bf16[256,256]{1,0:T(8,128)(2,1)S(1)}, u32[]{:S(2)}, u32[]{:S(2)}) collective-permute-start(bf16[256,256]{1,0:T(8,128)(2,1)S(1)} %bitcast.45), channel_id=1, source_target_pairs={{0,0},{4,1},{2,2},{6,3},{1,4},{5,5},{3,6},{7,7},{8,8},{12,9},{10,1... | collective-permute-start | bytes 393224 | tf_op jit(solution)/shard_map/ppermute | solution.py:24
  12.9 2.5 %collective-permute-start.4 = (bf16[256,768]{1,0:T(8,128)(2,1)S(1)}, bf16[256,768]{1,0:T(8,128)(2,1)S(1)}, u32[]{:S(2)}, u32[]{:S(2)}) collective-permute-start(bf16[256,768]{1,0:T(8,128)(2,1)S(1)} %pad_maximum_fusion), channel_id=1, source_target_pairs={{8,0},{12,1},{10,2},{14,3},{9,4},{13,5},{11,6},{15,7},{0,8},{4,9},... | collective-permute-start | bytes 1179656 | tf_op jit(solution)/shard_map/ppermute | solution.py:24
  15.5 4.2 %collective-permute-done.8.refs_9_ = bf16[256,256]{1,0:T(8,128)(2,1)S(1)} collective-permute-done((bf16[256,256]{1,0:T(8,128)(2,1)S(1)}, bf16[256,256]{1,0:T(8,128)(2,1)S(1)}, u32[]{:S(2)}, u32[]{:S(2)}) %collective-permute-start.8) | collective-permute-done | bytes 131104 | tf_op jit(solution)/shard_map/ppermute | solution.py:24
  19.6 1.6 %collective-permute-start.5 = (bf16[256,768]{1,0:T(8,128)(2,1)S(1)}, bf16[256,768]{1,0:T(8,128)(2,1)S(1)}, u32[]{:S(2)}, u32[]{:S(2)}) collective-permute-start(bf16[256,768]{1,0:T(8,128)(2,1)S(1)} %pad_maximum_fusion), channel_id=1, source_target_pairs={{16,0},{20,1},{18,2},{22,3},{17,4},{21,5},{19,6},{23,7},{24,8},{28... | collective-permute-start | bytes 1179656 | tf_op jit(solution)/shard_map/ppermute | solution.py:24
  21.2 3.5 %collective-permute-start.6 = (bf16[256,768]{1,0:T(8,128)(2,1)S(1)}, bf16[256,768]{1,0:T(8,128)(2,1)S(1)}, u32[]{:S(2)}, u32[]{:S(2)}) collective-permute-start(bf16[256,768]{1,0:T(8,128)(2,1)S(1)} %pad_maximum_fusion), channel_id=1, source_target_pairs={{24,0},{28,1},{26,2},{30,3},{25,4},{29,5},{27,6},{31,7},{16,8},{20... | collective-permute-start | bytes 1179656 | tf_op jit(solution)/shard_map/ppermute | solution.py:24
  24.7 2.8 %collective-permute-start.2 = (bf16[2,256,256]{2,1,0:T(8,128)(2,1)S(1)}, bf16[2,256,256]{2,1,0:T(8,128)(2,1)S(1)}, u32[]{:S(2)}, u32[]{:S(2)}) collective-permute-start(bf16[2,256,256]{2,1,0:T(8,128)(2,1)S(1)} %bitcast.40), channel_id=1, source_target_pairs={{6,0},{7,1},{4,2},{5,3},{2,4},{3,5},{0,6},{1,7},{14,8},{15,9},{12,... | collective-permute-start | bytes 786440 | tf_op jit(solution)/shard_map/ppermute | solution.py:24
  27.6 7.5 %collective-permute-done.2.refs_3_ = bf16[2,256,256]{2,1,0:T(8,128)(2,1)S(1)} collective-permute-done((bf16[2,256,256]{2,1,0:T(8,128)(2,1)S(1)}, bf16[2,256,256]{2,1,0:T(8,128)(2,1)S(1)}, u32[]{:S(2)}, u32[]{:S(2)}) %collective-permute-start.2) | collective-permute-done | bytes 262176 | tf_op jit(solution)/shard_map/ppermute | solution.py:24
  35.1 13.2 %collective-permute-done.5.refs_6_ = bf16[256,768]{1,0:T(8,128)(2,1)S(1)} collective-permute-done((bf16[256,768]{1,0:T(8,128)(2,1)S(1)}, bf16[256,768]{1,0:T(8,128)(2,1)S(1)}, u32[]{:S(2)}, u32[]{:S(2)}) %collective-permute-start.5) | collective-permute-done | bytes 393248 | tf_op jit(solution)/shard_map/ppermute | solution.py:24
  48.3 1.6 %products.1 = (f32[256,768]{1,0:T(8,128)S(1)}, f32[256,768]{1,0:T(8,128)S(1)}, f32[512,256]{1,0:T(8,128)S(1)}, bf16[512,256]{1,0:T(8,128)(2,1)S(1)}) custom-call(bf16[2,256,256]{2,1,0:T(8,128)(2,1)S(1)} %bitcast.41, bf16[2,256,256]{2,1,0:T(8,128)(2,1)S(1)} %collective-permute-done.refs_1_, bf16[2,256,256]{2,1,0:T(8,128)(2,1)S(1)} %collective-permute-done.1.refs_2_, ...), custom_call_target="tpu_custom_call" | custom-call | tf_op jit(solution)/shard_map/products/pallas_call | solution.py:147
  49.9 0.5 collective-permute-start.9
  50.4 1.0 %collective-permute-done.11 = bf16[512,256]{1,0:T(8,128)(2,1)S(1)} collective-permute-done((bf16[512,256]{1,0:T(8,128)(2,1)S(1)}, bf16[512,256]{1,0:T(8,128)(2,1)S(1)}, u32[]{:S(2)}, u32[]{:S(2)}) %collective-permute-start.11) | collective-permute-done | bytes 262176 | tf_op jit(solution)/shard_map/ppermute | solution.py:24
  51.5 5.4 %collective-permute-start.12 = (bf16[256,256]{1,0:T(8,128)(2,1)S(1)}, bf16[256,256]{1,0:T(8,128)(2,1)S(1)}, u32[]{:S(2)}, u32[]{:S(2)}) collective-permute-start(bf16[256,256]{1,0:T(8,128)(2,1)S(1)} %slice.51), channel_id=1, source_target_pairs={{8,0},{9,1},{10,2},{11,3},{12,4},{13,5},{14,6},{15,7},{0,8},{1,9},... | collective-permute-start | bytes 393224 | tf_op jit(solution)/shard_map/ppermute | solution.py:24
  56.9 3.7 %collective-permute-done.12 = bf16[256,256]{1,0:T(8,128)(2,1)S(1)} collective-permute-done((bf16[256,256]{1,0:T(8,128)(2,1)S(1)}, bf16[256,256]{1,0:T(8,128)(2,1)S(1)}, u32[]{:S(2)}, u32[]{:S(2)}) %collective-permute-start.12) | collective-permute-done | bytes 131104 | tf_op jit(solution)/shard_map/ppermute | solution.py:24
  60.6 1.5 %collective-permute-start.13 = (bf16[256,256]{1,0:T(8,128)(2,1)S(1)}, bf16[256,256]{1,0:T(8,128)(2,1)S(1)}, u32[]{:S(2)}, u32[]{:S(2)}) collective-permute-start(bf16[256,256]{1,0:T(8,128)(2,1)S(1)} %fusion), channel_id=1, source_target_pairs={{16,0},{17,1},{18,2},{19,3},{20,4},{21,5},{22,6},{23,7},{24,8},{25... | collective-permute-start | bytes 393224 | tf_op jit(solution)/shard_map/ppermute | solution.py:24
  62.2 5.9 %collective-permute-start.10 = (bf16[256,768]{1,0:T(8,128)(2,1)S(1)}, bf16[256,768]{1,0:T(8,128)(2,1)S(1)}, u32[]{:S(2)}, u32[]{:S(2)}) collective-permute-start(bf16[256,768]{1,0:T(8,128)(2,1)S(1)} %add_convert_fusion), channel_id=1, source_target_pairs={{0,0},{4,1},{2,2},{6,3},{1,4},{5,5},{3,6},{7,7},{8,8},{12,9},{10,1... | collective-permute-start | bytes 1179656 | tf_op jit(solution)/shard_map/ppermute | solution.py:24
  68.2 0.7 collective-permute-done.13
  68.9 5.2 %collective-permute-start.14 = (bf16[256,256]{1,0:T(8,128)(2,1)S(1)}, bf16[256,256]{1,0:T(8,128)(2,1)S(1)}, u32[]{:S(2)}, u32[]{:S(2)}) collective-permute-start(bf16[256,256]{1,0:T(8,128)(2,1)S(1)} %add_convert_fusion.1), channel_id=1, source_target_pairs={{0,0},{4,1},{2,2},{6,3},{1,4},{5,5},{3,6},{7,7},{8,8},{12,9},{10,1... | collective-permute-start | bytes 393224 | tf_op jit(solution)/shard_map/ppermute | solution.py:24
  74.2 1.9 %collective-permute-start.17 = (bf16[256,256]{1,0:T(8,128)(2,1)S(1)}, bf16[256,256]{1,0:T(8,128)(2,1)S(1)}, u32[]{:S(2)}, u32[]{:S(2)}) collective-permute-start(bf16[256,256]{1,0:T(8,128)(2,1)S(1)} %add_convert_fusion.1), channel_id=1, source_target_pairs={{9,0},{13,1},{11,2},{15,3},{8,4},{12,5},{10,6},{14,7},{1,8},{5,9},... | collective-permute-start | bytes 393224 | tf_op jit(solution)/shard_map/ppermute | solution.py:24
  76.2 1.9 %collective-permute-done.14.refs_0_ = bf16[256,256]{1,0:T(8,128)(2,1)S(1)} collective-permute-done((bf16[256,256]{1,0:T(8,128)(2,1)S(1)}, bf16[256,256]{1,0:T(8,128)(2,1)S(1)}, u32[]{:S(2)}, u32[]{:S(2)}) %collective-permute-start.14) | collective-permute-done | bytes 131104 | tf_op jit(solution)/shard_map/ppermute | solution.py:24
  78.1 0.4 collective-permute-done.15.refs_1_
  78.5 2.3 %collective-permute-done.16.refs_2_ = bf16[256,256]{1,0:T(8,128)(2,1)S(1)} collective-permute-done((bf16[256,256]{1,0:T(8,128)(2,1)S(1)}, bf16[256,256]{1,0:T(8,128)(2,1)S(1)}, u32[]{:S(2)}, u32[]{:S(2)}) %collective-permute-start.16) | collective-permute-done | bytes 131104 | tf_op jit(solution)/shard_map/ppermute | solution.py:24
  80.8 2.3 %collective-permute-done.17.refs_3_ = bf16[256,256]{1,0:T(8,128)(2,1)S(1)} collective-permute-done((bf16[256,256]{1,0:T(8,128)(2,1)S(1)}, bf16[256,256]{1,0:T(8,128)(2,1)S(1)}, u32[]{:S(2)}, u32[]{:S(2)}) %collective-permute-start.17) | collective-permute-done | bytes 131104 | tf_op jit(solution)/shard_map/ppermute | solution.py:24
  83.1 0.6 copy-done.6
  83.7 2.6 %finish.1 = (f32[2,256,256]{2,1,0:T(8,128)}, bf16[256,256]{1,0:T(8,128)(2,1)}, f32[256,256]{1,0:T(8,128)}) custom-call(bf16[256,256]{1,0:T(8,128)(2,1)} %copy-done.3, bf16[256,256]{1,0:T(8,128)(2,1)} %copy-done.4, bf16[256,256]{1,0:T(8,128)(2,1)} %copy-done.5, bf16[256,256]{1,0:T(8,128)(2,1)} %copy-done.6, f32[2,256,256]{2,1,0:T(8,128)} %bitcast.42, ...), custom_call_target="tpu_custom_call" | custom-call | tf_op jit(solution)/shard_map/finish/pallas_call | solution.py:193
  86.4 0.7 fusion.1
  87.0 0.1 maximum_multiply_fusion
  87.1 1.0 %copy.16 = bf16[1,1,256,2,1,256]{5,3,4,2,1,0:T(2,128)(2,1)} copy(bf16[1,1,256,2,1,256]{5,2,4,3,1,0:T(8,128)(2,1)S(1)} %maximum_multiply_fusion) | data formatting | bytes 524288
  (37 shorter events, 0.6 us)
Async XLA Ops:
  1.3 0.7 copy-start.7
  3.7 0.9 %copy-start.1 = (bf16[1,1,256,1,1,256]{5,2,4,3,1,0:T(8,128)(2,1)S(1)}, bf16[1,1,256,1,1,256]{5,2,4,3,1,0:T(8,128)(2,1)}, u32[]{:S(2)}) copy-start(bf16[1,1,256,1,1,256]{5,2,4,3,1,0:T(8,128)(2,1)} %param.11) | copy-start | bytes 393220
  4.6 4.7 %copy-start = (bf16[1,1,256,2,1,256]{5,3,4,2,1,0:T(2,128)(2,1)S(1)}, bf16[1,1,256,2,1,256]{5,3,4,2,1,0:T(2,128)(2,1)}, u32[]{:S(2)}) copy-start(bf16[1,1,256,2,1,256]{5,3,4,2,1,0:T(2,128)(2,1)} %param.9) | copy-start | bytes 786436
  4.6 6.0 %copy-start.2 = (bf16[1,1,256,256]{3,2,1,0:T(8,128)(2,1)S(1)}, bf16[1,1,256,256]{3,2,1,0:T(8,128)(2,1)}, u32[]{:S(2)}) copy-start(bf16[1,1,256,256]{3,2,1,0:T(8,128)(2,1)} %param.12) | copy-start | bytes 393220
  4.6 20.1 %collective-permute-start.3 = (bf16[256,768]{1,0:T(8,128)(2,1)S(1)}, bf16[256,768]{1,0:T(8,128)(2,1)S(1)}, u32[]{:S(2)}, u32[]{:S(2)}) collective-permute-start(bf16[256,768]{1,0:T(8,128)(2,1)S(1)} %pad_maximum_fusion), channel_id=1, source_target_pairs={{0,0},{4,1},{2,2},{6,3},{1,4},{5,5},{3,6},{7,7},{8,8},{12,9},{10,1... | collective-permute-start | bytes 1179656 | tf_op jit(solution)/shard_map/ppermute | solution.py:24
  9.4 11.9 %collective-permute-start = (bf16[2,256,256]{2,1,0:T(8,128)(2,1)S(1)}, bf16[2,256,256]{2,1,0:T(8,128)(2,1)S(1)}, u32[]{:S(2)}, u32[]{:S(2)}) collective-permute-start(bf16[2,256,256]{2,1,0:T(8,128)(2,1)S(1)} %bitcast.38), channel_id=1, source_target_pairs={{2,0},{3,1},{0,2},{1,3},{6,4},{7,5},{4,6},{5,7},{10,8},{11,9},{8,1... | collective-permute-start | bytes 786440 | tf_op jit(solution)/shard_map/ppermute | solution.py:24
  10.6 9.0 %collective-permute-start.8 = (bf16[256,256]{1,0:T(8,128)(2,1)S(1)}, bf16[256,256]{1,0:T(8,128)(2,1)S(1)}, u32[]{:S(2)}, u32[]{:S(2)}) collective-permute-start(bf16[256,256]{1,0:T(8,128)(2,1)S(1)} %bitcast.45), channel_id=1, source_target_pairs={{0,0},{4,1},{2,2},{6,3},{1,4},{5,5},{3,6},{7,7},{8,8},{12,9},{10,1... | collective-permute-start | bytes 393224 | tf_op jit(solution)/shard_map/ppermute | solution.py:24
  12.8 11.9 %collective-permute-start.1 = (bf16[2,256,256]{2,1,0:T(8,128)(2,1)S(1)}, bf16[2,256,256]{2,1,0:T(8,128)(2,1)S(1)}, u32[]{:S(2)}, u32[]{:S(2)}) collective-permute-start(bf16[2,256,256]{2,1,0:T(8,128)(2,1)S(1)} %bitcast.39), channel_id=1, source_target_pairs={{4,0},{5,1},{6,2},{7,3},{0,4},{1,5},{2,6},{3,7},{12,8},{13,9},{14,... | collective-permute-start | bytes 786440 | tf_op jit(solution)/shard_map/ppermute | solution.py:24
  12.9 22.1 %collective-permute-start.4 = (bf16[256,768]{1,0:T(8,128)(2,1)S(1)}, bf16[256,768]{1,0:T(8,128)(2,1)S(1)}, u32[]{:S(2)}, u32[]{:S(2)}) collective-permute-start(bf16[256,768]{1,0:T(8,128)(2,1)S(1)} %pad_maximum_fusion), channel_id=1, source_target_pairs={{8,0},{12,1},{10,2},{14,3},{9,4},{13,5},{11,6},{15,7},{0,8},{4,9},... | collective-permute-start | bytes 1179656 | tf_op jit(solution)/shard_map/ppermute | solution.py:24
  19.6 28.6 %collective-permute-start.5 = (bf16[256,768]{1,0:T(8,128)(2,1)S(1)}, bf16[256,768]{1,0:T(8,128)(2,1)S(1)}, u32[]{:S(2)}, u32[]{:S(2)}) collective-permute-start(bf16[256,768]{1,0:T(8,128)(2,1)S(1)} %pad_maximum_fusion), channel_id=1, source_target_pairs={{16,0},{20,1},{18,2},{22,3},{17,4},{21,5},{19,6},{23,7},{24,8},{28... | collective-permute-start | bytes 1179656 | tf_op jit(solution)/shard_map/ppermute | solution.py:24
  21.2 27.0 %collective-permute-start.6 = (bf16[256,768]{1,0:T(8,128)(2,1)S(1)}, bf16[256,768]{1,0:T(8,128)(2,1)S(1)}, u32[]{:S(2)}, u32[]{:S(2)}) collective-permute-start(bf16[256,768]{1,0:T(8,128)(2,1)S(1)} %pad_maximum_fusion), channel_id=1, source_target_pairs={{24,0},{28,1},{26,2},{30,3},{25,4},{29,5},{27,6},{31,7},{16,8},{20... | collective-permute-start | bytes 1179656 | tf_op jit(solution)/shard_map/ppermute | solution.py:24
  24.7 23.5 %collective-permute-start.7 = (bf16[256,768]{1,0:T(8,128)(2,1)S(1)}, bf16[256,768]{1,0:T(8,128)(2,1)S(1)}, u32[]{:S(2)}, u32[]{:S(2)}) collective-permute-start(bf16[256,768]{1,0:T(8,128)(2,1)S(1)} %collective-permute-done.3.refs_4_), channel_id=1, source_target_pairs={{1,0},{0,1},{3,2},{2,3},{5,4},{4,5},{7,6},{6,7},{9,8},{8,9},{11,10... | collective-permute-start | bytes 1179656 | tf_op jit(solution)/shard_map/ppermute | solution.py:24
  24.7 10.3 %collective-permute-start.2 = (bf16[2,256,256]{2,1,0:T(8,128)(2,1)S(1)}, bf16[2,256,256]{2,1,0:T(8,128)(2,1)S(1)}, u32[]{:S(2)}, u32[]{:S(2)}) collective-permute-start(bf16[2,256,256]{2,1,0:T(8,128)(2,1)S(1)} %bitcast.40), channel_id=1, source_target_pairs={{6,0},{7,1},{4,2},{5,3},{2,4},{3,5},{0,6},{1,7},{14,8},{15,9},{12,... | collective-permute-start | bytes 786440 | tf_op jit(solution)/shard_map/ppermute | solution.py:24
  49.8 1.6 %collective-permute-start.11 = (bf16[512,256]{1,0:T(8,128)(2,1)S(1)}, bf16[512,256]{1,0:T(8,128)(2,1)S(1)}, u32[]{:S(2)}, u32[]{:S(2)}) collective-permute-start(bf16[512,256]{1,0:T(8,128)(2,1)S(1)} %get-tuple-element.15), channel_id=1, source_target_pairs={{1,0},{0,1},{3,2},{2,3},{5,4},{4,5},{7,6},{6,7},{9,8},{8,9},{11,10... | collective-permute-start | bytes 786440 | tf_op jit(solution)/shard_map/ppermute | solution.py:24
  49.9 12.2 %collective-permute-start.9 = (f32[256,768]{1,0:T(8,128)S(1)}, f32[256,768]{1,0:T(8,128)S(1)}, u32[]{:S(2)}, u32[]{:S(2)}) collective-permute-start(f32[256,768]{1,0:T(8,128)S(1)} %get-tuple-element.13), channel_id=1, source_target_pairs={{1,0},{0,1},{3,2},{2,3},{5,4},{4,5},{7,6},{6,7},{9,8},{8,9},{11,10... | collective-permute-start | bytes 2359304 | tf_op jit(solution)/shard_map/ppermute | solution.py:24
  51.5 9.1 %collective-permute-start.12 = (bf16[256,256]{1,0:T(8,128)(2,1)S(1)}, bf16[256,256]{1,0:T(8,128)(2,1)S(1)}, u32[]{:S(2)}, u32[]{:S(2)}) collective-permute-start(bf16[256,256]{1,0:T(8,128)(2,1)S(1)} %slice.51), channel_id=1, source_target_pairs={{8,0},{9,1},{10,2},{11,3},{12,4},{13,5},{14,6},{15,7},{0,8},{1,9},... | collective-permute-start | bytes 393224 | tf_op jit(solution)/shard_map/ppermute | solution.py:24
  60.6 8.2 %collective-permute-start.13 = (bf16[256,256]{1,0:T(8,128)(2,1)S(1)}, bf16[256,256]{1,0:T(8,128)(2,1)S(1)}, u32[]{:S(2)}, u32[]{:S(2)}) collective-permute-start(bf16[256,256]{1,0:T(8,128)(2,1)S(1)} %fusion), channel_id=1, source_target_pairs={{16,0},{17,1},{18,2},{19,3},{20,4},{21,5},{22,6},{23,7},{24,8},{25... | collective-permute-start | bytes 393224 | tf_op jit(solution)/shard_map/ppermute | solution.py:24
  62.2 24.1 %collective-permute-start.10 = (bf16[256,768]{1,0:T(8,128)(2,1)S(1)}, bf16[256,768]{1,0:T(8,128)(2,1)S(1)}, u32[]{:S(2)}, u32[]{:S(2)}) collective-permute-start(bf16[256,768]{1,0:T(8,128)(2,1)S(1)} %add_convert_fusion), channel_id=1, source_target_pairs={{0,0},{4,1},{2,2},{6,3},{1,4},{5,5},{3,6},{7,7},{8,8},{12,9},{10,1... | collective-permute-start | bytes 1179656 | tf_op jit(solution)/shard_map/ppermute | solution.py:24
  68.9 9.2 %collective-permute-start.14 = (bf16[256,256]{1,0:T(8,128)(2,1)S(1)}, bf16[256,256]{1,0:T(8,128)(2,1)S(1)}, u32[]{:S(2)}, u32[]{:S(2)}) collective-permute-start(bf16[256,256]{1,0:T(8,128)(2,1)S(1)} %add_convert_fusion.1), channel_id=1, source_target_pairs={{0,0},{4,1},{2,2},{6,3},{1,4},{5,5},{3,6},{7,7},{8,8},{12,9},{10,1... | collective-permute-start | bytes 393224 | tf_op jit(solution)/shard_map/ppermute | solution.py:24
  74.1 4.3 %collective-permute-start.15 = (bf16[256,256]{1,0:T(8,128)(2,1)S(1)}, bf16[256,256]{1,0:T(8,128)(2,1)S(1)}, u32[]{:S(2)}, u32[]{:S(2)}) collective-permute-start(bf16[256,256]{1,0:T(8,128)(2,1)S(1)} %add_convert_fusion.1), channel_id=1, source_target_pairs={{1,0},{5,1},{3,2},{7,3},{0,4},{4,5},{2,6},{6,7},{9,8},{13,9},{11,1... | collective-permute-start | bytes 393224 | tf_op jit(solution)/shard_map/ppermute | solution.py:24
  74.1 6.7 %collective-permute-start.16 = (bf16[256,256]{1,0:T(8,128)(2,1)S(1)}, bf16[256,256]{1,0:T(8,128)(2,1)S(1)}, u32[]{:S(2)}, u32[]{:S(2)}) collective-permute-start(bf16[256,256]{1,0:T(8,128)(2,1)S(1)} %add_convert_fusion.1), channel_id=1, source_target_pairs={{8,0},{12,1},{10,2},{14,3},{9,4},{13,5},{11,6},{15,7},{0,8},{4,9},... | collective-permute-start | bytes 393224 | tf_op jit(solution)/shard_map/ppermute | solution.py:24
  74.2 8.8 %collective-permute-start.17 = (bf16[256,256]{1,0:T(8,128)(2,1)S(1)}, bf16[256,256]{1,0:T(8,128)(2,1)S(1)}, u32[]{:S(2)}, u32[]{:S(2)}) collective-permute-start(bf16[256,256]{1,0:T(8,128)(2,1)S(1)} %add_convert_fusion.1), channel_id=1, source_target_pairs={{9,0},{13,1},{11,2},{15,3},{8,4},{12,5},{10,6},{14,7},{1,8},{5,9},... | collective-permute-start | bytes 393224 | tf_op jit(solution)/shard_map/ppermute | solution.py:24
  78.1 5.0 %copy-start.3 = (bf16[256,256]{1,0:T(8,128)(2,1)}, bf16[256,256]{1,0:T(8,128)(2,1)S(1)}, u32[]{:S(2)}) copy-start(bf16[256,256]{1,0:T(8,128)(2,1)S(1)} %collective-permute-done.14.refs_0_) | copy-start | bytes 393220
  78.5 4.6 %copy-start.4 = (bf16[256,256]{1,0:T(8,128)(2,1)}, bf16[256,256]{1,0:T(8,128)(2,1)S(1)}, u32[]{:S(2)}) copy-start(bf16[256,256]{1,0:T(8,128)(2,1)S(1)} %collective-permute-done.15.refs_1_) | copy-start | bytes 393220
  80.8 2.3 %copy-start.5 = (bf16[256,256]{1,0:T(8,128)(2,1)}, bf16[256,256]{1,0:T(8,128)(2,1)S(1)}, u32[]{:S(2)}) copy-start(bf16[256,256]{1,0:T(8,128)(2,1)S(1)} %collective-permute-done.16.refs_2_) | copy-start | bytes 393220
  83.1 0.6 copy-start.6

commit v3 on v2

--- a/solution.py
+++ b/solution.py
@@ -36,31 +36,33 @@
 
 
 def product_kernel(high, wide, *refs):
-    a_refs = refs[: 2 * wide]
-    x_refs = refs[2 * wide : 2 * wide + high]
-    other_ref, couple_ref = refs[2 * wide + high : 2 * wide + high + 2]
-    keep_y, send_y, keep_g, send_g, a_all, x_all, x_row, y_all, g_all = refs[2 * wide + high + 2 :]
+    near_refs, far_ref = refs[:wide], refs[wide]
+    refs = refs[wide + 1 :]
+    x_refs, other_ref = refs[:high], refs[high]
+    keep_y, send_y, keep_g, send_g, a_all, x_all, x_row, y_all, g_all = refs[high + 1 :]
     block = other_ref.shape[0]
     z, y, x, k = place()
     low = z % 2
     turn = z ^ x
     swap = y ^ k
+    width = 3 * block
+    couple = x_refs[0][:, width:]
     for step in range(high):
-        x_all[pl.ds(pl.multiple_of((turn ^ step) * block, block), block), :] = x_refs[step][...]
+        x_all[pl.ds(pl.multiple_of((turn ^ step) * block, block), block), :] = x_refs[step][:, :width]
     for dy in range(2):
         for dx in range(wide):
             for kk in range(2):
                 t = kk * wide + dx
-                a_all[dy * block : (dy + 1) * block, t * block : (t + 1) * block] = a_refs[
-                    dy * wide + dx
-                ][kk]
-    x_row[pl.ds(pl.multiple_of(swap * block, block), block), :] = x_refs[0][...]
-    x_row[pl.ds(pl.multiple_of((1 - swap) * block, block), block), :] = other_ref[...]
+                a_all[dy * block : (dy + 1) * block, t * block : (t + 1) * block] = (
+                    far_ref[dx, kk] if dy else near_refs[dx][kk]
+                )
+    x_row[pl.ds(pl.multiple_of(swap * block, block), block), :] = x_refs[0][:, :width]
+    x_row[pl.ds(pl.multiple_of((1 - swap) * block, block), block), :] = other_ref[:, :width]
     total = jnp.dot(a_all[...], x_all[...], preferred_element_type=jnp.float32)
     near = total[:, :block].astype(jnp.bfloat16)
     far = total[:, block : 2 * block]
     last = total[:, 2 * block :] - jnp.dot(
-        near, couple_ref[...], preferred_element_type=jnp.float32
+        near, couple, preferred_element_type=jnp.float32
     )
     y_all[:, : 2 * block] = total[:, : 2 * block]
     y_all[:, 2 * block :] = last
@@ -117,32 +119,34 @@
     keep_two = pattern_two.reshape(1)
     flip = near[0] == 1
     one = factor_one.reshape(block, 2, block)
-    two = factor_two.reshape(block, block)
-    masked = one * keep_one.astype(jnp.bfloat16)[None, :, None]
-    zero, unit = masked[:, 0], masked[:, 1]
-    cols = jnp.concatenate(
-        [
-            jnp.where(flip, unit, zero),
-            jnp.where(flip, zero, unit),
-            two * keep_two.astype(jnp.bfloat16)[0],
-        ],
-        axis=1,
-    )
+    zero = one[:, 0] * keep_one[0].astype(jnp.bfloat16)
+    unit = one[:, 1] * keep_one[1].astype(jnp.bfloat16)
+    pair = jnp.concatenate([jnp.where(flip, unit, zero), jnp.where(flip, zero, unit)], axis=1)
+    last = factor_two.reshape(block, block) * keep_two[0].astype(jnp.bfloat16)
+    cols = jnp.concatenate([pair, last], axis=1)
     coupling = parent_block.reshape(block, block)
     anc = anc_inverse.reshape(block, 2, block).transpose(1, 0, 2)
 
-    pieces = [
-        send(cols, sizes, lambda z, y, x, k, d=d: (z ^ d, k, x, y)) for d in range(high)
-    ]
-    couple = send(coupling, sizes, lambda z, y, x, k: (z, k, x, y))
-    other = send(pieces[0], sizes, lambda z, y, x, k: (z, y, x, 1 - k))
-    ancs = [
-        anc
-        if dy == 0 and dx == 0
-        else send(anc, sizes, lambda z, y, x, k, dy=dy, dx=dx: (z, y ^ dy, x ^ dx, k))
-        for dy in range(2)
-        for dx in range(wide)
-    ]
+    def plane(value, dy, dx):
+        return send(value, sizes, lambda z, y, x, k: (z, y ^ dy, x ^ dx, k))
+
+    def across(value, d):
+        return send(value, sizes, lambda z, y, x, k: (z ^ d, k, x, y))
+
+    def beside(value):
+        return send(value, sizes, lambda z, y, x, k: (z ^ 1, y, x, k))
+
+    pieces = {d: across(cols, d) for d in [*range(2, high, 2), 1]}
+    own = across(jnp.concatenate([cols, coupling], axis=1), 0)
+    now = anc
+    near_anc = [anc] + [plane(now, 0, dx) for dx in range(1, wide)]
+    stacked = jnp.stack(near_anc)
+    far_anc = plane(stacked, 1, 0)
+    for d in range(3, high, 2):
+        pieces[d] = beside(pieces[d - 1])
+    pieces[1], own_now = lax.optimization_barrier((pieces[1], own))
+    other = send(own_now, sizes, lambda z, y, x, k: (z, y, x, 1 - k))
+    pieces = [own] + [pieces[d] for d in range(1, high)]
     width = 3 * block
     keep_y, send_y, keep_g, send_g = pl.pallas_call(
         functools.partial(product_kernel, high, wide),
@@ -161,7 +165,7 @@
         ],
         compiler_params=pltpu.CompilerParams(vmem_limit_bytes=48 * 1024 * 1024),
         name="products",
-    )(*ancs, *pieces, other, couple)
+    )(*near_anc, far_anc, *pieces, other)
 
     def core_swap(value):
         return send(value, sizes, lambda z, y, x, k: (z, y, x, 1 - k))

time: 88.4 us -> 75.3 us (0.85)
  starting transfers between devices: 39.2 us -> 22.9 us
  waiting for transfers between devices: 37.2 us -> 39.3 us
    ppermute x18 -> x16, starting transfers between devices: 39.2 us -> 22.9 us  [send(): return lax.ppermute(value, AXES, pairs)]
    ppermute x18 -> x16, waiting for transfers between devices: 37.2 us -> 39.3 us  [send(): return lax.ppermute(value, AXES, pairs)]
    select_n x1, other arithmetic: 0.02 us -> 1.35 us  [body(): jnp.where(flip, unit, zero)]
    mul x2 -> x1, other arithmetic: 1.05 us -> 0.01 us  [body(): last = factor_two.reshape(block, block) * keep_two[0].astype(jnp.bfloat16)]
    unnamed x18 -> x19, local copies, waits for them, and re-layouts: 3.17 us -> 3.33 us
  transfers between devices with their start and end apart: 18 -> 16, of which waited for: 10 -> 12; matrix products, arithmetic and copies ran while one was open for 0% -> 0% of each run, Pallas kernels for 3% -> 4%
where the time goes in v3:
time: 75.3 us; the launch traced here: 75 us
  waiting for transfers between devices  39.3 us (52%)
  starting transfers between devices  22.9 us (30%)
  Pallas kernels  4.23 us (6%)
  local copies, waits for them, and re-layouts  3.93 us (5%)
  other arithmetic  2.49 us (3%)
  between operations  2.14 us (3%)
    ppermute x16, waiting for transfers between devices, send(): return lax.ppermute(value, AXES, pairs)  39.3 us
    ppermute x16, starting transfers between devices, send(): return lax.ppermute(value, AXES, pairs)  22.9 us
    unnamed x19, local copies, waits for them, and re-layouts  3.33 us
    pallas_call x1, Pallas kernels, body(): pl.pallas_call(finish_kernel, out_shape=(jax.ShapeDtypeStruct((2, block,...  2.65 us
    pallas_call x1, Pallas kernels, body(): pl.pallas_call(functools.partial(product_kernel, high, wide), out_shape=(...  1.58 us
  transfers between devices with their start and end apart: 16, of which 12 were waited for; matrix products, arithmetic and copies ran while one was open for 0% of the time, Pallas kernels for 4%

profile of v3, /device:TPU:1, one launch (start us, length us, event | category | flops | bytes accessed | tf_op | source)
XLA Modules:
  0.0 75.0 jit_solution(4679244285414480788)
XLA Ops:
  1.3 0.6 copy-done.7
  2.0 0.6 fusion.2
  2.5 1.0 %copy.21 = bf16[1,1,256,2,1,256]{5,2,3,4,1,0:T(8,128)(2,1)S(1)} copy(bf16[1,1,256,2,1,256]{5,3,4,2,1,0:T(2,128)(2,1)} %param.10) | data formatting | bytes 524288 | tf_op args[1]
  4.3 1.4 %select_bitcast_fusion.3 = (bf16[256,256]{1,0:T(8,128)(2,1)S(1)}, bf16[256,256]{1,0:T(8,128)(2,1)S(1)}) fusion(pred[]{:T(512)} %bitcast.1, bf16[256,2,256]{2,0,1:T(8,128)(2,1)S(1)} %bitcast.48, bf16[]{:T(256)} %bitcast.9, bf16[]{:T(256)} %bitcast.8), kind=kLoop, calls=%fused_computation.21 | loop fusion | flops 262144 | bytes 524293 | tf_op jit(solution)/shard_map/jit(_where)/select_n | solution.py:124
  5.7 4.7 %collective-permute-start.2 = (bf16[256,1024]{1,0:T(8,128)(2,1)S(1)}, bf16[256,1024]{1,0:T(8,128)(2,1)S(1)}, u32[]{:S(2)}, u32[]{:S(2)}) collective-permute-start(bf16[256,1024]{1,0:T(8,128)(2,1)S(1)} %pad_maximum_fusion.1), channel_id=1, source_target_pairs={{0,0},{4,1},{2,2},{6,3},{1,4},{5,5},{3,6},{7,7},{8,8},{12,9},{10,1... | collective-permute-start | bytes 1572872 | tf_op jit(solution)/shard_map/ppermute | solution.py:24
  10.4 1.1 %collective-permute-start.3 = (bf16[256,768]{1,0:T(8,128)(2,1)S(1)}, bf16[256,768]{1,0:T(8,128)(2,1)S(1)}, u32[]{:S(2)}, u32[]{:S(2)}) collective-permute-start(bf16[256,768]{1,0:T(8,128)(2,1)S(1)} %pad_maximum_fusion.2), channel_id=1, source_target_pairs={{8,0},{12,1},{10,2},{14,3},{9,4},{13,5},{11,6},{15,7},{0,8},{4,9},... | collective-permute-start | bytes 1179656 | tf_op jit(solution)/shard_map/ppermute | solution.py:24
  11.6 1.3 %collective-permute-start = (bf16[2,256,256]{2,1,0:T(8,128)(2,1)S(1)}, bf16[2,256,256]{2,1,0:T(8,128)(2,1)S(1)}, u32[]{:S(2)}, u32[]{:S(2)}) collective-permute-start(bf16[2,256,256]{2,1,0:T(8,128)(2,1)S(1)} %bitcast.44), channel_id=1, source_target_pairs={{2,0},{3,1},{0,2},{1,3},{6,4},{7,5},{4,6},{5,7},{10,8},{11,9},{8,1... | collective-permute-start | bytes 786440 | tf_op jit(solution)/shard_map/ppermute | solution.py:24
  12.8 4.0 %collective-permute-start.4 = (bf16[256,768]{1,0:T(8,128)(2,1)S(1)}, bf16[256,768]{1,0:T(8,128)(2,1)S(1)}, u32[]{:S(2)}, u32[]{:S(2)}) collective-permute-start(bf16[256,768]{1,0:T(8,128)(2,1)S(1)} %pad_maximum_fusion.2), channel_id=1, source_target_pairs={{16,0},{20,1},{18,2},{22,3},{17,4},{21,5},{19,6},{23,7},{24,8},{28... | collective-permute-start | bytes 1179656 | tf_op jit(solution)/shard_map/ppermute | solution.py:24
  16.9 1.7 %collective-permute-done.refs_1_ = bf16[2,256,256]{2,1,0:T(8,128)(2,1)S(1)} collective-permute-done((bf16[2,256,256]{2,1,0:T(8,128)(2,1)S(1)}, bf16[2,256,256]{2,1,0:T(8,128)(2,1)S(1)}, u32[]{:S(2)}, u32[]{:S(2)}) %collective-permute-start) | collective-permute-done | bytes 262176 | tf_op jit(solution)/shard_map/ppermute | solution.py:24
  18.7 7.6 %collective-permute-done.3.refs_4_ = bf16[256,768]{1,0:T(8,128)(2,1)S(1)} collective-permute-done((bf16[256,768]{1,0:T(8,128)(2,1)S(1)}, bf16[256,768]{1,0:T(8,128)(2,1)S(1)}, u32[]{:S(2)}, u32[]{:S(2)}) %collective-permute-start.3) | collective-permute-done | bytes 393248 | tf_op jit(solution)/shard_map/ppermute | solution.py:24
  26.4 5.0 %collective-permute-done.4.refs_5_ = bf16[256,768]{1,0:T(8,128)(2,1)S(1)} collective-permute-done((bf16[256,768]{1,0:T(8,128)(2,1)S(1)}, bf16[256,768]{1,0:T(8,128)(2,1)S(1)}, u32[]{:S(2)}, u32[]{:S(2)}) %collective-permute-start.4) | collective-permute-done | bytes 393248 | tf_op jit(solution)/shard_map/ppermute | solution.py:24
  31.4 0.3 collective-permute-start.5
  31.7 7.6 %collective-permute-done.1.refs_2_ = bf16[2,2,256,256]{3,2,1,0:T(8,128)(2,1)S(1)} collective-permute-done((bf16[2,2,256,256]{3,2,1,0:T(8,128)(2,1)S(1)}, bf16[2,2,256,256]{3,2,1,0:T(8,128)(2,1)S(1)}, u32[]{:S(2)}, u32[]{:S(2)}) %collective-permute-start.1) | collective-permute-done | bytes 524320 | tf_op jit(solution)/shard_map/ppermute | solution.py:24
  39.2 1.2 %collective-permute-done.5.refs_6_ = bf16[256,768]{1,0:T(8,128)(2,1)S(1)} collective-permute-done((bf16[256,768]{1,0:T(8,128)(2,1)S(1)}, bf16[256,768]{1,0:T(8,128)(2,1)S(1)}, u32[]{:S(2)}, u32[]{:S(2)}) %collective-permute-start.5) | collective-permute-done | bytes 393248 | tf_op jit(solution)/shard_map/ppermute | solution.py:24
  40.4 1.6 %products.1 = (f32[256,768]{1,0:T(8,128)S(1)}, f32[256,768]{1,0:T(8,128)S(1)}, f32[512,256]{1,0:T(8,128)S(1)}, bf16[512,256]{1,0:T(8,128)(2,1)S(1)}) custom-call(bf16[2,256,256]{2,1,0:T(8,128)(2,1)S(1)} %bitcast.46, bf16[2,256,256]{2,1,0:T(8,128)(2,1)S(1)} %collective-permute-done.refs_1_, bf16[2,2,256,256]{3,2,1,0:T(8,128)(2,1)S(1)} %collective-permute-done.1.refs_2_, ...), custom_call_target="tpu_custom_call" | custom-call | tf_op jit(solution)/shard_map/products/pallas_call | solution.py:151
  42.1 0.5 collective-permute-start.7
  42.6 1.0 %collective-permute-done.9 = bf16[512,256]{1,0:T(8,128)(2,1)S(1)} collective-permute-done((bf16[512,256]{1,0:T(8,128)(2,1)S(1)}, bf16[512,256]{1,0:T(8,128)(2,1)S(1)}, u32[]{:S(2)}, u32[]{:S(2)}) %collective-permute-start.9) | collective-permute-done | bytes 262176 | tf_op jit(solution)/shard_map/ppermute | solution.py:24
  43.8 4.9 %collective-permute-done.10 = bf16[256,256]{1,0:T(8,128)(2,1)S(1)} collective-permute-done((bf16[256,256]{1,0:T(8,128)(2,1)S(1)}, bf16[256,256]{1,0:T(8,128)(2,1)S(1)}, u32[]{:S(2)}, u32[]{:S(2)}) %collective-permute-start.10) | collective-permute-done | bytes 131104 | tf_op jit(solution)/shard_map/ppermute | solution.py:24
  48.8 2.1 %collective-permute-start.11 = (bf16[256,256]{1,0:T(8,128)(2,1)S(1)}, bf16[256,256]{1,0:T(8,128)(2,1)S(1)}, u32[]{:S(2)}, u32[]{:S(2)}) collective-permute-start(bf16[256,256]{1,0:T(8,128)(2,1)S(1)} %fusion), channel_id=1, source_target_pairs={{16,0},{17,1},{18,2},{19,3},{20,4},{21,5},{22,6},{23,7},{24,8},{25... | collective-permute-start | bytes 393224 | tf_op jit(solution)/shard_map/ppermute | solution.py:24
  50.9 3.0 %collective-permute-start.8 = (bf16[256,768]{1,0:T(8,128)(2,1)S(1)}, bf16[256,768]{1,0:T(8,128)(2,1)S(1)}, u32[]{:S(2)}, u32[]{:S(2)}) collective-permute-start(bf16[256,768]{1,0:T(8,128)(2,1)S(1)} %add_convert_fusion), channel_id=1, source_target_pairs={{0,0},{4,1},{2,2},{6,3},{1,4},{5,5},{3,6},{7,7},{8,8},{12,9},{10,1... | collective-permute-start | bytes 1179656 | tf_op jit(solution)/shard_map/ppermute | solution.py:24
  53.9 3.4 %collective-permute-done.11 = bf16[256,256]{1,0:T(8,128)(2,1)S(1)} collective-permute-done((bf16[256,256]{1,0:T(8,128)(2,1)S(1)}, bf16[256,256]{1,0:T(8,128)(2,1)S(1)}, u32[]{:S(2)}, u32[]{:S(2)}) %collective-permute-start.11) | collective-permute-done | bytes 131104 | tf_op jit(solution)/shard_map/ppermute | solution.py:24
  57.3 3.7 %collective-permute-start.12 = (bf16[256,256]{1,0:T(8,128)(2,1)S(1)}, bf16[256,256]{1,0:T(8,128)(2,1)S(1)}, u32[]{:S(2)}, u32[]{:S(2)}) collective-permute-start(bf16[256,256]{1,0:T(8,128)(2,1)S(1)} %add_convert_fusion.1), channel_id=1, source_target_pairs={{0,0},{4,1},{2,2},{6,3},{1,4},{5,5},{3,6},{7,7},{8,8},{12,9},{10,1... | collective-permute-start | bytes 393224 | tf_op jit(solution)/shard_map/ppermute | solution.py:24
  61.1 0.5 collective-permute-start.14
  61.6 1.5 %collective-permute-start.15 = (bf16[256,256]{1,0:T(8,128)(2,1)S(1)}, bf16[256,256]{1,0:T(8,128)(2,1)S(1)}, u32[]{:S(2)}, u32[]{:S(2)}) collective-permute-start(bf16[256,256]{1,0:T(8,128)(2,1)S(1)} %add_convert_fusion.1), channel_id=1, source_target_pairs={{9,0},{13,1},{11,2},{15,3},{8,4},{12,5},{10,6},{14,7},{1,8},{5,9},... | collective-permute-start | bytes 393224 | tf_op jit(solution)/shard_map/ppermute | solution.py:24
  63.1 1.9 %collective-permute-done.12.refs_0_ = bf16[256,256]{1,0:T(8,128)(2,1)S(1)} collective-permute-done((bf16[256,256]{1,0:T(8,128)(2,1)S(1)}, bf16[256,256]{1,0:T(8,128)(2,1)S(1)}, u32[]{:S(2)}, u32[]{:S(2)}) %collective-permute-start.12) | collective-permute-done | bytes 131104 | tf_op jit(solution)/shard_map/ppermute | solution.py:24
  65.0 0.4 collective-permute-done.13.refs_1_
  65.4 2.3 %collective-permute-done.14.refs_2_ = bf16[256,256]{1,0:T(8,128)(2,1)S(1)} collective-permute-done((bf16[256,256]{1,0:T(8,128)(2,1)S(1)}, bf16[256,256]{1,0:T(8,128)(2,1)S(1)}, u32[]{:S(2)}, u32[]{:S(2)}) %collective-permute-start.14) | collective-permute-done | bytes 131104 | tf_op jit(solution)/shard_map/ppermute | solution.py:24
  67.7 2.3 %collective-permute-done.15.refs_3_ = bf16[256,256]{1,0:T(8,128)(2,1)S(1)} collective-permute-done((bf16[256,256]{1,0:T(8,128)(2,1)S(1)}, bf16[256,256]{1,0:T(8,128)(2,1)S(1)}, u32[]{:S(2)}, u32[]{:S(2)}) %collective-permute-start.15) | collective-permute-done | bytes 131104 | tf_op jit(solution)/shard_map/ppermute | solution.py:24
  70.0 0.6 copy-done.6
  70.6 2.7 %finish.1 = (f32[2,256,256]{2,1,0:T(8,128)}, bf16[256,256]{1,0:T(8,128)(2,1)}, f32[256,256]{1,0:T(8,128)}) custom-call(bf16[256,256]{1,0:T(8,128)(2,1)} %copy-done.3, bf16[256,256]{1,0:T(8,128)(2,1)} %copy-done.4, bf16[256,256]{1,0:T(8,128)(2,1)} %copy-done.5, bf16[256,256]{1,0:T(8,128)(2,1)} %copy-done.6, f32[2,256,256]{2,1,0:T(8,128)} %bitcast.49, ...), custom_call_target="tpu_custom_call" | custom-call | tf_op jit(solution)/shard_map/finish/pallas_call | solution.py:197
  73.3 0.7 fusion.1
  74.1 1.0 %copy.16 = bf16[1,1,256,2,1,256]{5,3,4,2,1,0:T(2,128)(2,1)} copy(bf16[1,1,256,2,1,256]{5,2,4,3,1,0:T(8,128)(2,1)S(1)} %maximum_multiply_fusion) | data formatting | bytes 524288
  (36 shorter events, 0.8 us)
Async XLA Ops:
  1.3 0.7 copy-start.7
  2.5 1.7 %copy-start.2 = (bf16[1,1,256,1,1,256]{5,2,4,3,1,0:T(8,128)(2,1)S(1)}, bf16[1,1,256,1,1,256]{5,2,4,3,1,0:T(8,128)(2,1)}, u32[]{:S(2)}) copy-start(bf16[1,1,256,1,1,256]{5,2,4,3,1,0:T(8,128)(2,1)} %param.11) | copy-start | bytes 393220
  4.3 1.4 %copy-start = (bf16[1,1,256,256]{3,2,1,0:T(8,128)(2,1)S(1)}, bf16[1,1,256,256]{3,2,1,0:T(8,128)(2,1)}, u32[]{:S(2)}) copy-start(bf16[1,1,256,256]{3,2,1,0:T(8,128)(2,1)} %param.12) | copy-start | bytes 393220
  5.7 5.8 %copy-start.1 = (bf16[1,1,256,2,1,256]{5,3,4,2,1,0:T(2,128)(2,1)S(1)}, bf16[1,1,256,2,1,256]{5,3,4,2,1,0:T(2,128)(2,1)}, u32[]{:S(2)}) copy-start(bf16[1,1,256,2,1,256]{5,3,4,2,1,0:T(2,128)(2,1)} %param.9) | copy-start | bytes 786436
  5.7 20.7 %collective-permute-start.2 = (bf16[256,1024]{1,0:T(8,128)(2,1)S(1)}, bf16[256,1024]{1,0:T(8,128)(2,1)S(1)}, u32[]{:S(2)}, u32[]{:S(2)}) collective-permute-start(bf16[256,1024]{1,0:T(8,128)(2,1)S(1)} %pad_maximum_fusion.1), channel_id=1, source_target_pairs={{0,0},{4,1},{2,2},{6,3},{1,4},{5,5},{3,6},{7,7},{8,8},{12,9},{10,1... | collective-permute-start | bytes 1572872 | tf_op jit(solution)/shard_map/ppermute | solution.py:24
  10.4 16.0 %collective-permute-start.3 = (bf16[256,768]{1,0:T(8,128)(2,1)S(1)}, bf16[256,768]{1,0:T(8,128)(2,1)S(1)}, u32[]{:S(2)}, u32[]{:S(2)}) collective-permute-start(bf16[256,768]{1,0:T(8,128)(2,1)S(1)} %pad_maximum_fusion.2), channel_id=1, source_target_pairs={{8,0},{12,1},{10,2},{14,3},{9,4},{13,5},{11,6},{15,7},{0,8},{4,9},... | collective-permute-start | bytes 1179656 | tf_op jit(solution)/shard_map/ppermute | solution.py:24
  11.6 7.1 %collective-permute-start = (bf16[2,256,256]{2,1,0:T(8,128)(2,1)S(1)}, bf16[2,256,256]{2,1,0:T(8,128)(2,1)S(1)}, u32[]{:S(2)}, u32[]{:S(2)}) collective-permute-start(bf16[2,256,256]{2,1,0:T(8,128)(2,1)S(1)} %bitcast.44), channel_id=1, source_target_pairs={{2,0},{3,1},{0,2},{1,3},{6,4},{7,5},{4,6},{5,7},{10,8},{11,9},{8,1... | collective-permute-start | bytes 786440 | tf_op jit(solution)/shard_map/ppermute | solution.py:24
  12.8 18.6 %collective-permute-start.4 = (bf16[256,768]{1,0:T(8,128)(2,1)S(1)}, bf16[256,768]{1,0:T(8,128)(2,1)S(1)}, u32[]{:S(2)}, u32[]{:S(2)}) collective-permute-start(bf16[256,768]{1,0:T(8,128)(2,1)S(1)} %pad_maximum_fusion.2), channel_id=1, source_target_pairs={{16,0},{20,1},{18,2},{22,3},{17,4},{21,5},{19,6},{23,7},{24,8},{28... | collective-permute-start | bytes 1179656 | tf_op jit(solution)/shard_map/ppermute | solution.py:24
  18.7 20.6 %collective-permute-start.1 = (bf16[2,2,256,256]{3,2,1,0:T(8,128)(2,1)S(1)}, bf16[2,2,256,256]{3,2,1,0:T(8,128)(2,1)S(1)}, u32[]{:S(2)}, u32[]{:S(2)}) collective-permute-start(bf16[2,2,256,256]{3,2,1,0:T(8,128)(2,1)S(1)} %pad_maximum_fusion), channel_id=1, source_target_pairs={{4,0},{5,1},{6,2},{7,3},{0,4},{1,5},{2,6},{3,7},{12,8},{13,9},{14,... | collective-permute-start | bytes 1572872 | tf_op jit(solution)/shard_map/ppermute | solution.py:24
  26.4 14.0 %collective-permute-start.6 = (bf16[256,1024]{1,0:T(8,128)(2,1)S(1)}, bf16[256,1024]{1,0:T(8,128)(2,1)S(1)}, u32[]{:S(2)}, u32[]{:S(2)}) collective-permute-start(bf16[256,1024]{1,0:T(8,128)(2,1)S(1)} %collective-permute-done.2.refs_3_), channel_id=1, source_target_pairs={{1,0},{0,1},{3,2},{2,3},{5,4},{4,5},{7,6},{6,7},{9,8},{8,9},{11,10... | collective-permute-start | bytes 1572872 | tf_op jit(solution)/shard_map/ppermute | solution.py:24
  31.4 9.0 %collective-permute-start.5 = (bf16[256,768]{1,0:T(8,128)(2,1)S(1)}, bf16[256,768]{1,0:T(8,128)(2,1)S(1)}, u32[]{:S(2)}, u32[]{:S(2)}) collective-permute-start(bf16[256,768]{1,0:T(8,128)(2,1)S(1)} %collective-permute-done.4.refs_5_), channel_id=1, source_target_pairs={{8,0},{9,1},{10,2},{11,3},{12,4},{13,5},{14,6},{15,7},{0,8},{1,9},... | collective-permute-start | bytes 1179656 | tf_op jit(solution)/shard_map/ppermute | solution.py:24
  42.0 1.6 %collective-permute-start.9 = (bf16[512,256]{1,0:T(8,128)(2,1)S(1)}, bf16[512,256]{1,0:T(8,128)(2,1)S(1)}, u32[]{:S(2)}, u32[]{:S(2)}) collective-permute-start(bf16[512,256]{1,0:T(8,128)(2,1)S(1)} %get-tuple-element.19), channel_id=1, source_target_pairs={{1,0},{0,1},{3,2},{2,3},{5,4},{4,5},{7,6},{6,7},{9,8},{8,9},{11,10... | collective-permute-start | bytes 786440 | tf_op jit(solution)/shard_map/ppermute | solution.py:24
  42.1 8.7 %collective-permute-start.7 = (f32[256,768]{1,0:T(8,128)S(1)}, f32[256,768]{1,0:T(8,128)S(1)}, u32[]{:S(2)}, u32[]{:S(2)}) collective-permute-start(f32[256,768]{1,0:T(8,128)S(1)} %get-tuple-element.17), channel_id=1, source_target_pairs={{1,0},{0,1},{3,2},{2,3},{5,4},{4,5},{7,6},{6,7},{9,8},{8,9},{11,10... | collective-permute-start | bytes 2359304 | tf_op jit(solution)/shard_map/ppermute | solution.py:24
  43.7 5.0 %collective-permute-start.10 = (bf16[256,256]{1,0:T(8,128)(2,1)S(1)}, bf16[256,256]{1,0:T(8,128)(2,1)S(1)}, u32[]{:S(2)}, u32[]{:S(2)}) collective-permute-start(bf16[256,256]{1,0:T(8,128)(2,1)S(1)} %slice.69), channel_id=1, source_target_pairs={{8,0},{9,1},{10,2},{11,3},{12,4},{13,5},{14,6},{15,7},{0,8},{1,9},... | collective-permute-start | bytes 393224 | tf_op jit(solution)/shard_map/ppermute | solution.py:24
  48.8 8.5 %collective-permute-start.11 = (bf16[256,256]{1,0:T(8,128)(2,1)S(1)}, bf16[256,256]{1,0:T(8,128)(2,1)S(1)}, u32[]{:S(2)}, u32[]{:S(2)}) collective-permute-start(bf16[256,256]{1,0:T(8,128)(2,1)S(1)} %fusion), channel_id=1, source_target_pairs={{16,0},{17,1},{18,2},{19,3},{20,4},{21,5},{22,6},{23,7},{24,8},{25... | collective-permute-start | bytes 393224 | tf_op jit(solution)/shard_map/ppermute | solution.py:24
  50.9 22.4 %collective-permute-start.8 = (bf16[256,768]{1,0:T(8,128)(2,1)S(1)}, bf16[256,768]{1,0:T(8,128)(2,1)S(1)}, u32[]{:S(2)}, u32[]{:S(2)}) collective-permute-start(bf16[256,768]{1,0:T(8,128)(2,1)S(1)} %add_convert_fusion), channel_id=1, source_target_pairs={{0,0},{4,1},{2,2},{6,3},{1,4},{5,5},{3,6},{7,7},{8,8},{12,9},{10,1... | collective-permute-start | bytes 1179656 | tf_op jit(solution)/shard_map/ppermute | solution.py:24
  57.3 7.7 %collective-permute-start.12 = (bf16[256,256]{1,0:T(8,128)(2,1)S(1)}, bf16[256,256]{1,0:T(8,128)(2,1)S(1)}, u32[]{:S(2)}, u32[]{:S(2)}) collective-permute-start(bf16[256,256]{1,0:T(8,128)(2,1)S(1)} %add_convert_fusion.1), channel_id=1, source_target_pairs={{0,0},{4,1},{2,2},{6,3},{1,4},{5,5},{3,6},{7,7},{8,8},{12,9},{10,1... | collective-permute-start | bytes 393224 | tf_op jit(solution)/shard_map/ppermute | solution.py:24
  61.0 4.3 %collective-permute-start.13 = (bf16[256,256]{1,0:T(8,128)(2,1)S(1)}, bf16[256,256]{1,0:T(8,128)(2,1)S(1)}, u32[]{:S(2)}, u32[]{:S(2)}) collective-permute-start(bf16[256,256]{1,0:T(8,128)(2,1)S(1)} %add_convert_fusion.1), channel_id=1, source_target_pairs={{1,0},{5,1},{3,2},{7,3},{0,4},{4,5},{2,6},{6,7},{9,8},{13,9},{11,1... | collective-permute-start | bytes 393224 | tf_op jit(solution)/shard_map/ppermute | solution.py:24
  61.1 6.7 %collective-permute-start.14 = (bf16[256,256]{1,0:T(8,128)(2,1)S(1)}, bf16[256,256]{1,0:T(8,128)(2,1)S(1)}, u32[]{:S(2)}, u32[]{:S(2)}) collective-permute-start(bf16[256,256]{1,0:T(8,128)(2,1)S(1)} %add_convert_fusion.1), channel_id=1, source_target_pairs={{8,0},{12,1},{10,2},{14,3},{9,4},{13,5},{11,6},{15,7},{0,8},{4,9},... | collective-permute-start | bytes 393224 | tf_op jit(solution)/shard_map/ppermute | solution.py:24
  61.6 8.4 %collective-permute-start.15 = (bf16[256,256]{1,0:T(8,128)(2,1)S(1)}, bf16[256,256]{1,0:T(8,128)(2,1)S(1)}, u32[]{:S(2)}, u32[]{:S(2)}) collective-permute-start(bf16[256,256]{1,0:T(8,128)(2,1)S(1)} %add_convert_fusion.1), channel_id=1, source_target_pairs={{9,0},{13,1},{11,2},{15,3},{8,4},{12,5},{10,6},{14,7},{1,8},{5,9},... | collective-permute-start | bytes 393224 | tf_op jit(solution)/shard_map/ppermute | solution.py:24
  65.0 5.0 %copy-start.3 = (bf16[256,256]{1,0:T(8,128)(2,1)}, bf16[256,256]{1,0:T(8,128)(2,1)S(1)}, u32[]{:S(2)}) copy-start(bf16[256,256]{1,0:T(8,128)(2,1)S(1)} %collective-permute-done.12.refs_0_) | copy-start | bytes 393220
  65.4 4.6 %copy-start.4 = (bf16[256,256]{1,0:T(8,128)(2,1)}, bf16[256,256]{1,0:T(8,128)(2,1)S(1)}, u32[]{:S(2)}) copy-start(bf16[256,256]{1,0:T(8,128)(2,1)S(1)} %collective-permute-done.13.refs_1_) | copy-start | bytes 393220
  67.7 2.3 %copy-start.5 = (bf16[256,256]{1,0:T(8,128)(2,1)}, bf16[256,256]{1,0:T(8,128)(2,1)S(1)}, u32[]{:S(2)}) copy-start(bf16[256,256]{1,0:T(8,128)(2,1)S(1)} %collective-permute-done.14.refs_2_) | copy-start | bytes 393220
  70.0 0.6 copy-start.6

commit v4 on v3

--- a/solution.py
+++ b/solution.py
@@ -36,7 +36,7 @@
 
 
 def product_kernel(high, wide, *refs):
-    near_refs, far_ref = refs[:wide], refs[wide]
+    near_refs, far_refs = refs[:2], refs[2 : wide + 1]
     refs = refs[wide + 1 :]
     x_refs, other_ref = refs[:high], refs[high]
     keep_y, send_y, keep_g, send_g, a_all, x_all, x_row, y_all, g_all = refs[high + 1 :]
@@ -54,7 +54,7 @@
             for kk in range(2):
                 t = kk * wide + dx
                 a_all[dy * block : (dy + 1) * block, t * block : (t + 1) * block] = (
-                    far_ref[dx, kk] if dy else near_refs[dx][kk]
+                    far_refs[dx - 1][dy, kk] if dx else near_refs[dy][kk]
                 )
     x_row[pl.ds(pl.multiple_of(swap * block, block), block), :] = x_refs[0][:, :width]
     x_row[pl.ds(pl.multiple_of((1 - swap) * block, block), block), :] = other_ref[:, :width]
@@ -76,6 +76,18 @@
     keep_g[block:] = g_all[2 * k + 1 - low]
     send_g[:block] = g_all[2 * (1 - k) + low].astype(jnp.bfloat16)
     send_g[block:] = g_all[2 * (1 - k) + 1 - low].astype(jnp.bfloat16)
+
+
+def inverse_kernel(y_ref, which_ref, one_ref, two_ref, out_one, out_two):
+    block = y_ref.shape[0]
+    flip = which_ref[0] == 1
+    near, far = y_ref[:, :block], y_ref[:, block : 2 * block]
+    zero = jnp.where(flip, far, near)
+    unit = jnp.where(flip, near, far)
+    out_one[:, 0, :] = jnp.where(one_ref[0] != 0, -zero, jnp.zeros_like(zero))
+    out_one[:, 1, :] = jnp.where(one_ref[1] != 0, -unit, jnp.zeros_like(unit))
+    last = y_ref[:, 2 * block :]
+    out_two[...] = jnp.where(two_ref[0] != 0, -last, jnp.zeros_like(last))
 
 
 def finish_kernel(*refs):
@@ -119,8 +131,8 @@
     keep_two = pattern_two.reshape(1)
     flip = near[0] == 1
     one = factor_one.reshape(block, 2, block)
-    zero = one[:, 0] * keep_one[0].astype(jnp.bfloat16)
-    unit = one[:, 1] * keep_one[1].astype(jnp.bfloat16)
+    one = jnp.where(keep_one[None, :, None] != 0, one, jnp.bfloat16(0))
+    zero, unit = one[:, 0], one[:, 1]
     pair = jnp.concatenate([jnp.where(flip, unit, zero), jnp.where(flip, zero, unit)], axis=1)
     last = factor_two.reshape(block, block) * keep_two[0].astype(jnp.bfloat16)
     cols = jnp.concatenate([pair, last], axis=1)
@@ -139,13 +151,13 @@
     pieces = {d: across(cols, d) for d in [*range(2, high, 2), 1]}
     own = across(jnp.concatenate([cols, coupling], axis=1), 0)
     now = anc
-    near_anc = [anc] + [plane(now, 0, dx) for dx in range(1, wide)]
+    near_anc = [anc, plane(now, 1, 0)]
     stacked = jnp.stack(near_anc)
-    far_anc = plane(stacked, 1, 0)
+    far_anc = [plane(stacked, 0, dx) for dx in range(1, wide)]
     for d in range(3, high, 2):
         pieces[d] = beside(pieces[d - 1])
-    pieces[1], own_now = lax.optimization_barrier((pieces[1], own))
-    other = send(own_now, sizes, lambda z, y, x, k: (z, y, x, 1 - k))
+    cols_now = cols
+    other = send(cols_now, sizes, lambda z, y, x, k: (z, 1 - k, x, y))
     pieces = [own] + [pieces[d] for d in range(1, high)]
     width = 3 * block
     keep_y, send_y, keep_g, send_g = pl.pallas_call(
@@ -165,7 +177,7 @@
         ],
         compiler_params=pltpu.CompilerParams(vmem_limit_bytes=48 * 1024 * 1024),
         name="products",
-    )(*near_anc, far_anc, *pieces, other)
+    )(*near_anc, *far_anc, *pieces, other)
 
     def core_swap(value):
         return send(value, sizes, lambda z, y, x, k: (z, y, x, 1 - k))
@@ -188,11 +200,17 @@
 
     row_y = (keep_y + core_swap(send_y)).astype(jnp.bfloat16)
     row_y = send(row_y, sizes, lambda z, y, x, k: (z, k, x, y))
-    near_y, far_y, last_y = row_y[:, :block], row_y[:, block : 2 * block], row_y[:, 2 * block :]
-    inv_zero = jnp.where(flip, far_y, near_y)
-    inv_unit = jnp.where(flip, near_y, far_y)
-    inv_one = jnp.stack([inv_zero, inv_unit], axis=1) * -keep_one.astype(jnp.bfloat16)[None, :, None]
-    inv_two = last_y * -keep_two.astype(jnp.bfloat16)[0]
+    inv_one, inv_two = pl.pallas_call(
+        inverse_kernel,
+        out_shape=(
+            jax.ShapeDtypeStruct((block, 2, block), jnp.bfloat16),
+            jax.ShapeDtypeStruct((block, block), jnp.bfloat16),
+        ),
+        in_specs=[pl.BlockSpec(memory_space=pltpu.VMEM)] + [pl.BlockSpec(memory_space=pltpu.SMEM)] * 3,
+        compiler_params=pltpu.CompilerParams(vmem_limit_bytes=8 * 1024 * 1024),
+        name="inverse",
+    )(row_y, near.astype(jnp.int32), keep_one, keep_two)
+    terms[0], inv_one, inv_two = lax.optimization_barrier((terms[0], inv_one, inv_two))
 
     out_one, out_parent, out_two = pl.pallas_call(
         finish_kernel,
@@ -204,6 +222,7 @@
         in_specs=[pl.BlockSpec(memory_space=pltpu.VMEM)] * 7
         + [pl.BlockSpec(memory_space=pltpu.SMEM)],
         scratch_shapes=[pltpu.VMEM((4, block, block), jnp.float32)],
+        compiler_params=pltpu.CompilerParams(vmem_limit_bytes=8 * 1024 * 1024),
         name="finish",
     )(
         *terms,

time: 75.3 us -> 71.2 us (0.946)
  waiting for transfers between devices: 39.3 us -> 35 us
  starting transfers between devices: 22.9 us -> 26.1 us
  other arithmetic: 2.49 us -> 0.49 us
  local copies, waits for them, and re-layouts: 3.93 us -> 2.57 us
    ppermute x16, waiting for transfers between devices: 39.3 us -> 35 us  [send(): return lax.ppermute(value, AXES, pairs)]
    ppermute x16, starting transfers between devices: 22.9 us -> 26.1 us  [send(): return lax.ppermute(value, AXES, pairs)]
    pallas_call x0 -> x1, Pallas kernels: none -> 1.81 us  [body(): pl.pallas_call(inverse_kernel, out_shape=(jax.ShapeDtypeStruct((block, 2,...]
    pallas_call x1, Pallas kernels: 2.65 us -> 1.32 us  [body(): pl.pallas_call(finish_kernel, out_shape=(jax.ShapeDtypeStruct((2, block,...]
    select_n x1, other arithmetic: 1.35 us -> 0.02 us  [body(): jnp.where(flip, unit, zero)]
    unnamed x19 -> x13, local copies, waits for them, and re-layouts: 3.33 us -> 2.56 us
  transfers between devices with their start and end apart: 16 -> 16, of which waited for: 12 -> 9; matrix products, arithmetic and copies ran while one was open for 0% -> 1% of each run, Pallas kernels for 4% -> 3%
where the time goes in v4:
time: 71.2 us; the launch traced here: 71 us
  waiting for transfers between devices  35 us (49%)
  starting transfers between devices  26.1 us (37%)
  Pallas kernels  4.71 us (7%)
  local copies, waits for them, and re-layouts  2.57 us (4%)
  between operations  2.14 us (3%)
    ppermute x16, waiting for transfers between devices, send(): return lax.ppermute(value, AXES, pairs)  35 us
    ppermute x16, starting transfers between devices, send(): return lax.ppermute(value, AXES, pairs)  26.1 us
    unnamed x13, local copies, waits for them, and re-layouts  2.56 us
    pallas_call x1, Pallas kernels, body(): pl.pallas_call(inverse_kernel, out_shape=(jax.ShapeDtypeStruct((block, 2,...  1.81 us
    pallas_call x1, Pallas kernels, body(): pl.pallas_call(functools.partial(product_kernel, high, wide), out_shape=(...  1.58 us
  transfers between devices with their start and end apart: 16, of which 9 were waited for; matrix products, arithmetic and copies ran while one was open for 1% of the time, Pallas kernels for 3%

profile of v4, /device:TPU:1, one launch (start us, length us, event | category | flops | bytes accessed | tf_op | source)
XLA Modules:
  0.0 71.0 jit_solution(656741410920219347)
XLA Ops:
  0.6 1.0 %copy.21 = bf16[1,1,256,2,1,256]{5,2,3,4,1,0:T(8,128)(2,1)S(1)} copy(bf16[1,1,256,2,1,256]{5,3,4,2,1,0:T(2,128)(2,1)} %param.9) | data formatting | bytes 524288 | tf_op args[0]
  1.7 2.1 %collective-permute-start = (bf16[2,256,256]{2,1,0:T(8,128)(2,1)S(1)}, bf16[2,256,256]{2,1,0:T(8,128)(2,1)S(1)}, u32[]{:S(2)}, u32[]{:S(2)}) collective-permute-start(bf16[2,256,256]{2,1,0:T(8,128)(2,1)S(1)} %bitcast.40), channel_id=1, source_target_pairs={{4,0},{5,1},{6,2},{7,3},{0,4},{1,5},{2,6},{3,7},{12,8},{13,9},{14,... | collective-permute-start | bytes 786440 | tf_op jit(solution)/shard_map/ppermute | solution.py:24
  5.1 0.6 copy-done.3
  5.8 0.1 bitcast_select_fusion
  5.9 0.9 %copy-done.5 = bf16[1,1,256,1,1,256]{5,2,4,3,1,0:T(8,128)(2,1)S(1)} copy-done((bf16[1,1,256,1,1,256]{5,2,4,3,1,0:T(8,128)(2,1)S(1)}, bf16[1,1,256,1,1,256]{5,2,4,3,1,0:T(8,128)(2,1)}, u32[]{:S(2)}) %copy-start.5) | copy-done | bytes 131096
  6.9 3.2 %collective-permute-start.4 = (bf16[256,768]{1,0:T(8,128)(2,1)S(1)}, bf16[256,768]{1,0:T(8,128)(2,1)S(1)}, u32[]{:S(2)}, u32[]{:S(2)}) collective-permute-start(bf16[256,768]{1,0:T(8,128)(2,1)S(1)} %pad_maximum_fusion.2), channel_id=1, source_target_pairs={{16,0},{20,1},{18,2},{22,3},{17,4},{21,5},{19,6},{23,7},{24,8},{28... | collective-permute-start | bytes 1179656 | tf_op jit(solution)/shard_map/ppermute | solution.py:24
  10.1 2.6 %collective-permute-start.2 = (bf16[256,1024]{1,0:T(8,128)(2,1)S(1)}, bf16[256,1024]{1,0:T(8,128)(2,1)S(1)}, u32[]{:S(2)}, u32[]{:S(2)}) collective-permute-start(bf16[256,1024]{1,0:T(8,128)(2,1)S(1)} %pad_maximum_fusion.1), channel_id=1, source_target_pairs={{0,0},{4,1},{2,2},{6,3},{1,4},{5,5},{3,6},{7,7},{8,8},{12,9},{10,1... | collective-permute-start | bytes 1572872 | tf_op jit(solution)/shard_map/ppermute | solution.py:24
  12.7 1.3 %collective-permute-start.1 = (bf16[2,2,256,256]{3,2,1,0:T(8,128)(2,1)S(1)}, bf16[2,2,256,256]{3,2,1,0:T(8,128)(2,1)S(1)}, u32[]{:S(2)}, u32[]{:S(2)}) collective-permute-start(bf16[2,2,256,256]{3,2,1,0:T(8,128)(2,1)S(1)} %pad_maximum_fusion), channel_id=1, source_target_pairs={{2,0},{3,1},{0,2},{1,3},{6,4},{7,5},{4,6},{5,7},{10,8},{11,9},{8,1... | collective-permute-start | bytes 1572872 | tf_op jit(solution)/shard_map/ppermute | solution.py:24
  14.0 2.4 %collective-permute-start.3 = (bf16[256,768]{1,0:T(8,128)(2,1)S(1)}, bf16[256,768]{1,0:T(8,128)(2,1)S(1)}, u32[]{:S(2)}, u32[]{:S(2)}) collective-permute-start(bf16[256,768]{1,0:T(8,128)(2,1)S(1)} %pad_maximum_fusion.2), channel_id=1, source_target_pairs={{8,0},{12,1},{10,2},{14,3},{9,4},{13,5},{11,6},{15,7},{0,8},{4,9},... | collective-permute-start | bytes 1179656 | tf_op jit(solution)/shard_map/ppermute | solution.py:24
  16.4 10.8 %collective-permute-done.4.refs_5_ = bf16[256,768]{1,0:T(8,128)(2,1)S(1)} collective-permute-done((bf16[256,768]{1,0:T(8,128)(2,1)S(1)}, bf16[256,768]{1,0:T(8,128)(2,1)S(1)}, u32[]{:S(2)}, u32[]{:S(2)}) %collective-permute-start.4) | collective-permute-done | bytes 393248 | tf_op jit(solution)/shard_map/ppermute | solution.py:24
  27.1 1.4 %collective-permute-start.5 = (bf16[256,768]{1,0:T(8,128)(2,1)S(1)}, bf16[256,768]{1,0:T(8,128)(2,1)S(1)}, u32[]{:S(2)}, u32[]{:S(2)}) collective-permute-start(bf16[256,768]{1,0:T(8,128)(2,1)S(1)} %collective-permute-done.4.refs_5_), channel_id=1, source_target_pairs={{8,0},{9,1},{10,2},{11,3},{12,4},{13,5},{14,6},{15,7},{0,8},{1,9},... | collective-permute-start | bytes 1179656 | tf_op jit(solution)/shard_map/ppermute | solution.py:24
  28.5 5.1 %collective-permute-done.3.refs_4_ = bf16[256,768]{1,0:T(8,128)(2,1)S(1)} collective-permute-done((bf16[256,768]{1,0:T(8,128)(2,1)S(1)}, bf16[256,768]{1,0:T(8,128)(2,1)S(1)}, u32[]{:S(2)}, u32[]{:S(2)}) %collective-permute-start.3) | collective-permute-done | bytes 393248 | tf_op jit(solution)/shard_map/ppermute | solution.py:24
  33.6 7.7 %collective-permute-done.5.refs_6_ = bf16[256,768]{1,0:T(8,128)(2,1)S(1)} collective-permute-done((bf16[256,768]{1,0:T(8,128)(2,1)S(1)}, bf16[256,768]{1,0:T(8,128)(2,1)S(1)}, u32[]{:S(2)}, u32[]{:S(2)}) %collective-permute-start.5) | collective-permute-done | bytes 393248 | tf_op jit(solution)/shard_map/ppermute | solution.py:24
  41.3 1.6 %products.1 = (f32[256,768]{1,0:T(8,128)S(1)}, f32[256,768]{1,0:T(8,128)S(1)}, f32[512,256]{1,0:T(8,128)S(1)}, bf16[512,256]{1,0:T(8,128)(2,1)S(1)}) custom-call(bf16[2,256,256]{2,1,0:T(8,128)(2,1)S(1)} %bitcast.42, bf16[2,256,256]{2,1,0:T(8,128)(2,1)S(1)} %collective-permute-done.refs_1_, bf16[2,2,256,256]{3,2,1,0:T(8,128)(2,1)S(1)} %collective-permute-done.1.refs_2_, ...), custom_call_target="tpu_custom_call" | custom-call | tf_op jit(solution)/shard_map/products/pallas_call | solution.py:163
  42.9 0.5 collective-permute-start.7
  43.3 0.1 collective-permute-start.11
  43.4 1.0 %collective-permute-done.7 = bf16[512,256]{1,0:T(8,128)(2,1)S(1)} collective-permute-done((bf16[512,256]{1,0:T(8,128)(2,1)S(1)}, bf16[512,256]{1,0:T(8,128)(2,1)S(1)}, u32[]{:S(2)}, u32[]{:S(2)}) %collective-permute-start.7) | collective-permute-done | bytes 262176 | tf_op jit(solution)/shard_map/ppermute | solution.py:24
  44.6 0.1 collective-permute-start.8
  44.6 4.7 %collective-permute-done.8 = bf16[256,256]{1,0:T(8,128)(2,1)S(1)} collective-permute-done((bf16[256,256]{1,0:T(8,128)(2,1)S(1)}, bf16[256,256]{1,0:T(8,128)(2,1)S(1)}, u32[]{:S(2)}, u32[]{:S(2)}) %collective-permute-start.8) | collective-permute-done | bytes 131104 | tf_op jit(solution)/shard_map/ppermute | solution.py:24
  49.4 2.4 %collective-permute-start.9 = (bf16[256,256]{1,0:T(8,128)(2,1)S(1)}, bf16[256,256]{1,0:T(8,128)(2,1)S(1)}, u32[]{:S(2)}, u32[]{:S(2)}) collective-permute-start(bf16[256,256]{1,0:T(8,128)(2,1)S(1)} %fusion), channel_id=1, source_target_pairs={{16,0},{17,1},{18,2},{19,3},{20,4},{21,5},{22,6},{23,7},{24,8},{25... | collective-permute-start | bytes 393224 | tf_op jit(solution)/shard_map/ppermute | solution.py:24
  51.7 0.1 add_convert_fusion
  51.9 3.9 %collective-permute-start.12 = (bf16[256,768]{1,0:T(8,128)(2,1)S(1)}, bf16[256,768]{1,0:T(8,128)(2,1)S(1)}, u32[]{:S(2)}, u32[]{:S(2)}) collective-permute-start(bf16[256,768]{1,0:T(8,128)(2,1)S(1)} %add_convert_fusion), channel_id=1, source_target_pairs={{0,0},{4,1},{2,2},{6,3},{1,4},{5,5},{3,6},{7,7},{8,8},{12,9},{10,1... | collective-permute-start | bytes 1179656 | tf_op jit(solution)/shard_map/ppermute | solution.py:24
  55.7 1.9 %collective-permute-done.9 = bf16[256,256]{1,0:T(8,128)(2,1)S(1)} collective-permute-done((bf16[256,256]{1,0:T(8,128)(2,1)S(1)}, bf16[256,256]{1,0:T(8,128)(2,1)S(1)}, u32[]{:S(2)}, u32[]{:S(2)}) %collective-permute-start.9) | collective-permute-done | bytes 131104 | tf_op jit(solution)/shard_map/ppermute | solution.py:24
  57.7 4.4 %collective-permute-start.10 = (bf16[256,256]{1,0:T(8,128)(2,1)S(1)}, bf16[256,256]{1,0:T(8,128)(2,1)S(1)}, u32[]{:S(2)}, u32[]{:S(2)}) collective-permute-start(bf16[256,256]{1,0:T(8,128)(2,1)S(1)} %add_convert_fusion.1), channel_id=1, source_target_pairs={{0,0},{4,1},{2,2},{6,3},{1,4},{5,5},{3,6},{7,7},{8,8},{12,9},{10,1... | collective-permute-start | bytes 393224 | tf_op jit(solution)/shard_map/ppermute | solution.py:24
  62.1 0.1 collective-permute-start.15
  62.2 0.5 collective-permute-start.14
  62.6 1.4 %collective-permute-start.13 = (bf16[256,256]{1,0:T(8,128)(2,1)S(1)}, bf16[256,256]{1,0:T(8,128)(2,1)S(1)}, u32[]{:S(2)}, u32[]{:S(2)}) collective-permute-start(bf16[256,256]{1,0:T(8,128)(2,1)S(1)} %add_convert_fusion.1), channel_id=1, source_target_pairs={{1,0},{5,1},{3,2},{7,3},{0,4},{4,5},{2,6},{6,7},{9,8},{13,9},{11,1... | collective-permute-start | bytes 393224 | tf_op jit(solution)/shard_map/ppermute | solution.py:24
  64.0 1.8 %inverse.1 = (bf16[256,2,256]{2,1,0:T(2,128)(2,1)}, bf16[256,256]{1,0:T(8,128)(2,1)}) custom-call(bf16[256,768]{1,0:T(8,128)(2,1)S(1)} %collective-permute-done.12.y_ref, s32[1]{0:T(128)S(6)} %select_n.27.which_ref.refs_7_, s32[2]{0:T(128)S(1)} %bitcast.48, s32[1]{0:T(128)} %bitcast.35.two_ref), custom_call_target="tpu_custom_call" | custom-call | tf_op jit(solution)/shard_map/inverse/pallas_call | solution.py:203
  65.8 1.9 %collective-permute-done.15.refs_3_ = bf16[256,256]{1,0:T(8,128)(2,1)S(1)} collective-permute-done((bf16[256,256]{1,0:T(8,128)(2,1)S(1)}, bf16[256,256]{1,0:T(8,128)(2,1)S(1)}, u32[]{:S(2)}, u32[]{:S(2)}) %collective-permute-start.15) | collective-permute-done | bytes 131104 | tf_op jit(solution)/shard_map/ppermute | solution.py:24
  67.7 1.2 %collective-permute-done.14.refs_2_ = bf16[256,256]{1,0:T(8,128)(2,1)S(1)} collective-permute-done((bf16[256,256]{1,0:T(8,128)(2,1)S(1)}, bf16[256,256]{1,0:T(8,128)(2,1)S(1)}, u32[]{:S(2)}, u32[]{:S(2)}) %collective-permute-start.14) | collective-permute-done | bytes 131104 | tf_op jit(solution)/shard_map/ppermute | solution.py:24
  68.9 0.8 %collective-permute-done.13.refs_1_ = bf16[256,256]{1,0:T(8,128)(2,1)S(1)} collective-permute-done((bf16[256,256]{1,0:T(8,128)(2,1)S(1)}, bf16[256,256]{1,0:T(8,128)(2,1)S(1)}, u32[]{:S(2)}, u32[]{:S(2)}) %collective-permute-start.13) | collective-permute-done | bytes 131104 | tf_op jit(solution)/shard_map/ppermute | solution.py:24
  69.7 1.3 %finish.1 = (f32[2,256,256]{2,1,0:T(8,128)}, bf16[256,256]{1,0:T(8,128)(2,1)}, f32[256,256]{1,0:T(8,128)}) custom-call(bf16[256,256]{1,0:T(8,128)(2,1)S(1)} %collective-permute-done.10.refs_0_, bf16[256,256]{1,0:T(8,128)(2,1)S(1)} %collective-permute-done.13.refs_1_, bf16[256,256]{1,0:T(8,128)(2,1)S(1)} %collective-permute-done.14.refs_2_, ...), custom_call_target="tpu_custom_call" | custom-call | tf_op jit(solution)/shard_map/finish/pallas_call | solution.py:215
  (28 shorter events, 0.4 us)
Async XLA Ops:
  0.6 5.2 %copy-start.4 = (bf16[1,1,256,2,1,256]{5,3,4,2,1,0:T(2,128)(2,1)S(1)}, bf16[1,1,256,2,1,256]{5,3,4,2,1,0:T(2,128)(2,1)}, u32[]{:S(2)}) copy-start(bf16[1,1,256,2,1,256]{5,3,4,2,1,0:T(2,128)(2,1)} %param.10) | copy-start | bytes 786436
  1.7 11.0 %collective-permute-start = (bf16[2,256,256]{2,1,0:T(8,128)(2,1)S(1)}, bf16[2,256,256]{2,1,0:T(8,128)(2,1)S(1)}, u32[]{:S(2)}, u32[]{:S(2)}) collective-permute-start(bf16[2,256,256]{2,1,0:T(8,128)(2,1)S(1)} %bitcast.40), channel_id=1, source_target_pairs={{4,0},{5,1},{6,2},{7,3},{0,4},{1,5},{2,6},{3,7},{12,8},{13,9},{14,... | collective-permute-start | bytes 786440 | tf_op jit(solution)/shard_map/ppermute | solution.py:24
  5.1 0.7 copy-start.3
  5.9 0.9 %copy-start.5 = (bf16[1,1,256,1,1,256]{5,2,4,3,1,0:T(8,128)(2,1)S(1)}, bf16[1,1,256,1,1,256]{5,2,4,3,1,0:T(8,128)(2,1)}, u32[]{:S(2)}) copy-start(bf16[1,1,256,1,1,256]{5,2,4,3,1,0:T(8,128)(2,1)} %param.11) | copy-start | bytes 393220
  6.8 3.2 %copy-start.1 = (bf16[1,1,256,256]{3,2,1,0:T(8,128)(2,1)S(1)}, bf16[1,1,256,256]{3,2,1,0:T(8,128)(2,1)}, u32[]{:S(2)}) copy-start(bf16[1,1,256,256]{3,2,1,0:T(8,128)(2,1)} %param.12) | copy-start | bytes 393220
  6.9 20.3 %collective-permute-start.4 = (bf16[256,768]{1,0:T(8,128)(2,1)S(1)}, bf16[256,768]{1,0:T(8,128)(2,1)S(1)}, u32[]{:S(2)}, u32[]{:S(2)}) collective-permute-start(bf16[256,768]{1,0:T(8,128)(2,1)S(1)} %pad_maximum_fusion.2), channel_id=1, source_target_pairs={{16,0},{20,1},{18,2},{22,3},{17,4},{21,5},{19,6},{23,7},{24,8},{28... | collective-permute-start | bytes 1179656 | tf_op jit(solution)/shard_map/ppermute | solution.py:24
  10.1 23.5 %collective-permute-start.2 = (bf16[256,1024]{1,0:T(8,128)(2,1)S(1)}, bf16[256,1024]{1,0:T(8,128)(2,1)S(1)}, u32[]{:S(2)}, u32[]{:S(2)}) collective-permute-start(bf16[256,1024]{1,0:T(8,128)(2,1)S(1)} %pad_maximum_fusion.1), channel_id=1, source_target_pairs={{0,0},{4,1},{2,2},{6,3},{1,4},{5,5},{3,6},{7,7},{8,8},{12,9},{10,1... | collective-permute-start | bytes 1572872 | tf_op jit(solution)/shard_map/ppermute | solution.py:24
  12.7 20.9 %collective-permute-start.1 = (bf16[2,2,256,256]{3,2,1,0:T(8,128)(2,1)S(1)}, bf16[2,2,256,256]{3,2,1,0:T(8,128)(2,1)S(1)}, u32[]{:S(2)}, u32[]{:S(2)}) collective-permute-start(bf16[2,2,256,256]{3,2,1,0:T(8,128)(2,1)S(1)} %pad_maximum_fusion), channel_id=1, source_target_pairs={{2,0},{3,1},{0,2},{1,3},{6,4},{7,5},{4,6},{5,7},{10,8},{11,9},{8,1... | collective-permute-start | bytes 1572872 | tf_op jit(solution)/shard_map/ppermute | solution.py:24
  14.0 14.5 %collective-permute-start.6 = (bf16[256,768]{1,0:T(8,128)(2,1)S(1)}, bf16[256,768]{1,0:T(8,128)(2,1)S(1)}, u32[]{:S(2)}, u32[]{:S(2)}) collective-permute-start(bf16[256,768]{1,0:T(8,128)(2,1)S(1)} %pad_maximum_fusion.2), channel_id=1, source_target_pairs={{4,0},{0,1},{6,2},{2,3},{5,4},{1,5},{7,6},{3,7},{12,8},{8,9},{14,1... | collective-permute-start | bytes 1179656 | tf_op jit(solution)/shard_map/ppermute | solution.py:24
  14.0 19.6 %collective-permute-start.3 = (bf16[256,768]{1,0:T(8,128)(2,1)S(1)}, bf16[256,768]{1,0:T(8,128)(2,1)S(1)}, u32[]{:S(2)}, u32[]{:S(2)}) collective-permute-start(bf16[256,768]{1,0:T(8,128)(2,1)S(1)} %pad_maximum_fusion.2), channel_id=1, source_target_pairs={{8,0},{12,1},{10,2},{14,3},{9,4},{13,5},{11,6},{15,7},{0,8},{4,9},... | collective-permute-start | bytes 1179656 | tf_op jit(solution)/shard_map/ppermute | solution.py:24
  27.1 14.1 %collective-permute-start.5 = (bf16[256,768]{1,0:T(8,128)(2,1)S(1)}, bf16[256,768]{1,0:T(8,128)(2,1)S(1)}, u32[]{:S(2)}, u32[]{:S(2)}) collective-permute-start(bf16[256,768]{1,0:T(8,128)(2,1)S(1)} %collective-permute-done.4.refs_5_), channel_id=1, source_target_pairs={{8,0},{9,1},{10,2},{11,3},{12,4},{13,5},{14,6},{15,7},{0,8},{1,9},... | collective-permute-start | bytes 1179656 | tf_op jit(solution)/shard_map/ppermute | solution.py:24
  42.9 1.6 %collective-permute-start.7 = (bf16[512,256]{1,0:T(8,128)(2,1)S(1)}, bf16[512,256]{1,0:T(8,128)(2,1)S(1)}, u32[]{:S(2)}, u32[]{:S(2)}) collective-permute-start(bf16[512,256]{1,0:T(8,128)(2,1)S(1)} %get-tuple-element.18), channel_id=1, source_target_pairs={{1,0},{0,1},{3,2},{2,3},{5,4},{4,5},{7,6},{6,7},{9,8},{8,9},{11,10... | collective-permute-start | bytes 786440 | tf_op jit(solution)/shard_map/ppermute | solution.py:24
  43.3 8.4 %collective-permute-start.11 = (f32[256,768]{1,0:T(8,128)S(1)}, f32[256,768]{1,0:T(8,128)S(1)}, u32[]{:S(2)}, u32[]{:S(2)}) collective-permute-start(f32[256,768]{1,0:T(8,128)S(1)} %get-tuple-element.20), channel_id=1, source_target_pairs={{1,0},{0,1},{3,2},{2,3},{5,4},{4,5},{7,6},{6,7},{9,8},{8,9},{11,10... | collective-permute-start | bytes 2359304 | tf_op jit(solution)/shard_map/ppermute | solution.py:24
  44.6 4.8 %collective-permute-start.8 = (bf16[256,256]{1,0:T(8,128)(2,1)S(1)}, bf16[256,256]{1,0:T(8,128)(2,1)S(1)}, u32[]{:S(2)}, u32[]{:S(2)}) collective-permute-start(bf16[256,256]{1,0:T(8,128)(2,1)S(1)} %slice.29), channel_id=1, source_target_pairs={{8,0},{9,1},{10,2},{11,3},{12,4},{13,5},{14,6},{15,7},{0,8},{1,9},... | collective-permute-start | bytes 393224 | tf_op jit(solution)/shard_map/ppermute | solution.py:24
  49.4 8.3 %collective-permute-start.9 = (bf16[256,256]{1,0:T(8,128)(2,1)S(1)}, bf16[256,256]{1,0:T(8,128)(2,1)S(1)}, u32[]{:S(2)}, u32[]{:S(2)}) collective-permute-start(bf16[256,256]{1,0:T(8,128)(2,1)S(1)} %fusion), channel_id=1, source_target_pairs={{16,0},{17,1},{18,2},{19,3},{20,4},{21,5},{22,6},{23,7},{24,8},{25... | collective-permute-start | bytes 393224 | tf_op jit(solution)/shard_map/ppermute | solution.py:24
  51.8 17.8 %copy-start = (f32[2,1,256,256]{3,2,1,0:T(8,128)S(1)}, f32[2,1,256,256]{3,2,1,0:T(8,128)}, u32[]{:S(2)}) copy-start(f32[2,1,256,256]{3,2,1,0:T(8,128)} %param.13) | copy-start | bytes 1572868
  51.9 12.2 %collective-permute-start.12 = (bf16[256,768]{1,0:T(8,128)(2,1)S(1)}, bf16[256,768]{1,0:T(8,128)(2,1)S(1)}, u32[]{:S(2)}, u32[]{:S(2)}) collective-permute-start(bf16[256,768]{1,0:T(8,128)(2,1)S(1)} %add_convert_fusion), channel_id=1, source_target_pairs={{0,0},{4,1},{2,2},{6,3},{1,4},{5,5},{3,6},{7,7},{8,8},{12,9},{10,1... | collective-permute-start | bytes 1179656 | tf_op jit(solution)/shard_map/ppermute | solution.py:24
  57.7 12.0 %copy-start.2 = (f32[1,1,256,256]{3,2,1,0:T(8,128)S(1)}, f32[1,1,256,256]{3,2,1,0:T(8,128)}, u32[]{:S(2)}) copy-start(f32[1,1,256,256]{3,2,1,0:T(8,128)} %param.14) | copy-start | bytes 786436
  57.7 8.2 %collective-permute-start.10 = (bf16[256,256]{1,0:T(8,128)(2,1)S(1)}, bf16[256,256]{1,0:T(8,128)(2,1)S(1)}, u32[]{:S(2)}, u32[]{:S(2)}) collective-permute-start(bf16[256,256]{1,0:T(8,128)(2,1)S(1)} %add_convert_fusion.1), channel_id=1, source_target_pairs={{0,0},{4,1},{2,2},{6,3},{1,4},{5,5},{3,6},{7,7},{8,8},{12,9},{10,1... | collective-permute-start | bytes 393224 | tf_op jit(solution)/shard_map/ppermute | solution.py:24
  62.1 5.7 %collective-permute-start.15 = (bf16[256,256]{1,0:T(8,128)(2,1)S(1)}, bf16[256,256]{1,0:T(8,128)(2,1)S(1)}, u32[]{:S(2)}, u32[]{:S(2)}) collective-permute-start(bf16[256,256]{1,0:T(8,128)(2,1)S(1)} %add_convert_fusion.1), channel_id=1, source_target_pairs={{9,0},{13,1},{11,2},{15,3},{8,4},{12,5},{10,6},{14,7},{1,8},{5,9},... | collective-permute-start | bytes 393224 | tf_op jit(solution)/shard_map/ppermute | solution.py:24
  62.2 6.8 %collective-permute-start.14 = (bf16[256,256]{1,0:T(8,128)(2,1)S(1)}, bf16[256,256]{1,0:T(8,128)(2,1)S(1)}, u32[]{:S(2)}, u32[]{:S(2)}) collective-permute-start(bf16[256,256]{1,0:T(8,128)(2,1)S(1)} %add_convert_fusion.1), channel_id=1, source_target_pairs={{8,0},{12,1},{10,2},{14,3},{9,4},{13,5},{11,6},{15,7},{0,8},{4,9},... | collective-permute-start | bytes 393224 | tf_op jit(solution)/shard_map/ppermute | solution.py:24
  62.6 7.0 %collective-permute-start.13 = (bf16[256,256]{1,0:T(8,128)(2,1)S(1)}, bf16[256,256]{1,0:T(8,128)(2,1)S(1)}, u32[]{:S(2)}, u32[]{:S(2)}) collective-permute-start(bf16[256,256]{1,0:T(8,128)(2,1)S(1)} %add_convert_fusion.1), channel_id=1, source_target_pairs={{1,0},{5,1},{3,2},{7,3},{0,4},{4,5},{2,6},{6,7},{9,8},{13,9},{11,1... | collective-permute-start | bytes 393224 | tf_op jit(solution)/shard_map/ppermute | solution.py:24

commit v5 on v4

--- a/solution.py
+++ b/solution.py
@@ -38,8 +38,8 @@
 def product_kernel(high, wide, *refs):
     near_refs, far_refs = refs[:2], refs[2 : wide + 1]
     refs = refs[wide + 1 :]
-    x_refs, other_ref = refs[:high], refs[high]
-    keep_y, send_y, keep_g, send_g, a_all, x_all, x_row, y_all, g_all = refs[high + 1 :]
+    x_refs, other_ref, refs = refs[: 3 * high // 2 - 1], refs[3 * high // 2 - 1], refs[3 * high // 2 :]
+    keep_y, send_y, keep_g, send_g, a_all, x_all, x_row, y_all, g_all = refs
     block = other_ref.shape[0]
     z, y, x, k = place()
     low = z % 2
@@ -47,8 +47,14 @@
     swap = y ^ k
     width = 3 * block
     couple = x_refs[0][:, width:]
+    source = iter(x_refs)
     for step in range(high):
-        x_all[pl.ds(pl.multiple_of((turn ^ step) * block, block), block), :] = x_refs[step][:, :width]
+        rows = pl.ds(pl.multiple_of((turn ^ step) * block, block), block)
+        if step < 3 or step % 2 == 0:
+            x_all[rows, :] = next(source)[:, :width]
+        else:
+            x_all[rows, : 2 * block] = next(source)[...]
+            x_all[rows, 2 * block :] = next(source)[...]
     for dy in range(2):
         for dx in range(wide):
             for kk in range(2):
@@ -145,8 +151,8 @@
     def across(value, d):
         return send(value, sizes, lambda z, y, x, k: (z ^ d, k, x, y))
 
-    def beside(value):
-        return send(value, sizes, lambda z, y, x, k: (z ^ 1, y, x, k))
+    def along(value, d):
+        return send(value, sizes, lambda z, y, x, k: (z ^ d, y, x, k))
 
     pieces = {d: across(cols, d) for d in [*range(2, high, 2), 1]}
     own = across(jnp.concatenate([cols, coupling], axis=1), 0)
@@ -155,10 +161,13 @@
     stacked = jnp.stack(near_anc)
     far_anc = [plane(stacked, 0, dx) for dx in range(1, wide)]
     for d in range(3, high, 2):
-        pieces[d] = beside(pieces[d - 1])
+        pieces[d] = (
+            along(pieces[d - 1][:, : 2 * block], 1),
+            along(pieces[1][:, 2 * block :], d - 1),
+        )
     cols_now = cols
     other = send(cols_now, sizes, lambda z, y, x, k: (z, 1 - k, x, y))
-    pieces = [own] + [pieces[d] for d in range(1, high)]
+    pieces = [own] + [p for d in range(1, high) for p in (pieces[d] if d in range(3, high, 2) else (pieces[d],))]
     width = 3 * block
     keep_y, send_y, keep_g, send_g = pl.pallas_call(
         functools.partial(product_kernel, high, wide),
@@ -181,9 +190,6 @@
 
     def core_swap(value):
         return send(value, sizes, lambda z, y, x, k: (z, y, x, 1 - k))
-
-    def along(value, d):
-        return send(value, sizes, lambda z, y, x, k: (z ^ d, y, x, k))
 
     chip = keep_g + core_swap(send_g).astype(jnp.float32)
     total = chip[:block] + along(chip[block:].astype(jnp.bfloat16), 1).astype(jnp.float32)

time: 71.2 us -> 68.6 us (0.963)
  waiting for transfers between devices: 35 us -> 28.7 us
  starting transfers between devices: 26.1 us -> 29.7 us
    ppermute x16 -> x17, waiting for transfers between devices: 35 us -> 28.7 us  [send(): return lax.ppermute(value, AXES, pairs)]
    ppermute x16 -> x17, starting transfers between devices: 26.1 us -> 29.7 us  [send(): return lax.ppermute(value, AXES, pairs)]
  transfers between devices with their start and end apart: 16 -> 17, of which waited for: 9 -> 10; matrix products, arithmetic and copies ran while one was open for 1% -> 1% of each run, Pallas kernels for 3% -> 3%
where the time goes in v5:
time: 68.6 us; the launch traced here: 68.3 us
  starting transfers between devices  29.7 us (43%)
  waiting for transfers between devices  28.7 us (42%)
  Pallas kernels  4.71 us (7%)
  local copies, waits for them, and re-layouts  2.6 us (4%)
  between operations  2.15 us (3%)
    ppermute x17, starting transfers between devices, send(): return lax.ppermute(value, AXES, pairs)  29.7 us
    ppermute x17, waiting for transfers between devices, send(): return lax.ppermute(value, AXES, pairs)  28.7 us
    unnamed x13, local copies, waits for them, and re-layouts  2.56 us
    pallas_call x1, Pallas kernels, body(): pl.pallas_call(inverse_kernel, out_shape=(jax.ShapeDtypeStruct((block, 2,...  1.81 us
    pallas_call x1, Pallas kernels, body(): pl.pallas_call(functools.partial(product_kernel, high, wide), out_shape=(...  1.58 us
  transfers between devices with their start and end apart: 17, of which 10 were waited for; matrix products, arithmetic and copies ran while one was open for 1% of the time, Pallas kernels for 3%

profile of v5, /device:TPU:1, one launch (start us, length us, event | category | flops | bytes accessed | tf_op | source)
XLA Modules:
  0.0 68.3 jit_solution(16611407252317444114)
XLA Ops:
  0.6 1.0 %copy.21 = bf16[1,1,256,2,1,256]{5,2,3,4,1,0:T(8,128)(2,1)S(1)} copy(bf16[1,1,256,2,1,256]{5,3,4,2,1,0:T(2,128)(2,1)} %param.9) | data formatting | bytes 524288 | tf_op args[0]
  1.7 2.1 %collective-permute-start = (bf16[2,256,256]{2,1,0:T(8,128)(2,1)S(1)}, bf16[2,256,256]{2,1,0:T(8,128)(2,1)S(1)}, u32[]{:S(2)}, u32[]{:S(2)}) collective-permute-start(bf16[2,256,256]{2,1,0:T(8,128)(2,1)S(1)} %bitcast.40), channel_id=1, source_target_pairs={{4,0},{5,1},{6,2},{7,3},{0,4},{1,5},{2,6},{3,7},{12,8},{13,9},{14,... | collective-permute-start | bytes 786440 | tf_op jit(solution)/shard_map/ppermute | solution.py:24
  5.1 0.6 copy-done.3
  5.8 0.1 bitcast_select_fusion
  5.9 0.9 %copy-done.5 = bf16[1,1,256,1,1,256]{5,2,4,3,1,0:T(8,128)(2,1)S(1)} copy-done((bf16[1,1,256,1,1,256]{5,2,4,3,1,0:T(8,128)(2,1)S(1)}, bf16[1,1,256,1,1,256]{5,2,4,3,1,0:T(8,128)(2,1)}, u32[]{:S(2)}) %copy-start.5) | copy-done | bytes 131096
  6.9 3.2 %collective-permute-start.4 = (bf16[256,768]{1,0:T(8,128)(2,1)S(1)}, bf16[256,768]{1,0:T(8,128)(2,1)S(1)}, u32[]{:S(2)}, u32[]{:S(2)}) collective-permute-start(bf16[256,768]{1,0:T(8,128)(2,1)S(1)} %pad_maximum_fusion.2), channel_id=1, source_target_pairs={{16,0},{20,1},{18,2},{22,3},{17,4},{21,5},{19,6},{23,7},{24,8},{28... | collective-permute-start | bytes 1179656 | tf_op jit(solution)/shard_map/ppermute | solution.py:24
  10.0 1.7 %collective-permute-start.3 = (bf16[256,768]{1,0:T(8,128)(2,1)S(1)}, bf16[256,768]{1,0:T(8,128)(2,1)S(1)}, u32[]{:S(2)}, u32[]{:S(2)}) collective-permute-start(bf16[256,768]{1,0:T(8,128)(2,1)S(1)} %pad_maximum_fusion.2), channel_id=1, source_target_pairs={{8,0},{12,1},{10,2},{14,3},{9,4},{13,5},{11,6},{15,7},{0,8},{4,9},... | collective-permute-start | bytes 1179656 | tf_op jit(solution)/shard_map/ppermute | solution.py:24
  11.8 3.0 %collective-permute-start.2 = (bf16[256,1024]{1,0:T(8,128)(2,1)S(1)}, bf16[256,1024]{1,0:T(8,128)(2,1)S(1)}, u32[]{:S(2)}, u32[]{:S(2)}) collective-permute-start(bf16[256,1024]{1,0:T(8,128)(2,1)S(1)} %pad_maximum_fusion.1), channel_id=1, source_target_pairs={{0,0},{4,1},{2,2},{6,3},{1,4},{5,5},{3,6},{7,7},{8,8},{12,9},{10,1... | collective-permute-start | bytes 1572872 | tf_op jit(solution)/shard_map/ppermute | solution.py:24
  14.8 1.3 %collective-permute-start.1 = (bf16[2,2,256,256]{3,2,1,0:T(8,128)(2,1)S(1)}, bf16[2,2,256,256]{3,2,1,0:T(8,128)(2,1)S(1)}, u32[]{:S(2)}, u32[]{:S(2)}) collective-permute-start(bf16[2,2,256,256]{3,2,1,0:T(8,128)(2,1)S(1)} %pad_maximum_fusion), channel_id=1, source_target_pairs={{2,0},{3,1},{0,2},{1,3},{6,4},{7,5},{4,6},{5,7},{10,8},{11,9},{8,1... | collective-permute-start | bytes 1572872 | tf_op jit(solution)/shard_map/ppermute | solution.py:24
  16.1 11.0 %collective-permute-done.4.refs_5_ = bf16[256,768]{1,0:T(8,128)(2,1)S(1)} collective-permute-done((bf16[256,768]{1,0:T(8,128)(2,1)S(1)}, bf16[256,768]{1,0:T(8,128)(2,1)S(1)}, u32[]{:S(2)}, u32[]{:S(2)}) %collective-permute-start.4) | collective-permute-done | bytes 393248 | tf_op jit(solution)/shard_map/ppermute | solution.py:24
  27.2 1.4 %collective-permute-start.5 = (bf16[256,512]{1,0:T(8,128)(2,1)S(1)}, bf16[256,512]{1,0:T(8,128)(2,1)S(1)}, u32[]{:S(2)}, u32[]{:S(2)}) collective-permute-start(bf16[256,512]{1,0:T(8,128)(2,1)S(1)} %slice.27), channel_id=1, source_target_pairs={{8,0},{9,1},{10,2},{11,3},{12,4},{13,5},{14,6},{15,7},{0,8},{1,9},... | collective-permute-start | bytes 786440 | tf_op jit(solution)/shard_map/ppermute | solution.py:24
  28.6 2.1 %collective-permute-start.6 = (bf16[256,256]{1,0:T(8,128)(2,1)S(1)}, bf16[256,256]{1,0:T(8,128)(2,1)S(1)}, u32[]{:S(2)}, u32[]{:S(2)}) collective-permute-start(bf16[256,256]{1,0:T(8,128)(2,1)S(1)} %slice.28), channel_id=1, source_target_pairs={{16,0},{17,1},{18,2},{19,3},{20,4},{21,5},{22,6},{23,7},{24,8},{25... | collective-permute-start | bytes 393224 | tf_op jit(solution)/shard_map/ppermute | solution.py:24
  30.7 5.9 %collective-permute-done.6.refs_7_ = bf16[256,256]{1,0:T(8,128)(2,1)S(1)} collective-permute-done((bf16[256,256]{1,0:T(8,128)(2,1)S(1)}, bf16[256,256]{1,0:T(8,128)(2,1)S(1)}, u32[]{:S(2)}, u32[]{:S(2)}) %collective-permute-start.6) | collective-permute-done | bytes 131104 | tf_op jit(solution)/shard_map/ppermute | solution.py:24
  36.6 0.2 collective-permute-done.5.refs_6_
  36.8 1.6 %products.1 = (f32[256,768]{1,0:T(8,128)S(1)}, f32[256,768]{1,0:T(8,128)S(1)}, f32[512,256]{1,0:T(8,128)S(1)}, bf16[512,256]{1,0:T(8,128)(2,1)S(1)}) custom-call(bf16[2,256,256]{2,1,0:T(8,128)(2,1)S(1)} %bitcast.42, bf16[2,256,256]{2,1,0:T(8,128)(2,1)S(1)} %collective-permute-done.refs_1_, bf16[2,2,256,256]{3,2,1,0:T(8,128)(2,1)S(1)} %collective-permute-done.1.refs_2_, ...), custom_call_target="tpu_custom_call" | custom-call | tf_op jit(solution)/shard_map/products/pallas_call | solution.py:172
  38.4 2.0 %collective-permute-start.8 = (bf16[512,256]{1,0:T(8,128)(2,1)S(1)}, bf16[512,256]{1,0:T(8,128)(2,1)S(1)}, u32[]{:S(2)}, u32[]{:S(2)}) collective-permute-start(bf16[512,256]{1,0:T(8,128)(2,1)S(1)} %get-tuple-element.18), channel_id=1, source_target_pairs={{1,0},{0,1},{3,2},{2,3},{5,4},{4,5},{7,6},{6,7},{9,8},{8,9},{11,10... | collective-permute-start | bytes 786440 | tf_op jit(solution)/shard_map/ppermute | solution.py:24
  40.4 0.1 collective-permute-start.12
  40.5 1.1 %collective-permute-done.8 = bf16[512,256]{1,0:T(8,128)(2,1)S(1)} collective-permute-done((bf16[512,256]{1,0:T(8,128)(2,1)S(1)}, bf16[512,256]{1,0:T(8,128)(2,1)S(1)}, u32[]{:S(2)}, u32[]{:S(2)}) %collective-permute-start.8) | collective-permute-done | bytes 262176 | tf_op jit(solution)/shard_map/ppermute | solution.py:24
  41.7 2.0 %collective-permute-start.9 = (bf16[256,256]{1,0:T(8,128)(2,1)S(1)}, bf16[256,256]{1,0:T(8,128)(2,1)S(1)}, u32[]{:S(2)}, u32[]{:S(2)}) collective-permute-start(bf16[256,256]{1,0:T(8,128)(2,1)S(1)} %slice.39), channel_id=1, source_target_pairs={{8,0},{9,1},{10,2},{11,3},{12,4},{13,5},{14,6},{15,7},{0,8},{1,9},... | collective-permute-start | bytes 393224 | tf_op jit(solution)/shard_map/ppermute | solution.py:24
  43.7 3.6 %collective-permute-done.9 = bf16[256,256]{1,0:T(8,128)(2,1)S(1)} collective-permute-done((bf16[256,256]{1,0:T(8,128)(2,1)S(1)}, bf16[256,256]{1,0:T(8,128)(2,1)S(1)}, u32[]{:S(2)}, u32[]{:S(2)}) %collective-permute-start.9) | collective-permute-done | bytes 131104 | tf_op jit(solution)/shard_map/ppermute | solution.py:24
  47.3 1.5 %collective-permute-start.10 = (bf16[256,256]{1,0:T(8,128)(2,1)S(1)}, bf16[256,256]{1,0:T(8,128)(2,1)S(1)}, u32[]{:S(2)}, u32[]{:S(2)}) collective-permute-start(bf16[256,256]{1,0:T(8,128)(2,1)S(1)} %fusion), channel_id=1, source_target_pairs={{16,0},{17,1},{18,2},{19,3},{20,4},{21,5},{22,6},{23,7},{24,8},{25... | collective-permute-start | bytes 393224 | tf_op jit(solution)/shard_map/ppermute | solution.py:24
  48.8 0.1 add_convert_fusion
  48.9 3.5 %collective-permute-start.13 = (bf16[256,768]{1,0:T(8,128)(2,1)S(1)}, bf16[256,768]{1,0:T(8,128)(2,1)S(1)}, u32[]{:S(2)}, u32[]{:S(2)}) collective-permute-start(bf16[256,768]{1,0:T(8,128)(2,1)S(1)} %add_convert_fusion), channel_id=1, source_target_pairs={{0,0},{4,1},{2,2},{6,3},{1,4},{5,5},{3,6},{7,7},{8,8},{12,9},{10,1... | collective-permute-start | bytes 1179656 | tf_op jit(solution)/shard_map/ppermute | solution.py:24
  52.5 3.1 %collective-permute-done.10 = bf16[256,256]{1,0:T(8,128)(2,1)S(1)} collective-permute-done((bf16[256,256]{1,0:T(8,128)(2,1)S(1)}, bf16[256,256]{1,0:T(8,128)(2,1)S(1)}, u32[]{:S(2)}, u32[]{:S(2)}) %collective-permute-start.10) | collective-permute-done | bytes 131104 | tf_op jit(solution)/shard_map/ppermute | solution.py:24
  55.6 3.8 %collective-permute-start.11 = (bf16[256,256]{1,0:T(8,128)(2,1)S(1)}, bf16[256,256]{1,0:T(8,128)(2,1)S(1)}, u32[]{:S(2)}, u32[]{:S(2)}) collective-permute-start(bf16[256,256]{1,0:T(8,128)(2,1)S(1)} %add_convert_fusion.1), channel_id=1, source_target_pairs={{0,0},{4,1},{2,2},{6,3},{1,4},{5,5},{3,6},{7,7},{8,8},{12,9},{10,1... | collective-permute-start | bytes 393224 | tf_op jit(solution)/shard_map/ppermute | solution.py:24
  59.6 1.8 %collective-permute-start.14 = (bf16[256,256]{1,0:T(8,128)(2,1)S(1)}, bf16[256,256]{1,0:T(8,128)(2,1)S(1)}, u32[]{:S(2)}, u32[]{:S(2)}) collective-permute-start(bf16[256,256]{1,0:T(8,128)(2,1)S(1)} %add_convert_fusion.1), channel_id=1, source_target_pairs={{1,0},{5,1},{3,2},{7,3},{0,4},{4,5},{2,6},{6,7},{9,8},{13,9},{11,1... | collective-permute-start | bytes 393224 | tf_op jit(solution)/shard_map/ppermute | solution.py:24
  61.4 1.8 %inverse.1 = (bf16[256,2,256]{2,1,0:T(2,128)(2,1)}, bf16[256,256]{1,0:T(8,128)(2,1)}) custom-call(bf16[256,768]{1,0:T(8,128)(2,1)S(1)} %collective-permute-done.13.y_ref, s32[1]{0:T(128)S(6)} %select_n.27.which_ref.refs_7_, s32[2]{0:T(128)S(1)} %bitcast.48, s32[1]{0:T(128)} %bitcast.35.two_ref), custom_call_target="tpu_custom_call" | custom-call | tf_op jit(solution)/shard_map/inverse/pallas_call | solution.py:209
  63.2 1.0 %collective-permute-done.11.refs_0_ = bf16[256,256]{1,0:T(8,128)(2,1)S(1)} collective-permute-done((bf16[256,256]{1,0:T(8,128)(2,1)S(1)}, bf16[256,256]{1,0:T(8,128)(2,1)S(1)}, u32[]{:S(2)}, u32[]{:S(2)}) %collective-permute-start.11) | collective-permute-done | bytes 131104 | tf_op jit(solution)/shard_map/ppermute | solution.py:24
  64.1 1.0 %collective-permute-done.16.refs_3_ = bf16[256,256]{1,0:T(8,128)(2,1)S(1)} collective-permute-done((bf16[256,256]{1,0:T(8,128)(2,1)S(1)}, bf16[256,256]{1,0:T(8,128)(2,1)S(1)}, u32[]{:S(2)}, u32[]{:S(2)}) %collective-permute-start.16) | collective-permute-done | bytes 131104 | tf_op jit(solution)/shard_map/ppermute | solution.py:24
  65.1 1.2 %collective-permute-done.15.refs_2_ = bf16[256,256]{1,0:T(8,128)(2,1)S(1)} collective-permute-done((bf16[256,256]{1,0:T(8,128)(2,1)S(1)}, bf16[256,256]{1,0:T(8,128)(2,1)S(1)}, u32[]{:S(2)}, u32[]{:S(2)}) %collective-permute-start.15) | collective-permute-done | bytes 131104 | tf_op jit(solution)/shard_map/ppermute | solution.py:24
  66.3 0.8 %collective-permute-done.14.refs_1_ = bf16[256,256]{1,0:T(8,128)(2,1)S(1)} collective-permute-done((bf16[256,256]{1,0:T(8,128)(2,1)S(1)}, bf16[256,256]{1,0:T(8,128)(2,1)S(1)}, u32[]{:S(2)}, u32[]{:S(2)}) %collective-permute-start.14) | collective-permute-done | bytes 131104 | tf_op jit(solution)/shard_map/ppermute | solution.py:24
  67.0 1.3 %finish.1 = (f32[2,256,256]{2,1,0:T(8,128)}, bf16[256,256]{1,0:T(8,128)(2,1)}, f32[256,256]{1,0:T(8,128)}) custom-call(bf16[256,256]{1,0:T(8,128)(2,1)S(1)} %collective-permute-done.11.refs_0_, bf16[256,256]{1,0:T(8,128)(2,1)S(1)} %collective-permute-done.14.refs_1_, bf16[256,256]{1,0:T(8,128)(2,1)S(1)} %collective-permute-done.15.refs_2_, ...), custom_call_target="tpu_custom_call" | custom-call | tf_op jit(solution)/shard_map/finish/pallas_call | solution.py:221
  (32 shorter events, 0.5 us)
Async XLA Ops:
  0.6 5.2 %copy-start.4 = (bf16[1,1,256,2,1,256]{5,3,4,2,1,0:T(2,128)(2,1)S(1)}, bf16[1,1,256,2,1,256]{5,3,4,2,1,0:T(2,128)(2,1)}, u32[]{:S(2)}) copy-start(bf16[1,1,256,2,1,256]{5,3,4,2,1,0:T(2,128)(2,1)} %param.10) | copy-start | bytes 786436
  1.7 13.1 %collective-permute-start = (bf16[2,256,256]{2,1,0:T(8,128)(2,1)S(1)}, bf16[2,256,256]{2,1,0:T(8,128)(2,1)S(1)}, u32[]{:S(2)}, u32[]{:S(2)}) collective-permute-start(bf16[2,256,256]{2,1,0:T(8,128)(2,1)S(1)} %bitcast.40), channel_id=1, source_target_pairs={{4,0},{5,1},{6,2},{7,3},{0,4},{1,5},{2,6},{3,7},{12,8},{13,9},{14,... | collective-permute-start | bytes 786440 | tf_op jit(solution)/shard_map/ppermute | solution.py:24
  5.1 0.7 copy-start.3
  5.9 0.9 %copy-start.5 = (bf16[1,1,256,1,1,256]{5,2,4,3,1,0:T(8,128)(2,1)S(1)}, bf16[1,1,256,1,1,256]{5,2,4,3,1,0:T(8,128)(2,1)}, u32[]{:S(2)}) copy-start(bf16[1,1,256,1,1,256]{5,2,4,3,1,0:T(8,128)(2,1)} %param.11) | copy-start | bytes 393220
  6.8 4.9 %copy-start.1 = (bf16[1,1,256,256]{3,2,1,0:T(8,128)(2,1)S(1)}, bf16[1,1,256,256]{3,2,1,0:T(8,128)(2,1)}, u32[]{:S(2)}) copy-start(bf16[1,1,256,256]{3,2,1,0:T(8,128)(2,1)} %param.12) | copy-start | bytes 393220
  6.9 20.3 %collective-permute-start.4 = (bf16[256,768]{1,0:T(8,128)(2,1)S(1)}, bf16[256,768]{1,0:T(8,128)(2,1)S(1)}, u32[]{:S(2)}, u32[]{:S(2)}) collective-permute-start(bf16[256,768]{1,0:T(8,128)(2,1)S(1)} %pad_maximum_fusion.2), channel_id=1, source_target_pairs={{16,0},{20,1},{18,2},{22,3},{17,4},{21,5},{19,6},{23,7},{24,8},{28... | collective-permute-start | bytes 1179656 | tf_op jit(solution)/shard_map/ppermute | solution.py:24
  10.0 18.6 %collective-permute-start.3 = (bf16[256,768]{1,0:T(8,128)(2,1)S(1)}, bf16[256,768]{1,0:T(8,128)(2,1)S(1)}, u32[]{:S(2)}, u32[]{:S(2)}) collective-permute-start(bf16[256,768]{1,0:T(8,128)(2,1)S(1)} %pad_maximum_fusion.2), channel_id=1, source_target_pairs={{8,0},{12,1},{10,2},{14,3},{9,4},{13,5},{11,6},{15,7},{0,8},{4,9},... | collective-permute-start | bytes 1179656 | tf_op jit(solution)/shard_map/ppermute | solution.py:24
  11.8 24.8 %collective-permute-start.2 = (bf16[256,1024]{1,0:T(8,128)(2,1)S(1)}, bf16[256,1024]{1,0:T(8,128)(2,1)S(1)}, u32[]{:S(2)}, u32[]{:S(2)}) collective-permute-start(bf16[256,1024]{1,0:T(8,128)(2,1)S(1)} %pad_maximum_fusion.1), channel_id=1, source_target_pairs={{0,0},{4,1},{2,2},{6,3},{1,4},{5,5},{3,6},{7,7},{8,8},{12,9},{10,1... | collective-permute-start | bytes 1572872 | tf_op jit(solution)/shard_map/ppermute | solution.py:24
  14.8 22.0 %collective-permute-start.1 = (bf16[2,2,256,256]{3,2,1,0:T(8,128)(2,1)S(1)}, bf16[2,2,256,256]{3,2,1,0:T(8,128)(2,1)S(1)}, u32[]{:S(2)}, u32[]{:S(2)}) collective-permute-start(bf16[2,2,256,256]{3,2,1,0:T(8,128)(2,1)S(1)} %pad_maximum_fusion), channel_id=1, source_target_pairs={{2,0},{3,1},{0,2},{1,3},{6,4},{7,5},{4,6},{5,7},{10,8},{11,9},{8,1... | collective-permute-start | bytes 1572872 | tf_op jit(solution)/shard_map/ppermute | solution.py:24
  16.1 14.6 %collective-permute-start.7 = (bf16[256,768]{1,0:T(8,128)(2,1)S(1)}, bf16[256,768]{1,0:T(8,128)(2,1)S(1)}, u32[]{:S(2)}, u32[]{:S(2)}) collective-permute-start(bf16[256,768]{1,0:T(8,128)(2,1)S(1)} %pad_maximum_fusion.2), channel_id=1, source_target_pairs={{4,0},{0,1},{6,2},{2,3},{5,4},{1,5},{7,6},{3,7},{12,8},{8,9},{14,1... | collective-permute-start | bytes 1179656 | tf_op jit(solution)/shard_map/ppermute | solution.py:24
  27.2 9.6 %collective-permute-start.5 = (bf16[256,512]{1,0:T(8,128)(2,1)S(1)}, bf16[256,512]{1,0:T(8,128)(2,1)S(1)}, u32[]{:S(2)}, u32[]{:S(2)}) collective-permute-start(bf16[256,512]{1,0:T(8,128)(2,1)S(1)} %slice.27), channel_id=1, source_target_pairs={{8,0},{9,1},{10,2},{11,3},{12,4},{13,5},{14,6},{15,7},{0,8},{1,9},... | collective-permute-start | bytes 786440 | tf_op jit(solution)/shard_map/ppermute | solution.py:24
  28.6 8.0 %collective-permute-start.6 = (bf16[256,256]{1,0:T(8,128)(2,1)S(1)}, bf16[256,256]{1,0:T(8,128)(2,1)S(1)}, u32[]{:S(2)}, u32[]{:S(2)}) collective-permute-start(bf16[256,256]{1,0:T(8,128)(2,1)S(1)} %slice.28), channel_id=1, source_target_pairs={{16,0},{17,1},{18,2},{19,3},{20,4},{21,5},{22,6},{23,7},{24,8},{25... | collective-permute-start | bytes 393224 | tf_op jit(solution)/shard_map/ppermute | solution.py:24
  38.4 3.2 %collective-permute-start.8 = (bf16[512,256]{1,0:T(8,128)(2,1)S(1)}, bf16[512,256]{1,0:T(8,128)(2,1)S(1)}, u32[]{:S(2)}, u32[]{:S(2)}) collective-permute-start(bf16[512,256]{1,0:T(8,128)(2,1)S(1)} %get-tuple-element.18), channel_id=1, source_target_pairs={{1,0},{0,1},{3,2},{2,3},{5,4},{4,5},{7,6},{6,7},{9,8},{8,9},{11,10... | collective-permute-start | bytes 786440 | tf_op jit(solution)/shard_map/ppermute | solution.py:24
  40.4 8.4 %collective-permute-start.12 = (f32[256,768]{1,0:T(8,128)S(1)}, f32[256,768]{1,0:T(8,128)S(1)}, u32[]{:S(2)}, u32[]{:S(2)}) collective-permute-start(f32[256,768]{1,0:T(8,128)S(1)} %get-tuple-element.20), channel_id=1, source_target_pairs={{1,0},{0,1},{3,2},{2,3},{5,4},{4,5},{7,6},{6,7},{9,8},{8,9},{11,10... | collective-permute-start | bytes 2359304 | tf_op jit(solution)/shard_map/ppermute | solution.py:24
  41.7 5.6 %collective-permute-start.9 = (bf16[256,256]{1,0:T(8,128)(2,1)S(1)}, bf16[256,256]{1,0:T(8,128)(2,1)S(1)}, u32[]{:S(2)}, u32[]{:S(2)}) collective-permute-start(bf16[256,256]{1,0:T(8,128)(2,1)S(1)} %slice.39), channel_id=1, source_target_pairs={{8,0},{9,1},{10,2},{11,3},{12,4},{13,5},{14,6},{15,7},{0,8},{1,9},... | collective-permute-start | bytes 393224 | tf_op jit(solution)/shard_map/ppermute | solution.py:24
  47.3 8.3 %collective-permute-start.10 = (bf16[256,256]{1,0:T(8,128)(2,1)S(1)}, bf16[256,256]{1,0:T(8,128)(2,1)S(1)}, u32[]{:S(2)}, u32[]{:S(2)}) collective-permute-start(bf16[256,256]{1,0:T(8,128)(2,1)S(1)} %fusion), channel_id=1, source_target_pairs={{16,0},{17,1},{18,2},{19,3},{20,4},{21,5},{22,6},{23,7},{24,8},{25... | collective-permute-start | bytes 393224 | tf_op jit(solution)/shard_map/ppermute | solution.py:24
  48.9 18.1 %copy-start = (f32[2,1,256,256]{3,2,1,0:T(8,128)S(1)}, f32[2,1,256,256]{3,2,1,0:T(8,128)}, u32[]{:S(2)}) copy-start(f32[2,1,256,256]{3,2,1,0:T(8,128)} %param.13) | copy-start | bytes 1572868
  48.9 12.4 %collective-permute-start.13 = (bf16[256,768]{1,0:T(8,128)(2,1)S(1)}, bf16[256,768]{1,0:T(8,128)(2,1)S(1)}, u32[]{:S(2)}, u32[]{:S(2)}) collective-permute-start(bf16[256,768]{1,0:T(8,128)(2,1)S(1)} %add_convert_fusion), channel_id=1, source_target_pairs={{0,0},{4,1},{2,2},{6,3},{1,4},{5,5},{3,6},{7,7},{8,8},{12,9},{10,1... | collective-permute-start | bytes 1179656 | tf_op jit(solution)/shard_map/ppermute | solution.py:24
  55.6 11.4 %copy-start.2 = (f32[1,1,256,256]{3,2,1,0:T(8,128)S(1)}, f32[1,1,256,256]{3,2,1,0:T(8,128)}, u32[]{:S(2)}) copy-start(f32[1,1,256,256]{3,2,1,0:T(8,128)} %param.14) | copy-start | bytes 786436
  55.6 8.5 %collective-permute-start.11 = (bf16[256,256]{1,0:T(8,128)(2,1)S(1)}, bf16[256,256]{1,0:T(8,128)(2,1)S(1)}, u32[]{:S(2)}, u32[]{:S(2)}) collective-permute-start(bf16[256,256]{1,0:T(8,128)(2,1)S(1)} %add_convert_fusion.1), channel_id=1, source_target_pairs={{0,0},{4,1},{2,2},{6,3},{1,4},{5,5},{3,6},{7,7},{8,8},{12,9},{10,1... | collective-permute-start | bytes 393224 | tf_op jit(solution)/shard_map/ppermute | solution.py:24
  59.4 5.7 %collective-permute-start.16 = (bf16[256,256]{1,0:T(8,128)(2,1)S(1)}, bf16[256,256]{1,0:T(8,128)(2,1)S(1)}, u32[]{:S(2)}, u32[]{:S(2)}) collective-permute-start(bf16[256,256]{1,0:T(8,128)(2,1)S(1)} %add_convert_fusion.1), channel_id=1, source_target_pairs={{9,0},{13,1},{11,2},{15,3},{8,4},{12,5},{10,6},{14,7},{1,8},{5,9},... | collective-permute-start | bytes 393224 | tf_op jit(solution)/shard_map/ppermute | solution.py:24
  59.5 6.8 %collective-permute-start.15 = (bf16[256,256]{1,0:T(8,128)(2,1)S(1)}, bf16[256,256]{1,0:T(8,128)(2,1)S(1)}, u32[]{:S(2)}, u32[]{:S(2)}) collective-permute-start(bf16[256,256]{1,0:T(8,128)(2,1)S(1)} %add_convert_fusion.1), channel_id=1, source_target_pairs={{8,0},{12,1},{10,2},{14,3},{9,4},{13,5},{11,6},{15,7},{0,8},{4,9},... | collective-permute-start | bytes 393224 | tf_op jit(solution)/shard_map/ppermute | solution.py:24
  59.6 7.4 %collective-permute-start.14 = (bf16[256,256]{1,0:T(8,128)(2,1)S(1)}, bf16[256,256]{1,0:T(8,128)(2,1)S(1)}, u32[]{:S(2)}, u32[]{:S(2)}) collective-permute-start(bf16[256,256]{1,0:T(8,128)(2,1)S(1)} %add_convert_fusion.1), channel_id=1, source_target_pairs={{1,0},{5,1},{3,2},{7,3},{0,4},{4,5},{2,6},{6,7},{9,8},{13,9},{11,1... | collective-permute-start | bytes 393224 | tf_op jit(solution)/shard_map/ppermute | solution.py:24

commit v6 on v5

--- a/solution.py
+++ b/solution.py
@@ -27,6 +27,10 @@
 def place():
     row, col = lax.axis_index("row"), lax.axis_index("col")
     return row // 2, row % 2, col // 2, col % 2
+
+
+def copy_kernel(source_ref, out_ref):
+    out_ref[...] = source_ref[...]
 
 
 def tdot(left, right):
@@ -154,6 +158,17 @@
     def along(value, d):
         return send(value, sizes, lambda z, y, x, k: (z ^ d, y, x, k))
 
+    def staged(value, flops):
+        return pl.pallas_call(
+            copy_kernel,
+            out_shape=jax.ShapeDtypeStruct(value.shape, value.dtype),
+            cost_estimate=pl.CostEstimate(
+                flops=flops, bytes_accessed=4 * value.size, transcendentals=0
+            ),
+            compiler_params=pltpu.CompilerParams(vmem_limit_bytes=4 * 1024 * 1024),
+            name="stage",
+        )(value)
+
     pieces = {d: across(cols, d) for d in [*range(2, high, 2), 1]}
     own = across(jnp.concatenate([cols, coupling], axis=1), 0)
     now = anc
@@ -162,7 +177,7 @@
     far_anc = [plane(stacked, 0, dx) for dx in range(1, wide)]
     for d in range(3, high, 2):
         pieces[d] = (
-            along(pieces[d - 1][:, : 2 * block], 1),
+            staged(along(pieces[d - 1][:, : 2 * block], 1), 2*10**9),
             along(pieces[1][:, 2 * block :], d - 1),
         )
     cols_now = cols

time: 68.6 us -> 67.6 us (0.985)
  waiting for transfers between devices: 28.7 us -> 27.8 us
  local copies, waits for them, and re-layouts: 2.6 us -> 1.74 us
  starting transfers between devices: 29.7 us -> 30.5 us
    ppermute x17, waiting for transfers between devices: 28.7 us -> 27.8 us  [send(): return lax.ppermute(value, AXES, pairs)]
    unnamed x13, local copies, waits for them, and re-layouts: 2.56 us -> 1.7 us
    ppermute x17, starting transfers between devices: 29.7 us -> 30.5 us  [send(): return lax.ppermute(value, AXES, pairs)]
  transfers between devices with their start and end apart: 17 -> 17, of which waited for: 10 -> 8; matrix products, arithmetic and copies ran while one was open for 1% -> 1% of each run, Pallas kernels for 3% -> 3%
where the time goes in v6:
time: 67.6 us; the launch traced here: 67.4 us
  starting transfers between devices  30.5 us (45%)
  waiting for transfers between devices  27.8 us (41%)
  Pallas kernels  4.73 us (7%)
  between operations  2.18 us (3%)
  local copies, waits for them, and re-layouts  1.74 us (3%)
    ppermute x17, starting transfers between devices, send(): return lax.ppermute(value, AXES, pairs)  30.5 us
    ppermute x17, waiting for transfers between devices, send(): return lax.ppermute(value, AXES, pairs)  27.8 us
    pallas_call x1, Pallas kernels, body(): pl.pallas_call(inverse_kernel, out_shape=(jax.ShapeDtypeStruct((block, 2,...  1.81 us
    unnamed x13, local copies, waits for them, and re-layouts  1.7 us
    pallas_call x1, Pallas kernels, body(): pl.pallas_call(functools.partial(product_kernel, high, wide), out_shape=(...  1.58 us
  transfers between devices with their start and end apart: 17, of which 8 were waited for; matrix products, arithmetic and copies ran while one was open for 1% of the time, Pallas kernels for 3%

profile of v6, /device:TPU:1, one launch (start us, length us, event | category | flops | bytes accessed | tf_op | source)
XLA Modules:
  0.0 67.4 jit_solution(17252345099305607647)
XLA Ops:
  0.7 1.0 %copy.21 = bf16[1,1,256,2,1,256]{5,2,3,4,1,0:T(8,128)(2,1)S(1)} copy(bf16[1,1,256,2,1,256]{5,3,4,2,1,0:T(2,128)(2,1)} %param.9) | data formatting | bytes 524288 | tf_op args[0]
  1.7 2.1 %collective-permute-start = (bf16[2,256,256]{2,1,0:T(8,128)(2,1)S(1)}, bf16[2,256,256]{2,1,0:T(8,128)(2,1)S(1)}, u32[]{:S(2)}, u32[]{:S(2)}) collective-permute-start(bf16[2,256,256]{2,1,0:T(8,128)(2,1)S(1)} %bitcast.40), channel_id=1, source_target_pairs={{4,0},{5,1},{6,2},{7,3},{0,4},{1,5},{2,6},{3,7},{12,8},{13,9},{14,... | collective-permute-start | bytes 786440 | tf_op jit(solution)/shard_map/ppermute | solution.py:24
  5.2 0.6 copy-done.3
  5.8 0.1 bitcast_select_fusion
  6.0 3.2 %collective-permute-start.4 = (bf16[256,768]{1,0:T(8,128)(2,1)S(1)}, bf16[256,768]{1,0:T(8,128)(2,1)S(1)}, u32[]{:S(2)}, u32[]{:S(2)}) collective-permute-start(bf16[256,768]{1,0:T(8,128)(2,1)S(1)} %pad_maximum_fusion.2), channel_id=1, source_target_pairs={{16,0},{20,1},{18,2},{22,3},{17,4},{21,5},{19,6},{23,7},{24,8},{28... | collective-permute-start | bytes 1179656 | tf_op jit(solution)/shard_map/ppermute | solution.py:24
  9.2 1.7 %collective-permute-start.3 = (bf16[256,768]{1,0:T(8,128)(2,1)S(1)}, bf16[256,768]{1,0:T(8,128)(2,1)S(1)}, u32[]{:S(2)}, u32[]{:S(2)}) collective-permute-start(bf16[256,768]{1,0:T(8,128)(2,1)S(1)} %pad_maximum_fusion.2), channel_id=1, source_target_pairs={{8,0},{12,1},{10,2},{14,3},{9,4},{13,5},{11,6},{15,7},{0,8},{4,9},... | collective-permute-start | bytes 1179656 | tf_op jit(solution)/shard_map/ppermute | solution.py:24
  10.9 3.0 %collective-permute-start.2 = (bf16[256,1024]{1,0:T(8,128)(2,1)S(1)}, bf16[256,1024]{1,0:T(8,128)(2,1)S(1)}, u32[]{:S(2)}, u32[]{:S(2)}) collective-permute-start(bf16[256,1024]{1,0:T(8,128)(2,1)S(1)} %pad_maximum_fusion.1), channel_id=1, source_target_pairs={{0,0},{4,1},{2,2},{6,3},{1,4},{5,5},{3,6},{7,7},{8,8},{12,9},{10,1... | collective-permute-start | bytes 1572872 | tf_op jit(solution)/shard_map/ppermute | solution.py:24
  14.0 1.3 %collective-permute-start.1 = (bf16[2,2,256,256]{3,2,1,0:T(8,128)(2,1)S(1)}, bf16[2,2,256,256]{3,2,1,0:T(8,128)(2,1)S(1)}, u32[]{:S(2)}, u32[]{:S(2)}) collective-permute-start(bf16[2,2,256,256]{3,2,1,0:T(8,128)(2,1)S(1)} %pad_maximum_fusion), channel_id=1, source_target_pairs={{2,0},{3,1},{0,2},{1,3},{6,4},{7,5},{4,6},{5,7},{10,8},{11,9},{8,1... | collective-permute-start | bytes 1572872 | tf_op jit(solution)/shard_map/ppermute | solution.py:24
  15.3 11.0 %collective-permute-done.4.refs_5_ = bf16[256,768]{1,0:T(8,128)(2,1)S(1)} collective-permute-done((bf16[256,768]{1,0:T(8,128)(2,1)S(1)}, bf16[256,768]{1,0:T(8,128)(2,1)S(1)}, u32[]{:S(2)}, u32[]{:S(2)}) %collective-permute-start.4) | collective-permute-done | bytes 393248 | tf_op jit(solution)/shard_map/ppermute | solution.py:24
  26.3 1.4 %collective-permute-start.5 = (bf16[256,512]{1,0:T(8,128)(2,1)S(1)}, bf16[256,512]{1,0:T(8,128)(2,1)S(1)}, u32[]{:S(2)}, u32[]{:S(2)}) collective-permute-start(bf16[256,512]{1,0:T(8,128)(2,1)S(1)} %slice.27), channel_id=1, source_target_pairs={{8,0},{9,1},{10,2},{11,3},{12,4},{13,5},{14,6},{15,7},{0,8},{1,9},... | collective-permute-start | bytes 786440 | tf_op jit(solution)/shard_map/ppermute | solution.py:24
  27.8 2.6 %collective-permute-start.6 = (bf16[256,256]{1,0:T(8,128)(2,1)S(1)}, bf16[256,256]{1,0:T(8,128)(2,1)S(1)}, u32[]{:S(2)}, u32[]{:S(2)}) collective-permute-start(bf16[256,256]{1,0:T(8,128)(2,1)S(1)} %slice.28), channel_id=1, source_target_pairs={{16,0},{17,1},{18,2},{19,3},{20,4},{21,5},{22,6},{23,7},{24,8},{25... | collective-permute-start | bytes 393224 | tf_op jit(solution)/shard_map/ppermute | solution.py:24
  30.3 5.6 %collective-permute-done.5.source_ref = bf16[256,512]{1,0:T(8,128)(2,1)S(1)} collective-permute-done((bf16[256,512]{1,0:T(8,128)(2,1)S(1)}, bf16[256,512]{1,0:T(8,128)(2,1)S(1)}, u32[]{:S(2)}, u32[]{:S(2)}) %collective-permute-start.5) | collective-permute-done | bytes 262176 | tf_op jit(solution)/shard_map/ppermute | solution.py:24
  36.0 1.6 %products.1 = (f32[256,768]{1,0:T(8,128)S(1)}, f32[256,768]{1,0:T(8,128)S(1)}, f32[512,256]{1,0:T(8,128)S(1)}, bf16[512,256]{1,0:T(8,128)(2,1)S(1)}) custom-call(bf16[2,256,256]{2,1,0:T(8,128)(2,1)S(1)} %bitcast.42, bf16[2,256,256]{2,1,0:T(8,128)(2,1)S(1)} %collective-permute-done.refs_1_, bf16[2,2,256,256]{3,2,1,0:T(8,128)(2,1)S(1)} %collective-permute-done.1.refs_2_, ...), custom_call_target="tpu_custom_call" | custom-call | tf_op jit(solution)/shard_map/products/pallas_call | solution.py:187
  37.6 2.0 %collective-permute-start.8 = (bf16[512,256]{1,0:T(8,128)(2,1)S(1)}, bf16[512,256]{1,0:T(8,128)(2,1)S(1)}, u32[]{:S(2)}, u32[]{:S(2)}) collective-permute-start(bf16[512,256]{1,0:T(8,128)(2,1)S(1)} %get-tuple-element.18), channel_id=1, source_target_pairs={{1,0},{0,1},{3,2},{2,3},{5,4},{4,5},{7,6},{6,7},{9,8},{8,9},{11,10... | collective-permute-start | bytes 786440 | tf_op jit(solution)/shard_map/ppermute | solution.py:24
  39.6 0.1 collective-permute-start.12
  39.7 1.1 %collective-permute-done.8 = bf16[512,256]{1,0:T(8,128)(2,1)S(1)} collective-permute-done((bf16[512,256]{1,0:T(8,128)(2,1)S(1)}, bf16[512,256]{1,0:T(8,128)(2,1)S(1)}, u32[]{:S(2)}, u32[]{:S(2)}) %collective-permute-start.8) | collective-permute-done | bytes 262176 | tf_op jit(solution)/shard_map/ppermute | solution.py:24
  40.8 0.1 convert_add_fusion
  40.9 1.9 %collective-permute-start.9 = (bf16[256,256]{1,0:T(8,128)(2,1)S(1)}, bf16[256,256]{1,0:T(8,128)(2,1)S(1)}, u32[]{:S(2)}, u32[]{:S(2)}) collective-permute-start(bf16[256,256]{1,0:T(8,128)(2,1)S(1)} %slice.39), channel_id=1, source_target_pairs={{8,0},{9,1},{10,2},{11,3},{12,4},{13,5},{14,6},{15,7},{0,8},{1,9},... | collective-permute-start | bytes 393224 | tf_op jit(solution)/shard_map/ppermute | solution.py:24
  42.8 3.6 %collective-permute-done.9 = bf16[256,256]{1,0:T(8,128)(2,1)S(1)} collective-permute-done((bf16[256,256]{1,0:T(8,128)(2,1)S(1)}, bf16[256,256]{1,0:T(8,128)(2,1)S(1)}, u32[]{:S(2)}, u32[]{:S(2)}) %collective-permute-start.9) | collective-permute-done | bytes 131104 | tf_op jit(solution)/shard_map/ppermute | solution.py:24
  46.4 1.5 %collective-permute-start.10 = (bf16[256,256]{1,0:T(8,128)(2,1)S(1)}, bf16[256,256]{1,0:T(8,128)(2,1)S(1)}, u32[]{:S(2)}, u32[]{:S(2)}) collective-permute-start(bf16[256,256]{1,0:T(8,128)(2,1)S(1)} %fusion), channel_id=1, source_target_pairs={{16,0},{17,1},{18,2},{19,3},{20,4},{21,5},{22,6},{23,7},{24,8},{25... | collective-permute-start | bytes 393224 | tf_op jit(solution)/shard_map/ppermute | solution.py:24
  48.0 0.1 add_convert_fusion
  48.1 4.0 %collective-permute-start.13 = (bf16[256,768]{1,0:T(8,128)(2,1)S(1)}, bf16[256,768]{1,0:T(8,128)(2,1)S(1)}, u32[]{:S(2)}, u32[]{:S(2)}) collective-permute-start(bf16[256,768]{1,0:T(8,128)(2,1)S(1)} %add_convert_fusion), channel_id=1, source_target_pairs={{0,0},{4,1},{2,2},{6,3},{1,4},{5,5},{3,6},{7,7},{8,8},{12,9},{10,1... | collective-permute-start | bytes 1179656 | tf_op jit(solution)/shard_map/ppermute | solution.py:24
  52.0 2.7 %collective-permute-done.10 = bf16[256,256]{1,0:T(8,128)(2,1)S(1)} collective-permute-done((bf16[256,256]{1,0:T(8,128)(2,1)S(1)}, bf16[256,256]{1,0:T(8,128)(2,1)S(1)}, u32[]{:S(2)}, u32[]{:S(2)}) %collective-permute-start.10) | collective-permute-done | bytes 131104 | tf_op jit(solution)/shard_map/ppermute | solution.py:24
  54.8 3.7 %collective-permute-start.11 = (bf16[256,256]{1,0:T(8,128)(2,1)S(1)}, bf16[256,256]{1,0:T(8,128)(2,1)S(1)}, u32[]{:S(2)}, u32[]{:S(2)}) collective-permute-start(bf16[256,256]{1,0:T(8,128)(2,1)S(1)} %add_convert_fusion.1), channel_id=1, source_target_pairs={{0,0},{4,1},{2,2},{6,3},{1,4},{5,5},{3,6},{7,7},{8,8},{12,9},{10,1... | collective-permute-start | bytes 393224 | tf_op jit(solution)/shard_map/ppermute | solution.py:24
  58.5 0.1 collective-permute-start.16
  58.6 0.1 collective-permute-start.15
  58.7 1.8 %collective-permute-start.14 = (bf16[256,256]{1,0:T(8,128)(2,1)S(1)}, bf16[256,256]{1,0:T(8,128)(2,1)S(1)}, u32[]{:S(2)}, u32[]{:S(2)}) collective-permute-start(bf16[256,256]{1,0:T(8,128)(2,1)S(1)} %add_convert_fusion.1), channel_id=1, source_target_pairs={{1,0},{5,1},{3,2},{7,3},{0,4},{4,5},{2,6},{6,7},{9,8},{13,9},{11,1... | collective-permute-start | bytes 393224 | tf_op jit(solution)/shard_map/ppermute | solution.py:24
  60.5 1.8 %inverse.1 = (bf16[256,2,256]{2,1,0:T(2,128)(2,1)}, bf16[256,256]{1,0:T(8,128)(2,1)}) custom-call(bf16[256,768]{1,0:T(8,128)(2,1)S(1)} %collective-permute-done.13.y_ref, s32[1]{0:T(128)S(6)} %select_n.27.which_ref.refs_7_, s32[2]{0:T(128)S(1)} %bitcast.48, s32[1]{0:T(128)} %bitcast.35.two_ref), custom_call_target="tpu_custom_call" | custom-call | tf_op jit(solution)/shard_map/inverse/pallas_call | solution.py:224
  62.3 1.9 %collective-permute-done.16.refs_3_ = bf16[256,256]{1,0:T(8,128)(2,1)S(1)} collective-permute-done((bf16[256,256]{1,0:T(8,128)(2,1)S(1)}, bf16[256,256]{1,0:T(8,128)(2,1)S(1)}, u32[]{:S(2)}, u32[]{:S(2)}) %collective-permute-start.16) | collective-permute-done | bytes 131104 | tf_op jit(solution)/shard_map/ppermute | solution.py:24
  64.2 1.2 %collective-permute-done.15.refs_2_ = bf16[256,256]{1,0:T(8,128)(2,1)S(1)} collective-permute-done((bf16[256,256]{1,0:T(8,128)(2,1)S(1)}, bf16[256,256]{1,0:T(8,128)(2,1)S(1)}, u32[]{:S(2)}, u32[]{:S(2)}) %collective-permute-start.15) | collective-permute-done | bytes 131104 | tf_op jit(solution)/shard_map/ppermute | solution.py:24
  65.3 0.8 %collective-permute-done.14.refs_1_ = bf16[256,256]{1,0:T(8,128)(2,1)S(1)} collective-permute-done((bf16[256,256]{1,0:T(8,128)(2,1)S(1)}, bf16[256,256]{1,0:T(8,128)(2,1)S(1)}, u32[]{:S(2)}, u32[]{:S(2)}) %collective-permute-start.14) | collective-permute-done | bytes 131104 | tf_op jit(solution)/shard_map/ppermute | solution.py:24
  66.1 1.3 %finish.1 = (f32[2,256,256]{2,1,0:T(8,128)}, bf16[256,256]{1,0:T(8,128)(2,1)}, f32[256,256]{1,0:T(8,128)}) custom-call(bf16[256,256]{1,0:T(8,128)(2,1)S(1)} %collective-permute-done.11.refs_0_, bf16[256,256]{1,0:T(8,128)(2,1)S(1)} %collective-permute-done.14.refs_1_, bf16[256,256]{1,0:T(8,128)(2,1)S(1)} %collective-permute-done.15.refs_2_, ...), custom_call_target="tpu_custom_call" | custom-call | tf_op jit(solution)/shard_map/finish/pallas_call | solution.py:236
  (33 shorter events, 0.4 us)
Async XLA Ops:
  0.6 5.2 %copy-start.5 = (bf16[1,1,256,1,1,256]{5,2,4,3,1,0:T(8,128)(2,1)S(1)}, bf16[1,1,256,1,1,256]{5,2,4,3,1,0:T(8,128)(2,1)}, u32[]{:S(2)}) copy-start(bf16[1,1,256,1,1,256]{5,2,4,3,1,0:T(8,128)(2,1)} %param.11) | copy-start | bytes 393220
  0.6 5.2 %copy-start.4 = (bf16[1,1,256,2,1,256]{5,3,4,2,1,0:T(2,128)(2,1)S(1)}, bf16[1,1,256,2,1,256]{5,3,4,2,1,0:T(2,128)(2,1)}, u32[]{:S(2)}) copy-start(bf16[1,1,256,2,1,256]{5,3,4,2,1,0:T(2,128)(2,1)} %param.10) | copy-start | bytes 786436
  1.7 12.2 %collective-permute-start = (bf16[2,256,256]{2,1,0:T(8,128)(2,1)S(1)}, bf16[2,256,256]{2,1,0:T(8,128)(2,1)S(1)}, u32[]{:S(2)}, u32[]{:S(2)}) collective-permute-start(bf16[2,256,256]{2,1,0:T(8,128)(2,1)S(1)} %bitcast.40), channel_id=1, source_target_pairs={{4,0},{5,1},{6,2},{7,3},{0,4},{1,5},{2,6},{3,7},{12,8},{13,9},{14,... | collective-permute-start | bytes 786440 | tf_op jit(solution)/shard_map/ppermute | solution.py:24
  5.1 0.7 copy-start.3
  6.0 4.9 %copy-start.1 = (bf16[1,1,256,256]{3,2,1,0:T(8,128)(2,1)S(1)}, bf16[1,1,256,256]{3,2,1,0:T(8,128)(2,1)}, u32[]{:S(2)}) copy-start(bf16[1,1,256,256]{3,2,1,0:T(8,128)(2,1)} %param.12) | copy-start | bytes 393220
  6.0 20.3 %collective-permute-start.4 = (bf16[256,768]{1,0:T(8,128)(2,1)S(1)}, bf16[256,768]{1,0:T(8,128)(2,1)S(1)}, u32[]{:S(2)}, u32[]{:S(2)}) collective-permute-start(bf16[256,768]{1,0:T(8,128)(2,1)S(1)} %pad_maximum_fusion.2), channel_id=1, source_target_pairs={{16,0},{20,1},{18,2},{22,3},{17,4},{21,5},{19,6},{23,7},{24,8},{28... | collective-permute-start | bytes 1179656 | tf_op jit(solution)/shard_map/ppermute | solution.py:24
  9.2 18.6 %collective-permute-start.3 = (bf16[256,768]{1,0:T(8,128)(2,1)S(1)}, bf16[256,768]{1,0:T(8,128)(2,1)S(1)}, u32[]{:S(2)}, u32[]{:S(2)}) collective-permute-start(bf16[256,768]{1,0:T(8,128)(2,1)S(1)} %pad_maximum_fusion.2), channel_id=1, source_target_pairs={{8,0},{12,1},{10,2},{14,3},{9,4},{13,5},{11,6},{15,7},{0,8},{4,9},... | collective-permute-start | bytes 1179656 | tf_op jit(solution)/shard_map/ppermute | solution.py:24
  10.9 25.1 %collective-permute-start.2 = (bf16[256,1024]{1,0:T(8,128)(2,1)S(1)}, bf16[256,1024]{1,0:T(8,128)(2,1)S(1)}, u32[]{:S(2)}, u32[]{:S(2)}) collective-permute-start(bf16[256,1024]{1,0:T(8,128)(2,1)S(1)} %pad_maximum_fusion.1), channel_id=1, source_target_pairs={{0,0},{4,1},{2,2},{6,3},{1,4},{5,5},{3,6},{7,7},{8,8},{12,9},{10,1... | collective-permute-start | bytes 1572872 | tf_op jit(solution)/shard_map/ppermute | solution.py:24
  14.0 22.0 %collective-permute-start.1 = (bf16[2,2,256,256]{3,2,1,0:T(8,128)(2,1)S(1)}, bf16[2,2,256,256]{3,2,1,0:T(8,128)(2,1)S(1)}, u32[]{:S(2)}, u32[]{:S(2)}) collective-permute-start(bf16[2,2,256,256]{3,2,1,0:T(8,128)(2,1)S(1)} %pad_maximum_fusion), channel_id=1, source_target_pairs={{2,0},{3,1},{0,2},{1,3},{6,4},{7,5},{4,6},{5,7},{10,8},{11,9},{8,1... | collective-permute-start | bytes 1572872 | tf_op jit(solution)/shard_map/ppermute | solution.py:24
  26.3 9.6 %collective-permute-start.5 = (bf16[256,512]{1,0:T(8,128)(2,1)S(1)}, bf16[256,512]{1,0:T(8,128)(2,1)S(1)}, u32[]{:S(2)}, u32[]{:S(2)}) collective-permute-start(bf16[256,512]{1,0:T(8,128)(2,1)S(1)} %slice.27), channel_id=1, source_target_pairs={{8,0},{9,1},{10,2},{11,3},{12,4},{13,5},{14,6},{15,7},{0,8},{1,9},... | collective-permute-start | bytes 786440 | tf_op jit(solution)/shard_map/ppermute | solution.py:24
  27.7 8.2 %collective-permute-start.7 = (bf16[256,768]{1,0:T(8,128)(2,1)S(1)}, bf16[256,768]{1,0:T(8,128)(2,1)S(1)}, u32[]{:S(2)}, u32[]{:S(2)}) collective-permute-start(bf16[256,768]{1,0:T(8,128)(2,1)S(1)} %pad_maximum_fusion.2), channel_id=1, source_target_pairs={{4,0},{0,1},{6,2},{2,3},{5,4},{1,5},{7,6},{3,7},{12,8},{8,9},{14,1... | collective-permute-start | bytes 1179656 | tf_op jit(solution)/shard_map/ppermute | solution.py:24
  27.8 8.2 %collective-permute-start.6 = (bf16[256,256]{1,0:T(8,128)(2,1)S(1)}, bf16[256,256]{1,0:T(8,128)(2,1)S(1)}, u32[]{:S(2)}, u32[]{:S(2)}) collective-permute-start(bf16[256,256]{1,0:T(8,128)(2,1)S(1)} %slice.28), channel_id=1, source_target_pairs={{16,0},{17,1},{18,2},{19,3},{20,4},{21,5},{22,6},{23,7},{24,8},{25... | collective-permute-start | bytes 393224 | tf_op jit(solution)/shard_map/ppermute | solution.py:24
  37.6 3.2 %collective-permute-start.8 = (bf16[512,256]{1,0:T(8,128)(2,1)S(1)}, bf16[512,256]{1,0:T(8,128)(2,1)S(1)}, u32[]{:S(2)}, u32[]{:S(2)}) collective-permute-start(bf16[512,256]{1,0:T(8,128)(2,1)S(1)} %get-tuple-element.18), channel_id=1, source_target_pairs={{1,0},{0,1},{3,2},{2,3},{5,4},{4,5},{7,6},{6,7},{9,8},{8,9},{11,10... | collective-permute-start | bytes 786440 | tf_op jit(solution)/shard_map/ppermute | solution.py:24
  39.6 8.3 %collective-permute-start.12 = (f32[256,768]{1,0:T(8,128)S(1)}, f32[256,768]{1,0:T(8,128)S(1)}, u32[]{:S(2)}, u32[]{:S(2)}) collective-permute-start(f32[256,768]{1,0:T(8,128)S(1)} %get-tuple-element.20), channel_id=1, source_target_pairs={{1,0},{0,1},{3,2},{2,3},{5,4},{4,5},{7,6},{6,7},{9,8},{8,9},{11,10... | collective-permute-start | bytes 2359304 | tf_op jit(solution)/shard_map/ppermute | solution.py:24
  40.9 5.5 %collective-permute-start.9 = (bf16[256,256]{1,0:T(8,128)(2,1)S(1)}, bf16[256,256]{1,0:T(8,128)(2,1)S(1)}, u32[]{:S(2)}, u32[]{:S(2)}) collective-permute-start(bf16[256,256]{1,0:T(8,128)(2,1)S(1)} %slice.39), channel_id=1, source_target_pairs={{8,0},{9,1},{10,2},{11,3},{12,4},{13,5},{14,6},{15,7},{0,8},{1,9},... | collective-permute-start | bytes 393224 | tf_op jit(solution)/shard_map/ppermute | solution.py:24
  46.4 8.3 %collective-permute-start.10 = (bf16[256,256]{1,0:T(8,128)(2,1)S(1)}, bf16[256,256]{1,0:T(8,128)(2,1)S(1)}, u32[]{:S(2)}, u32[]{:S(2)}) collective-permute-start(bf16[256,256]{1,0:T(8,128)(2,1)S(1)} %fusion), channel_id=1, source_target_pairs={{16,0},{17,1},{18,2},{19,3},{20,4},{21,5},{22,6},{23,7},{24,8},{25... | collective-permute-start | bytes 393224 | tf_op jit(solution)/shard_map/ppermute | solution.py:24
  48.1 18.0 %copy-start = (f32[2,1,256,256]{3,2,1,0:T(8,128)S(1)}, f32[2,1,256,256]{3,2,1,0:T(8,128)}, u32[]{:S(2)}) copy-start(f32[2,1,256,256]{3,2,1,0:T(8,128)} %param.13) | copy-start | bytes 1572868
  48.1 12.4 %collective-permute-start.13 = (bf16[256,768]{1,0:T(8,128)(2,1)S(1)}, bf16[256,768]{1,0:T(8,128)(2,1)S(1)}, u32[]{:S(2)}, u32[]{:S(2)}) collective-permute-start(bf16[256,768]{1,0:T(8,128)(2,1)S(1)} %add_convert_fusion), channel_id=1, source_target_pairs={{0,0},{4,1},{2,2},{6,3},{1,4},{5,5},{3,6},{7,7},{8,8},{12,9},{10,1... | collective-permute-start | bytes 1179656 | tf_op jit(solution)/shard_map/ppermute | solution.py:24
  54.7 11.4 %copy-start.2 = (f32[1,1,256,256]{3,2,1,0:T(8,128)S(1)}, f32[1,1,256,256]{3,2,1,0:T(8,128)}, u32[]{:S(2)}) copy-start(f32[1,1,256,256]{3,2,1,0:T(8,128)} %param.14) | copy-start | bytes 786436
  54.8 7.5 %collective-permute-start.11 = (bf16[256,256]{1,0:T(8,128)(2,1)S(1)}, bf16[256,256]{1,0:T(8,128)(2,1)S(1)}, u32[]{:S(2)}, u32[]{:S(2)}) collective-permute-start(bf16[256,256]{1,0:T(8,128)(2,1)S(1)} %add_convert_fusion.1), channel_id=1, source_target_pairs={{0,0},{4,1},{2,2},{6,3},{1,4},{5,5},{3,6},{7,7},{8,8},{12,9},{10,1... | collective-permute-start | bytes 393224 | tf_op jit(solution)/shard_map/ppermute | solution.py:24
  58.5 5.7 %collective-permute-start.16 = (bf16[256,256]{1,0:T(8,128)(2,1)S(1)}, bf16[256,256]{1,0:T(8,128)(2,1)S(1)}, u32[]{:S(2)}, u32[]{:S(2)}) collective-permute-start(bf16[256,256]{1,0:T(8,128)(2,1)S(1)} %add_convert_fusion.1), channel_id=1, source_target_pairs={{9,0},{13,1},{11,2},{15,3},{8,4},{12,5},{10,6},{14,7},{1,8},{5,9},... | collective-permute-start | bytes 393224 | tf_op jit(solution)/shard_map/ppermute | solution.py:24
  58.6 6.8 %collective-permute-start.15 = (bf16[256,256]{1,0:T(8,128)(2,1)S(1)}, bf16[256,256]{1,0:T(8,128)(2,1)S(1)}, u32[]{:S(2)}, u32[]{:S(2)}) collective-permute-start(bf16[256,256]{1,0:T(8,128)(2,1)S(1)} %add_convert_fusion.1), channel_id=1, source_target_pairs={{8,0},{12,1},{10,2},{14,3},{9,4},{13,5},{11,6},{15,7},{0,8},{4,9},... | collective-permute-start | bytes 393224 | tf_op jit(solution)/shard_map/ppermute | solution.py:24
  58.7 7.4 %collective-permute-start.14 = (bf16[256,256]{1,0:T(8,128)(2,1)S(1)}, bf16[256,256]{1,0:T(8,128)(2,1)S(1)}, u32[]{:S(2)}, u32[]{:S(2)}) collective-permute-start(bf16[256,256]{1,0:T(8,128)(2,1)S(1)} %add_convert_fusion.1), channel_id=1, source_target_pairs={{1,0},{5,1},{3,2},{7,3},{0,4},{4,5},{2,6},{6,7},{9,8},{13,9},{11,1... | collective-permute-start | bytes 393224 | tf_op jit(solution)/shard_map/ppermute | solution.py:24

commit v7 on v6

--- a/solution.py
+++ b/solution.py
@@ -94,8 +94,9 @@
     near, far = y_ref[:, :block], y_ref[:, block : 2 * block]
     zero = jnp.where(flip, far, near)
     unit = jnp.where(flip, near, far)
-    out_one[:, 0, :] = jnp.where(one_ref[0] != 0, -zero, jnp.zeros_like(zero))
-    out_one[:, 1, :] = jnp.where(one_ref[1] != 0, -unit, jnp.zeros_like(unit))
+    zero = jnp.where(one_ref[0] != 0, -zero, jnp.zeros_like(zero))
+    unit = jnp.where(one_ref[1] != 0, -unit, jnp.zeros_like(unit))
+    out_one[...] = jnp.stack([zero, unit], axis=1)
     last = y_ref[:, 2 * block :]
     out_two[...] = jnp.where(two_ref[0] != 0, -last, jnp.zeros_like(last))
 

time: 67.6 us -> 67.6 us (level)
  no operation moved by 1% of the time
where the time goes in v7:
time: 67.6 us; the launch traced here: 67.4 us
  starting transfers between devices  30.5 us (45%)
  waiting for transfers between devices  27.9 us (41%)
  Pallas kernels  4.66 us (7%)
  between operations  2.18 us (3%)
  local copies, waits for them, and re-layouts  1.74 us (3%)
    ppermute x17, starting transfers between devices, send(): return lax.ppermute(value, AXES, pairs)  30.5 us
    ppermute x17, waiting for transfers between devices, send(): return lax.ppermute(value, AXES, pairs)  27.9 us
    pallas_call x1, Pallas kernels, body(): pl.pallas_call(inverse_kernel, out_shape=(jax.ShapeDtypeStruct((block, 2,...  1.74 us
    unnamed x13, local copies, waits for them, and re-layouts  1.7 us
    pallas_call x1, Pallas kernels, body(): pl.pallas_call(functools.partial(product_kernel, high, wide), out_shape=(...  1.58 us
  transfers between devices with their start and end apart: 17, of which 8 were waited for; matrix products, arithmetic and copies ran while one was open for 1% of the time, Pallas kernels for 3%

profile of v7, /device:TPU:1, one launch (start us, length us, event | category | flops | bytes accessed | tf_op | source)
XLA Modules:
  0.0 67.4 jit_solution(6384761771839145246)
XLA Ops:
  0.7 1.0 %copy.21 = bf16[1,1,256,2,1,256]{5,2,3,4,1,0:T(8,128)(2,1)S(1)} copy(bf16[1,1,256,2,1,256]{5,3,4,2,1,0:T(2,128)(2,1)} %param.9) | data formatting | bytes 524288 | tf_op args[0]
  1.7 2.1 %collective-permute-start = (bf16[2,256,256]{2,1,0:T(8,128)(2,1)S(1)}, bf16[2,256,256]{2,1,0:T(8,128)(2,1)S(1)}, u32[]{:S(2)}, u32[]{:S(2)}) collective-permute-start(bf16[2,256,256]{2,1,0:T(8,128)(2,1)S(1)} %bitcast.40), channel_id=1, source_target_pairs={{4,0},{5,1},{6,2},{7,3},{0,4},{1,5},{2,6},{3,7},{12,8},{13,9},{14,... | collective-permute-start | bytes 786440 | tf_op jit(solution)/shard_map/ppermute | solution.py:24
  5.2 0.6 copy-done.3
  5.8 0.1 bitcast_select_fusion
  6.0 3.2 %collective-permute-start.4 = (bf16[256,768]{1,0:T(8,128)(2,1)S(1)}, bf16[256,768]{1,0:T(8,128)(2,1)S(1)}, u32[]{:S(2)}, u32[]{:S(2)}) collective-permute-start(bf16[256,768]{1,0:T(8,128)(2,1)S(1)} %pad_maximum_fusion.2), channel_id=1, source_target_pairs={{16,0},{20,1},{18,2},{22,3},{17,4},{21,5},{19,6},{23,7},{24,8},{28... | collective-permute-start | bytes 1179656 | tf_op jit(solution)/shard_map/ppermute | solution.py:24
  9.2 1.7 %collective-permute-start.3 = (bf16[256,768]{1,0:T(8,128)(2,1)S(1)}, bf16[256,768]{1,0:T(8,128)(2,1)S(1)}, u32[]{:S(2)}, u32[]{:S(2)}) collective-permute-start(bf16[256,768]{1,0:T(8,128)(2,1)S(1)} %pad_maximum_fusion.2), channel_id=1, source_target_pairs={{8,0},{12,1},{10,2},{14,3},{9,4},{13,5},{11,6},{15,7},{0,8},{4,9},... | collective-permute-start | bytes 1179656 | tf_op jit(solution)/shard_map/ppermute | solution.py:24
  10.9 3.0 %collective-permute-start.2 = (bf16[256,1024]{1,0:T(8,128)(2,1)S(1)}, bf16[256,1024]{1,0:T(8,128)(2,1)S(1)}, u32[]{:S(2)}, u32[]{:S(2)}) collective-permute-start(bf16[256,1024]{1,0:T(8,128)(2,1)S(1)} %pad_maximum_fusion.1), channel_id=1, source_target_pairs={{0,0},{4,1},{2,2},{6,3},{1,4},{5,5},{3,6},{7,7},{8,8},{12,9},{10,1... | collective-permute-start | bytes 1572872 | tf_op jit(solution)/shard_map/ppermute | solution.py:24
  14.0 1.3 %collective-permute-start.1 = (bf16[2,2,256,256]{3,2,1,0:T(8,128)(2,1)S(1)}, bf16[2,2,256,256]{3,2,1,0:T(8,128)(2,1)S(1)}, u32[]{:S(2)}, u32[]{:S(2)}) collective-permute-start(bf16[2,2,256,256]{3,2,1,0:T(8,128)(2,1)S(1)} %pad_maximum_fusion), channel_id=1, source_target_pairs={{2,0},{3,1},{0,2},{1,3},{6,4},{7,5},{4,6},{5,7},{10,8},{11,9},{8,1... | collective-permute-start | bytes 1572872 | tf_op jit(solution)/shard_map/ppermute | solution.py:24
  15.3 11.0 %collective-permute-done.4.refs_5_ = bf16[256,768]{1,0:T(8,128)(2,1)S(1)} collective-permute-done((bf16[256,768]{1,0:T(8,128)(2,1)S(1)}, bf16[256,768]{1,0:T(8,128)(2,1)S(1)}, u32[]{:S(2)}, u32[]{:S(2)}) %collective-permute-start.4) | collective-permute-done | bytes 393248 | tf_op jit(solution)/shard_map/ppermute | solution.py:24
  26.3 1.4 %collective-permute-start.5 = (bf16[256,512]{1,0:T(8,128)(2,1)S(1)}, bf16[256,512]{1,0:T(8,128)(2,1)S(1)}, u32[]{:S(2)}, u32[]{:S(2)}) collective-permute-start(bf16[256,512]{1,0:T(8,128)(2,1)S(1)} %slice.27), channel_id=1, source_target_pairs={{8,0},{9,1},{10,2},{11,3},{12,4},{13,5},{14,6},{15,7},{0,8},{1,9},... | collective-permute-start | bytes 786440 | tf_op jit(solution)/shard_map/ppermute | solution.py:24
  27.8 2.6 %collective-permute-start.6 = (bf16[256,256]{1,0:T(8,128)(2,1)S(1)}, bf16[256,256]{1,0:T(8,128)(2,1)S(1)}, u32[]{:S(2)}, u32[]{:S(2)}) collective-permute-start(bf16[256,256]{1,0:T(8,128)(2,1)S(1)} %slice.28), channel_id=1, source_target_pairs={{16,0},{17,1},{18,2},{19,3},{20,4},{21,5},{22,6},{23,7},{24,8},{25... | collective-permute-start | bytes 393224 | tf_op jit(solution)/shard_map/ppermute | solution.py:24
  30.3 5.6 %collective-permute-done.5.source_ref = bf16[256,512]{1,0:T(8,128)(2,1)S(1)} collective-permute-done((bf16[256,512]{1,0:T(8,128)(2,1)S(1)}, bf16[256,512]{1,0:T(8,128)(2,1)S(1)}, u32[]{:S(2)}, u32[]{:S(2)}) %collective-permute-start.5) | collective-permute-done | bytes 262176 | tf_op jit(solution)/shard_map/ppermute | solution.py:24
  36.0 1.6 %products.1 = (f32[256,768]{1,0:T(8,128)S(1)}, f32[256,768]{1,0:T(8,128)S(1)}, f32[512,256]{1,0:T(8,128)S(1)}, bf16[512,256]{1,0:T(8,128)(2,1)S(1)}) custom-call(bf16[2,256,256]{2,1,0:T(8,128)(2,1)S(1)} %bitcast.42, bf16[2,256,256]{2,1,0:T(8,128)(2,1)S(1)} %collective-permute-done.refs_1_, bf16[2,2,256,256]{3,2,1,0:T(8,128)(2,1)S(1)} %collective-permute-done.1.refs_2_, ...), custom_call_target="tpu_custom_call" | custom-call | tf_op jit(solution)/shard_map/products/pallas_call | solution.py:188
  37.6 2.0 %collective-permute-start.8 = (bf16[512,256]{1,0:T(8,128)(2,1)S(1)}, bf16[512,256]{1,0:T(8,128)(2,1)S(1)}, u32[]{:S(2)}, u32[]{:S(2)}) collective-permute-start(bf16[512,256]{1,0:T(8,128)(2,1)S(1)} %get-tuple-element.18), channel_id=1, source_target_pairs={{1,0},{0,1},{3,2},{2,3},{5,4},{4,5},{7,6},{6,7},{9,8},{8,9},{11,10... | collective-permute-start | bytes 786440 | tf_op jit(solution)/shard_map/ppermute | solution.py:24
  39.6 0.1 collective-permute-start.12
  39.7 1.1 %collective-permute-done.8 = bf16[512,256]{1,0:T(8,128)(2,1)S(1)} collective-permute-done((bf16[512,256]{1,0:T(8,128)(2,1)S(1)}, bf16[512,256]{1,0:T(8,128)(2,1)S(1)}, u32[]{:S(2)}, u32[]{:S(2)}) %collective-permute-start.8) | collective-permute-done | bytes 262176 | tf_op jit(solution)/shard_map/ppermute | solution.py:24
  40.8 0.1 convert_add_fusion
  40.9 1.9 %collective-permute-start.9 = (bf16[256,256]{1,0:T(8,128)(2,1)S(1)}, bf16[256,256]{1,0:T(8,128)(2,1)S(1)}, u32[]{:S(2)}, u32[]{:S(2)}) collective-permute-start(bf16[256,256]{1,0:T(8,128)(2,1)S(1)} %slice.39), channel_id=1, source_target_pairs={{8,0},{9,1},{10,2},{11,3},{12,4},{13,5},{14,6},{15,7},{0,8},{1,9},... | collective-permute-start | bytes 393224 | tf_op jit(solution)/shard_map/ppermute | solution.py:24
  42.8 3.6 %collective-permute-done.9 = bf16[256,256]{1,0:T(8,128)(2,1)S(1)} collective-permute-done((bf16[256,256]{1,0:T(8,128)(2,1)S(1)}, bf16[256,256]{1,0:T(8,128)(2,1)S(1)}, u32[]{:S(2)}, u32[]{:S(2)}) %collective-permute-start.9) | collective-permute-done | bytes 131104 | tf_op jit(solution)/shard_map/ppermute | solution.py:24
  46.4 1.5 %collective-permute-start.10 = (bf16[256,256]{1,0:T(8,128)(2,1)S(1)}, bf16[256,256]{1,0:T(8,128)(2,1)S(1)}, u32[]{:S(2)}, u32[]{:S(2)}) collective-permute-start(bf16[256,256]{1,0:T(8,128)(2,1)S(1)} %fusion), channel_id=1, source_target_pairs={{16,0},{17,1},{18,2},{19,3},{20,4},{21,5},{22,6},{23,7},{24,8},{25... | collective-permute-start | bytes 393224 | tf_op jit(solution)/shard_map/ppermute | solution.py:24
  48.0 0.1 add_convert_fusion
  48.1 4.0 %collective-permute-start.13 = (bf16[256,768]{1,0:T(8,128)(2,1)S(1)}, bf16[256,768]{1,0:T(8,128)(2,1)S(1)}, u32[]{:S(2)}, u32[]{:S(2)}) collective-permute-start(bf16[256,768]{1,0:T(8,128)(2,1)S(1)} %add_convert_fusion), channel_id=1, source_target_pairs={{0,0},{4,1},{2,2},{6,3},{1,4},{5,5},{3,6},{7,7},{8,8},{12,9},{10,1... | collective-permute-start | bytes 1179656 | tf_op jit(solution)/shard_map/ppermute | solution.py:24
  52.0 2.7 %collective-permute-done.10 = bf16[256,256]{1,0:T(8,128)(2,1)S(1)} collective-permute-done((bf16[256,256]{1,0:T(8,128)(2,1)S(1)}, bf16[256,256]{1,0:T(8,128)(2,1)S(1)}, u32[]{:S(2)}, u32[]{:S(2)}) %collective-permute-start.10) | collective-permute-done | bytes 131104 | tf_op jit(solution)/shard_map/ppermute | solution.py:24
  54.8 3.7 %collective-permute-start.11 = (bf16[256,256]{1,0:T(8,128)(2,1)S(1)}, bf16[256,256]{1,0:T(8,128)(2,1)S(1)}, u32[]{:S(2)}, u32[]{:S(2)}) collective-permute-start(bf16[256,256]{1,0:T(8,128)(2,1)S(1)} %add_convert_fusion.1), channel_id=1, source_target_pairs={{0,0},{4,1},{2,2},{6,3},{1,4},{5,5},{3,6},{7,7},{8,8},{12,9},{10,1... | collective-permute-start | bytes 393224 | tf_op jit(solution)/shard_map/ppermute | solution.py:24
  58.5 0.1 collective-permute-start.16
  58.6 0.1 collective-permute-start.15
  58.7 1.8 %collective-permute-start.14 = (bf16[256,256]{1,0:T(8,128)(2,1)S(1)}, bf16[256,256]{1,0:T(8,128)(2,1)S(1)}, u32[]{:S(2)}, u32[]{:S(2)}) collective-permute-start(bf16[256,256]{1,0:T(8,128)(2,1)S(1)} %add_convert_fusion.1), channel_id=1, source_target_pairs={{1,0},{5,1},{3,2},{7,3},{0,4},{4,5},{2,6},{6,7},{9,8},{13,9},{11,1... | collective-permute-start | bytes 393224 | tf_op jit(solution)/shard_map/ppermute | solution.py:24
  60.5 1.7 %inverse.1 = (bf16[256,2,256]{2,1,0:T(2,128)(2,1)}, bf16[256,256]{1,0:T(8,128)(2,1)}) custom-call(bf16[256,768]{1,0:T(8,128)(2,1)S(1)} %collective-permute-done.13.y_ref, s32[1]{0:T(128)S(6)} %select_n.27.which_ref.refs_7_, s32[2]{0:T(128)S(1)} %bitcast.48, s32[1]{0:T(128)} %bitcast.35.two_ref), custom_call_target="tpu_custom_call" | custom-call | tf_op jit(solution)/shard_map/inverse/pallas_call | solution.py:225
  62.2 2.0 %collective-permute-done.16.refs_3_ = bf16[256,256]{1,0:T(8,128)(2,1)S(1)} collective-permute-done((bf16[256,256]{1,0:T(8,128)(2,1)S(1)}, bf16[256,256]{1,0:T(8,128)(2,1)S(1)}, u32[]{:S(2)}, u32[]{:S(2)}) %collective-permute-start.16) | collective-permute-done | bytes 131104 | tf_op jit(solution)/shard_map/ppermute | solution.py:24
  64.2 1.2 %collective-permute-done.15.refs_2_ = bf16[256,256]{1,0:T(8,128)(2,1)S(1)} collective-permute-done((bf16[256,256]{1,0:T(8,128)(2,1)S(1)}, bf16[256,256]{1,0:T(8,128)(2,1)S(1)}, u32[]{:S(2)}, u32[]{:S(2)}) %collective-permute-start.15) | collective-permute-done | bytes 131104 | tf_op jit(solution)/shard_map/ppermute | solution.py:24
  65.3 0.8 %collective-permute-done.14.refs_1_ = bf16[256,256]{1,0:T(8,128)(2,1)S(1)} collective-permute-done((bf16[256,256]{1,0:T(8,128)(2,1)S(1)}, bf16[256,256]{1,0:T(8,128)(2,1)S(1)}, u32[]{:S(2)}, u32[]{:S(2)}) %collective-permute-start.14) | collective-permute-done | bytes 131104 | tf_op jit(solution)/shard_map/ppermute | solution.py:24
  66.1 1.3 %finish.1 = (f32[2,256,256]{2,1,0:T(8,128)}, bf16[256,256]{1,0:T(8,128)(2,1)}, f32[256,256]{1,0:T(8,128)}) custom-call(bf16[256,256]{1,0:T(8,128)(2,1)S(1)} %collective-permute-done.11.refs_0_, bf16[256,256]{1,0:T(8,128)(2,1)S(1)} %collective-permute-done.14.refs_1_, bf16[256,256]{1,0:T(8,128)(2,1)S(1)} %collective-permute-done.15.refs_2_, ...), custom_call_target="tpu_custom_call" | custom-call | tf_op jit(solution)/shard_map/finish/pallas_call | solution.py:237
  (33 shorter events, 0.4 us)
Async XLA Ops:
  0.6 5.2 %copy-start.5 = (bf16[1,1,256,1,1,256]{5,2,4,3,1,0:T(8,128)(2,1)S(1)}, bf16[1,1,256,1,1,256]{5,2,4,3,1,0:T(8,128)(2,1)}, u32[]{:S(2)}) copy-start(bf16[1,1,256,1,1,256]{5,2,4,3,1,0:T(8,128)(2,1)} %param.11) | copy-start | bytes 393220
  0.6 5.2 %copy-start.4 = (bf16[1,1,256,2,1,256]{5,3,4,2,1,0:T(2,128)(2,1)S(1)}, bf16[1,1,256,2,1,256]{5,3,4,2,1,0:T(2,128)(2,1)}, u32[]{:S(2)}) copy-start(bf16[1,1,256,2,1,256]{5,3,4,2,1,0:T(2,128)(2,1)} %param.10) | copy-start | bytes 786436
  1.7 12.2 %collective-permute-start = (bf16[2,256,256]{2,1,0:T(8,128)(2,1)S(1)}, bf16[2,256,256]{2,1,0:T(8,128)(2,1)S(1)}, u32[]{:S(2)}, u32[]{:S(2)}) collective-permute-start(bf16[2,256,256]{2,1,0:T(8,128)(2,1)S(1)} %bitcast.40), channel_id=1, source_target_pairs={{4,0},{5,1},{6,2},{7,3},{0,4},{1,5},{2,6},{3,7},{12,8},{13,9},{14,... | collective-permute-start | bytes 786440 | tf_op jit(solution)/shard_map/ppermute | solution.py:24
  5.1 0.7 copy-start.3
  6.0 4.9 %copy-start.1 = (bf16[1,1,256,256]{3,2,1,0:T(8,128)(2,1)S(1)}, bf16[1,1,256,256]{3,2,1,0:T(8,128)(2,1)}, u32[]{:S(2)}) copy-start(bf16[1,1,256,256]{3,2,1,0:T(8,128)(2,1)} %param.12) | copy-start | bytes 393220
  6.0 20.3 %collective-permute-start.4 = (bf16[256,768]{1,0:T(8,128)(2,1)S(1)}, bf16[256,768]{1,0:T(8,128)(2,1)S(1)}, u32[]{:S(2)}, u32[]{:S(2)}) collective-permute-start(bf16[256,768]{1,0:T(8,128)(2,1)S(1)} %pad_maximum_fusion.2), channel_id=1, source_target_pairs={{16,0},{20,1},{18,2},{22,3},{17,4},{21,5},{19,6},{23,7},{24,8},{28... | collective-permute-start | bytes 1179656 | tf_op jit(solution)/shard_map/ppermute | solution.py:24
  9.2 18.6 %collective-permute-start.3 = (bf16[256,768]{1,0:T(8,128)(2,1)S(1)}, bf16[256,768]{1,0:T(8,128)(2,1)S(1)}, u32[]{:S(2)}, u32[]{:S(2)}) collective-permute-start(bf16[256,768]{1,0:T(8,128)(2,1)S(1)} %pad_maximum_fusion.2), channel_id=1, source_target_pairs={{8,0},{12,1},{10,2},{14,3},{9,4},{13,5},{11,6},{15,7},{0,8},{4,9},... | collective-permute-start | bytes 1179656 | tf_op jit(solution)/shard_map/ppermute | solution.py:24
  10.9 25.1 %collective-permute-start.2 = (bf16[256,1024]{1,0:T(8,128)(2,1)S(1)}, bf16[256,1024]{1,0:T(8,128)(2,1)S(1)}, u32[]{:S(2)}, u32[]{:S(2)}) collective-permute-start(bf16[256,1024]{1,0:T(8,128)(2,1)S(1)} %pad_maximum_fusion.1), channel_id=1, source_target_pairs={{0,0},{4,1},{2,2},{6,3},{1,4},{5,5},{3,6},{7,7},{8,8},{12,9},{10,1... | collective-permute-start | bytes 1572872 | tf_op jit(solution)/shard_map/ppermute | solution.py:24
  14.0 22.0 %collective-permute-start.1 = (bf16[2,2,256,256]{3,2,1,0:T(8,128)(2,1)S(1)}, bf16[2,2,256,256]{3,2,1,0:T(8,128)(2,1)S(1)}, u32[]{:S(2)}, u32[]{:S(2)}) collective-permute-start(bf16[2,2,256,256]{3,2,1,0:T(8,128)(2,1)S(1)} %pad_maximum_fusion), channel_id=1, source_target_pairs={{2,0},{3,1},{0,2},{1,3},{6,4},{7,5},{4,6},{5,7},{10,8},{11,9},{8,1... | collective-permute-start | bytes 1572872 | tf_op jit(solution)/shard_map/ppermute | solution.py:24
  26.3 9.6 %collective-permute-start.5 = (bf16[256,512]{1,0:T(8,128)(2,1)S(1)}, bf16[256,512]{1,0:T(8,128)(2,1)S(1)}, u32[]{:S(2)}, u32[]{:S(2)}) collective-permute-start(bf16[256,512]{1,0:T(8,128)(2,1)S(1)} %slice.27), channel_id=1, source_target_pairs={{8,0},{9,1},{10,2},{11,3},{12,4},{13,5},{14,6},{15,7},{0,8},{1,9},... | collective-permute-start | bytes 786440 | tf_op jit(solution)/shard_map/ppermute | solution.py:24
  27.7 8.2 %collective-permute-start.7 = (bf16[256,768]{1,0:T(8,128)(2,1)S(1)}, bf16[256,768]{1,0:T(8,128)(2,1)S(1)}, u32[]{:S(2)}, u32[]{:S(2)}) collective-permute-start(bf16[256,768]{1,0:T(8,128)(2,1)S(1)} %pad_maximum_fusion.2), channel_id=1, source_target_pairs={{4,0},{0,1},{6,2},{2,3},{5,4},{1,5},{7,6},{3,7},{12,8},{8,9},{14,1... | collective-permute-start | bytes 1179656 | tf_op jit(solution)/shard_map/ppermute | solution.py:24
  27.8 8.2 %collective-permute-start.6 = (bf16[256,256]{1,0:T(8,128)(2,1)S(1)}, bf16[256,256]{1,0:T(8,128)(2,1)S(1)}, u32[]{:S(2)}, u32[]{:S(2)}) collective-permute-start(bf16[256,256]{1,0:T(8,128)(2,1)S(1)} %slice.28), channel_id=1, source_target_pairs={{16,0},{17,1},{18,2},{19,3},{20,4},{21,5},{22,6},{23,7},{24,8},{25... | collective-permute-start | bytes 393224 | tf_op jit(solution)/shard_map/ppermute | solution.py:24
  37.6 3.2 %collective-permute-start.8 = (bf16[512,256]{1,0:T(8,128)(2,1)S(1)}, bf16[512,256]{1,0:T(8,128)(2,1)S(1)}, u32[]{:S(2)}, u32[]{:S(2)}) collective-permute-start(bf16[512,256]{1,0:T(8,128)(2,1)S(1)} %get-tuple-element.18), channel_id=1, source_target_pairs={{1,0},{0,1},{3,2},{2,3},{5,4},{4,5},{7,6},{6,7},{9,8},{8,9},{11,10... | collective-permute-start | bytes 786440 | tf_op jit(solution)/shard_map/ppermute | solution.py:24
  39.6 8.3 %collective-permute-start.12 = (f32[256,768]{1,0:T(8,128)S(1)}, f32[256,768]{1,0:T(8,128)S(1)}, u32[]{:S(2)}, u32[]{:S(2)}) collective-permute-start(f32[256,768]{1,0:T(8,128)S(1)} %get-tuple-element.20), channel_id=1, source_target_pairs={{1,0},{0,1},{3,2},{2,3},{5,4},{4,5},{7,6},{6,7},{9,8},{8,9},{11,10... | collective-permute-start | bytes 2359304 | tf_op jit(solution)/shard_map/ppermute | solution.py:24
  40.9 5.5 %collective-permute-start.9 = (bf16[256,256]{1,0:T(8,128)(2,1)S(1)}, bf16[256,256]{1,0:T(8,128)(2,1)S(1)}, u32[]{:S(2)}, u32[]{:S(2)}) collective-permute-start(bf16[256,256]{1,0:T(8,128)(2,1)S(1)} %slice.39), channel_id=1, source_target_pairs={{8,0},{9,1},{10,2},{11,3},{12,4},{13,5},{14,6},{15,7},{0,8},{1,9},... | collective-permute-start | bytes 393224 | tf_op jit(solution)/shard_map/ppermute | solution.py:24
  46.4 8.3 %collective-permute-start.10 = (bf16[256,256]{1,0:T(8,128)(2,1)S(1)}, bf16[256,256]{1,0:T(8,128)(2,1)S(1)}, u32[]{:S(2)}, u32[]{:S(2)}) collective-permute-start(bf16[256,256]{1,0:T(8,128)(2,1)S(1)} %fusion), channel_id=1, source_target_pairs={{16,0},{17,1},{18,2},{19,3},{20,4},{21,5},{22,6},{23,7},{24,8},{25... | collective-permute-start | bytes 393224 | tf_op jit(solution)/shard_map/ppermute | solution.py:24
  48.1 18.0 %copy-start = (f32[2,1,256,256]{3,2,1,0:T(8,128)S(1)}, f32[2,1,256,256]{3,2,1,0:T(8,128)}, u32[]{:S(2)}) copy-start(f32[2,1,256,256]{3,2,1,0:T(8,128)} %param.13) | copy-start | bytes 1572868
  48.1 12.4 %collective-permute-start.13 = (bf16[256,768]{1,0:T(8,128)(2,1)S(1)}, bf16[256,768]{1,0:T(8,128)(2,1)S(1)}, u32[]{:S(2)}, u32[]{:S(2)}) collective-permute-start(bf16[256,768]{1,0:T(8,128)(2,1)S(1)} %add_convert_fusion), channel_id=1, source_target_pairs={{0,0},{4,1},{2,2},{6,3},{1,4},{5,5},{3,6},{7,7},{8,8},{12,9},{10,1... | collective-permute-start | bytes 1179656 | tf_op jit(solution)/shard_map/ppermute | solution.py:24
  54.7 11.4 %copy-start.2 = (f32[1,1,256,256]{3,2,1,0:T(8,128)S(1)}, f32[1,1,256,256]{3,2,1,0:T(8,128)}, u32[]{:S(2)}) copy-start(f32[1,1,256,256]{3,2,1,0:T(8,128)} %param.14) | copy-start | bytes 786436
  54.8 7.5 %collective-permute-start.11 = (bf16[256,256]{1,0:T(8,128)(2,1)S(1)}, bf16[256,256]{1,0:T(8,128)(2,1)S(1)}, u32[]{:S(2)}, u32[]{:S(2)}) collective-permute-start(bf16[256,256]{1,0:T(8,128)(2,1)S(1)} %add_convert_fusion.1), channel_id=1, source_target_pairs={{0,0},{4,1},{2,2},{6,3},{1,4},{5,5},{3,6},{7,7},{8,8},{12,9},{10,1... | collective-permute-start | bytes 393224 | tf_op jit(solution)/shard_map/ppermute | solution.py:24
  58.5 5.7 %collective-permute-start.16 = (bf16[256,256]{1,0:T(8,128)(2,1)S(1)}, bf16[256,256]{1,0:T(8,128)(2,1)S(1)}, u32[]{:S(2)}, u32[]{:S(2)}) collective-permute-start(bf16[256,256]{1,0:T(8,128)(2,1)S(1)} %add_convert_fusion.1), channel_id=1, source_target_pairs={{9,0},{13,1},{11,2},{15,3},{8,4},{12,5},{10,6},{14,7},{1,8},{5,9},... | collective-permute-start | bytes 393224 | tf_op jit(solution)/shard_map/ppermute | solution.py:24
  58.6 6.8 %collective-permute-start.15 = (bf16[256,256]{1,0:T(8,128)(2,1)S(1)}, bf16[256,256]{1,0:T(8,128)(2,1)S(1)}, u32[]{:S(2)}, u32[]{:S(2)}) collective-permute-start(bf16[256,256]{1,0:T(8,128)(2,1)S(1)} %add_convert_fusion.1), channel_id=1, source_target_pairs={{8,0},{12,1},{10,2},{14,3},{9,4},{13,5},{11,6},{15,7},{0,8},{4,9},... | collective-permute-start | bytes 393224 | tf_op jit(solution)/shard_map/ppermute | solution.py:24
  58.7 7.4 %collective-permute-start.14 = (bf16[256,256]{1,0:T(8,128)(2,1)S(1)}, bf16[256,256]{1,0:T(8,128)(2,1)S(1)}, u32[]{:S(2)}, u32[]{:S(2)}) collective-permute-start(bf16[256,256]{1,0:T(8,128)(2,1)S(1)} %add_convert_fusion.1), channel_id=1, source_target_pairs={{1,0},{5,1},{3,2},{7,3},{0,4},{4,5},{2,6},{6,7},{9,8},{13,9},{11,1... | collective-permute-start | bytes 393224 | tf_op jit(solution)/shard_map/ppermute | solution.py:24
